TPU v7x, 256 devices: a whole 4x4x8 slice. The times are simulated.
256 devices in a mesh: row: 64 (over x_hi, y, z), rep: 4 (over x_lo, core).
Axes of the slice: x: 4 (x_hi: 2, x_lo: 2; x = x_hi * 2 + x_lo), y: 4, z: 8, core: 2. Of those that a mesh axis runs over, the one named last changes fastest.
Arguments:
- features: bfloat16 [65536, 256], P(('row', 'rep')), may hold values from -1 to 2
- degree: int32 [65536], P(('row', 'rep')), may hold values from 1472 to 5889
- tiles: bfloat16 [64, 4, 16, 22, 128, 128], P('row', 'rep'), may hold values from 0 to 1, as said below
- tile_rows: int32 [64, 4, 16, 22], P('row', 'rep'), may hold values from 0 to 7, as said below
- tile_cols: int32 [64, 4, 16, 22], P('row', 'rep'), may hold values from 0 to 7
- live: int32 [64, 4, 16], P('row', 'rep'), may hold values from 1 to 22, as said below
- weight: bfloat16 [256, 256], replicated, may hold values from -0.375 to 0.375
Outputs:
- activated: bfloat16 [65536, 256], P(('row', 'rep'))
Inputs may be any that keep to these rules, and one draw needn't show every extreme that they name: `tiles`: tile entries are 0 or 1. Within one list (one r, q, k) the pairs (tile_rows, tile_cols) of all 22 slots are distinct. `live`: in every draw all lists of one row shard use all 22 slots.
All inputs are finite; a program needn't handle non-finite values.
Results may differ from a plain program's by a relative error of at most 0.0031.
Values may be sent and summed in bfloat16 or wider, within the bound.
No kernel may reach another device: no remote copies, remote signals or barrier semaphores. Data moves between devices by JAX's collectives and lax.ppermute only.
A program may use at most 64 MiB of HBM per device.

v0:
```python
import jax
import jax.numpy as jnp
from jax import lax
from jax.sharding import PartitionSpec as P


def passed_along(block, axis, distance):
    devices = range(lax.axis_size(axis))
    route = [((i - distance) % len(devices), i) for i in devices]
    return lax.ppermute(block, axis, route)


def accumulate(total, current, tile_stack, dest_rows, source_cols, counts, step):
    tile_size = tile_stack.shape[-1]
    block_count = current.shape[0] // tile_size
    slab = lax.dynamic_index_in_dim(tile_stack, step, 0, keepdims=False)
    dest = lax.dynamic_index_in_dim(dest_rows, step, 0, keepdims=False)
    source = lax.dynamic_index_in_dim(source_cols, step, 0, keepdims=False)
    alive_count = lax.dynamic_index_in_dim(counts, step, 0, keepdims=False)
    blocks = current.reshape(block_count, tile_size, current.shape[1])
    picked = jnp.take(blocks, source, axis=0)
    products = jnp.einsum("sij,sjf->sif", slab, picked, preferred_element_type=jnp.float32)
    slot_ids = jnp.arange(dest.shape[0], dtype=jnp.int32)
    products = jnp.where((slot_ids < alive_count)[:, None, None], products, 0.0)
    shaped = total.reshape(block_count, tile_size, total.shape[1])
    return shaped.at[dest].add(products).reshape(total.shape)


def local(features, degree, tiles, tile_rows, tile_cols, live, weight):
    rep_count = lax.axis_size("rep")
    rep_index = lax.axis_index("rep")
    scale = lax.rsqrt(degree.astype(jnp.float32))
    scaled = (features.astype(jnp.float32) * scale[:, None]).astype(jnp.bfloat16)
    panel = lax.all_gather(scaled, "rep", axis=0, tiled=True)
    for level in range(rep_count.bit_length() - 1):
        moved = passed_along(panel, "row", 1 << level)
        panel = jnp.where(rep_index >> level & 1 == 1, moved, panel)
    tile_stack = tiles[0, 0]
    dest_rows = tile_rows[0, 0]
    source_cols = tile_cols[0, 0]
    counts = live[0, 0]
    steps = tile_stack.shape[0]

    def apply_step(total, current, step):
        return accumulate(total, current, tile_stack, dest_rows, source_cols, counts, step)

    empty = jnp.zeros(panel.shape, jnp.float32)

    def turn_single(step, carry):
        total, current = carry
        total = apply_step(total, current, step)
        current = passed_along(current, "row", rep_count)
        return (total, current)

    total, current_last = lax.fori_loop(0, steps - 1, turn_single, (empty, panel))
    total = apply_step(total, current_last, steps - 1)
    share = lax.psum_scatter(total, "rep", scatter_dimension=0, tiled=True)
    normed = share * scale[:, None]
    product = jnp.dot(normed, weight.astype(jnp.float32), precision=lax.Precision.HIGHEST)
    return jax.nn.relu(product).astype(jnp.bfloat16)


def solution(mesh):
    in_specs = (
        P(("row", "rep"), None),
        P(("row", "rep")),
        P("row", "rep", None, None, None, None),
        P("row", "rep", None, None),
        P("row", "rep", None, None),
        P("row", "rep", None),
        P(),
    )
    out_specs = P(("row", "rep"), None)
    return jax.shard_map(local, mesh=mesh, in_specs=in_specs, out_specs=out_specs, check_vma=False)
```

profile of v0, /device:TPU:6, one launch (start us, length us, event | category | flops | bytes accessed | tf_op | source)
XLA Modules:
  0.0 566.7 jit_solution(4895911773397118695)
XLA Ops:
  8.3 6.8 %all_gather.3 = bf16[1024,256]{1,0:T(8,128)(2,1)S(1)} all-gather(bf16[256,256]{1,0:T(8,128)(2,1)S(1)} %multiply_convert_fusion), channel_id=1, replica_groups=mesh['row'=64,'rep'=4] {'rep'}, dimensions={0}, use_global_device_ids=true | all-gather | bytes 655360 | tf_op jit(solution)/shard_map/all_gather | solution.py:34
  18.2 18.4 %collective-permute-done.1 = bf16[1024,256]{1,0:T(8,128)(2,1)S(1)} collective-permute-done((bf16[1024,256]{1,0:T(8,128)(2,1)S(1)}, bf16[1024,256]{1,0:T(8,128)(2,1)S(1)}, u32[]{:S(2)}, u32[]{:S(2)}) %collective-permute-start.1) | collective-permute-done | bytes 524320 | tf_op jit(solution)/shard_map/ppermute | solution.py:10
  38.8 26.4 %collective-permute-done.2 = bf16[1024,256]{1,0:T(8,128)(2,1)S(1)} collective-permute-done((bf16[1024,256]{1,0:T(8,128)(2,1)S(1)}, bf16[1024,256]{1,0:T(8,128)(2,1)S(1)}, u32[]{:S(2)}, u32[]{:S(2)}) %collective-permute-start.2) | collective-permute-done | bytes 524320 | tf_op jit(solution)/shard_map/ppermute | solution.py:10
  66.1 379.9 %while.15 = (s32[]{:T(128)}, f32[1024,256]{1,0:T(8,128)S(1)}, bf16[1024,256]{1,0:T(8,128)(2,1)}, s32[16,22]{1,0:T(8,128)}, s32[16]{0:T(128)S(1)}, /*index=5*/bf1...) while((s32[]{:T(128)}, f32[1024,256]{1,0:T(8,128)S(1)}, bf16[1024,256]{1,0:T(8,128)(2,1)}, ...), condition=%wide.region_2.4_spmd, body=%wide.region_0.3_spmd.sunk | while | flops 186713312 | bytes 19731296 | solution.py:55
  73.7 6.0 %scatter_fusion = f32[8,128,256]{2,1,0:T(8,128)S(1)} fusion(f32[8,128,256]{2,1,0:T(8,128)S(1)} %bitcast.55, s32[22]{0:T(128)S(1)} %fusion.26, f32[22,128,256]{2,1,0:T(8,128)} %convolution_select_fusion.2), kind=kCustom, calls=%fused_computation.2.clone.1 | custom fusion | flops 720896 | bytes 8650840 | tf_op jit(solution)/shard_map/while/body/eval_jaxpr/scatter-add | solution.py:26
  79.7 17.5 %collective-permute-done = bf16[1024,256]{1,0:T(8,128)(2,1)} collective-permute-done((bf16[1024,256]{1,0:T(8,128)(2,1)S(1)}, bf16[1024,256]{1,0:T(8,128)(2,1)}, u32[]{:S(2)}, u32[]{:S(2)}) %collective-permute-start) | collective-permute-done | bytes 524320 | tf_op jit(solution)/shard_map/while/body/eval_jaxpr/ppermute | solution.py:10
  104.8 6.0 %scatter_fusion = f32[8,128,256]{2,1,0:T(8,128)S(1)} fusion(f32[8,128,256]{2,1,0:T(8,128)S(1)} %bitcast.55, s32[22]{0:T(128)S(1)} %fusion.26, f32[22,128,256]{2,1,0:T(8,128)} %convolution_select_fusion.2), kind=kCustom, calls=%fused_computation.2.clone.1 | custom fusion | flops 720896 | bytes 8650840 | tf_op jit(solution)/shard_map/while/body/eval_jaxpr/scatter-add | solution.py:26
  110.8 9.8 %collective-permute-done = bf16[1024,256]{1,0:T(8,128)(2,1)} collective-permute-done((bf16[1024,256]{1,0:T(8,128)(2,1)S(1)}, bf16[1024,256]{1,0:T(8,128)(2,1)}, u32[]{:S(2)}, u32[]{:S(2)}) %collective-permute-start) | collective-permute-done | bytes 524320 | tf_op jit(solution)/shard_map/while/body/eval_jaxpr/ppermute | solution.py:10
  128.2 6.0 %scatter_fusion = f32[8,128,256]{2,1,0:T(8,128)S(1)} fusion(f32[8,128,256]{2,1,0:T(8,128)S(1)} %bitcast.55, s32[22]{0:T(128)S(1)} %fusion.26, f32[22,128,256]{2,1,0:T(8,128)} %convolution_select_fusion.2), kind=kCustom, calls=%fused_computation.2.clone.1 | custom fusion | flops 720896 | bytes 8650840 | tf_op jit(solution)/shard_map/while/body/eval_jaxpr/scatter-add | solution.py:26
  134.2 12.7 %collective-permute-done = bf16[1024,256]{1,0:T(8,128)(2,1)} collective-permute-done((bf16[1024,256]{1,0:T(8,128)(2,1)S(1)}, bf16[1024,256]{1,0:T(8,128)(2,1)}, u32[]{:S(2)}, u32[]{:S(2)}) %collective-permute-start) | collective-permute-done | bytes 524320 | tf_op jit(solution)/shard_map/while/body/eval_jaxpr/ppermute | solution.py:10
  154.5 6.0 %scatter_fusion = f32[8,128,256]{2,1,0:T(8,128)S(1)} fusion(f32[8,128,256]{2,1,0:T(8,128)S(1)} %bitcast.55, s32[22]{0:T(128)S(1)} %fusion.26, f32[22,128,256]{2,1,0:T(8,128)} %convolution_select_fusion.2), kind=kCustom, calls=%fused_computation.2.clone.1 | custom fusion | flops 720896 | bytes 8650840 | tf_op jit(solution)/shard_map/while/body/eval_jaxpr/scatter-add | solution.py:26
  160.5 10.0 %collective-permute-done = bf16[1024,256]{1,0:T(8,128)(2,1)} collective-permute-done((bf16[1024,256]{1,0:T(8,128)(2,1)S(1)}, bf16[1024,256]{1,0:T(8,128)(2,1)}, u32[]{:S(2)}, u32[]{:S(2)}) %collective-permute-start) | collective-permute-done | bytes 524320 | tf_op jit(solution)/shard_map/while/body/eval_jaxpr/ppermute | solution.py:10
  184.2 12.5 %collective-permute-done = bf16[1024,256]{1,0:T(8,128)(2,1)} collective-permute-done((bf16[1024,256]{1,0:T(8,128)(2,1)S(1)}, bf16[1024,256]{1,0:T(8,128)(2,1)}, u32[]{:S(2)}, u32[]{:S(2)}) %collective-permute-start) | collective-permute-done | bytes 524320 | tf_op jit(solution)/shard_map/while/body/eval_jaxpr/ppermute | solution.py:10
  204.3 6.0 %scatter_fusion = f32[8,128,256]{2,1,0:T(8,128)S(1)} fusion(f32[8,128,256]{2,1,0:T(8,128)S(1)} %bitcast.55, s32[22]{0:T(128)S(1)} %fusion.26, f32[22,128,256]{2,1,0:T(8,128)} %convolution_select_fusion.2), kind=kCustom, calls=%fused_computation.2.clone.1 | custom fusion | flops 720896 | bytes 8650840 | tf_op jit(solution)/shard_map/while/body/eval_jaxpr/scatter-add | solution.py:26
  210.3 10.2 %collective-permute-done = bf16[1024,256]{1,0:T(8,128)(2,1)} collective-permute-done((bf16[1024,256]{1,0:T(8,128)(2,1)S(1)}, bf16[1024,256]{1,0:T(8,128)(2,1)}, u32[]{:S(2)}, u32[]{:S(2)}) %collective-permute-start) | collective-permute-done | bytes 524320 | tf_op jit(solution)/shard_map/while/body/eval_jaxpr/ppermute | solution.py:10
  234.1 12.4 %collective-permute-done = bf16[1024,256]{1,0:T(8,128)(2,1)} collective-permute-done((bf16[1024,256]{1,0:T(8,128)(2,1)S(1)}, bf16[1024,256]{1,0:T(8,128)(2,1)}, u32[]{:S(2)}, u32[]{:S(2)}) %collective-permute-start) | collective-permute-done | bytes 524320 | tf_op jit(solution)/shard_map/while/body/eval_jaxpr/ppermute | solution.py:10
  260.2 10.3 %collective-permute-done = bf16[1024,256]{1,0:T(8,128)(2,1)} collective-permute-done((bf16[1024,256]{1,0:T(8,128)(2,1)S(1)}, bf16[1024,256]{1,0:T(8,128)(2,1)}, u32[]{:S(2)}, u32[]{:S(2)}) %collective-permute-start) | collective-permute-done | bytes 524320 | tf_op jit(solution)/shard_map/while/body/eval_jaxpr/ppermute | solution.py:10
  278.1 6.0 %scatter_fusion = f32[8,128,256]{2,1,0:T(8,128)S(1)} fusion(f32[8,128,256]{2,1,0:T(8,128)S(1)} %bitcast.55, s32[22]{0:T(128)S(1)} %fusion.26, f32[22,128,256]{2,1,0:T(8,128)} %convolution_select_fusion.2), kind=kCustom, calls=%fused_computation.2.clone.1 | custom fusion | flops 720896 | bytes 8650840 | tf_op jit(solution)/shard_map/while/body/eval_jaxpr/scatter-add | solution.py:26
  284.1 12.3 %collective-permute-done = bf16[1024,256]{1,0:T(8,128)(2,1)} collective-permute-done((bf16[1024,256]{1,0:T(8,128)(2,1)S(1)}, bf16[1024,256]{1,0:T(8,128)(2,1)}, u32[]{:S(2)}, u32[]{:S(2)}) %collective-permute-start) | collective-permute-done | bytes 524320 | tf_op jit(solution)/shard_map/while/body/eval_jaxpr/ppermute | solution.py:10
  304.1 6.0 %scatter_fusion = f32[8,128,256]{2,1,0:T(8,128)S(1)} fusion(f32[8,128,256]{2,1,0:T(8,128)S(1)} %bitcast.55, s32[22]{0:T(128)S(1)} %fusion.26, f32[22,128,256]{2,1,0:T(8,128)} %convolution_select_fusion.2), kind=kCustom, calls=%fused_computation.2.clone.1 | custom fusion | flops 720896 | bytes 8650840 | tf_op jit(solution)/shard_map/while/body/eval_jaxpr/scatter-add | solution.py:26
  310.1 10.4 %collective-permute-done = bf16[1024,256]{1,0:T(8,128)(2,1)} collective-permute-done((bf16[1024,256]{1,0:T(8,128)(2,1)S(1)}, bf16[1024,256]{1,0:T(8,128)(2,1)}, u32[]{:S(2)}, u32[]{:S(2)}) %collective-permute-start) | collective-permute-done | bytes 524320 | tf_op jit(solution)/shard_map/while/body/eval_jaxpr/ppermute | solution.py:10
  328.1 6.0 %scatter_fusion = f32[8,128,256]{2,1,0:T(8,128)S(1)} fusion(f32[8,128,256]{2,1,0:T(8,128)S(1)} %bitcast.55, s32[22]{0:T(128)S(1)} %fusion.26, f32[22,128,256]{2,1,0:T(8,128)} %convolution_select_fusion.2), kind=kCustom, calls=%fused_computation.2.clone.1 | custom fusion | flops 720896 | bytes 8650840 | tf_op jit(solution)/shard_map/while/body/eval_jaxpr/scatter-add | solution.py:26
  334.1 12.3 %collective-permute-done = bf16[1024,256]{1,0:T(8,128)(2,1)} collective-permute-done((bf16[1024,256]{1,0:T(8,128)(2,1)S(1)}, bf16[1024,256]{1,0:T(8,128)(2,1)}, u32[]{:S(2)}, u32[]{:S(2)}) %collective-permute-start) | collective-permute-done | bytes 524320 | tf_op jit(solution)/shard_map/while/body/eval_jaxpr/ppermute | solution.py:10
  354.0 6.0 %scatter_fusion = f32[8,128,256]{2,1,0:T(8,128)S(1)} fusion(f32[8,128,256]{2,1,0:T(8,128)S(1)} %bitcast.55, s32[22]{0:T(128)S(1)} %fusion.26, f32[22,128,256]{2,1,0:T(8,128)} %convolution_select_fusion.2), kind=kCustom, calls=%fused_computation.2.clone.1 | custom fusion | flops 720896 | bytes 8650840 | tf_op jit(solution)/shard_map/while/body/eval_jaxpr/scatter-add | solution.py:26
  360.0 10.4 %collective-permute-done = bf16[1024,256]{1,0:T(8,128)(2,1)} collective-permute-done((bf16[1024,256]{1,0:T(8,128)(2,1)S(1)}, bf16[1024,256]{1,0:T(8,128)(2,1)}, u32[]{:S(2)}, u32[]{:S(2)}) %collective-permute-start) | collective-permute-done | bytes 524320 | tf_op jit(solution)/shard_map/while/body/eval_jaxpr/ppermute | solution.py:10
  384.0 12.3 %collective-permute-done = bf16[1024,256]{1,0:T(8,128)(2,1)} collective-permute-done((bf16[1024,256]{1,0:T(8,128)(2,1)S(1)}, bf16[1024,256]{1,0:T(8,128)(2,1)}, u32[]{:S(2)}, u32[]{:S(2)}) %collective-permute-start) | collective-permute-done | bytes 524320 | tf_op jit(solution)/shard_map/while/body/eval_jaxpr/ppermute | solution.py:10
  403.9 6.0 %scatter_fusion = f32[8,128,256]{2,1,0:T(8,128)S(1)} fusion(f32[8,128,256]{2,1,0:T(8,128)S(1)} %bitcast.55, s32[22]{0:T(128)S(1)} %fusion.26, f32[22,128,256]{2,1,0:T(8,128)} %convolution_select_fusion.2), kind=kCustom, calls=%fused_computation.2.clone.1 | custom fusion | flops 720896 | bytes 8650840 | tf_op jit(solution)/shard_map/while/body/eval_jaxpr/scatter-add | solution.py:26
  409.9 10.5 %collective-permute-done = bf16[1024,256]{1,0:T(8,128)(2,1)} collective-permute-done((bf16[1024,256]{1,0:T(8,128)(2,1)S(1)}, bf16[1024,256]{1,0:T(8,128)(2,1)}, u32[]{:S(2)}, u32[]{:S(2)}) %collective-permute-start) | collective-permute-done | bytes 524320 | tf_op jit(solution)/shard_map/while/body/eval_jaxpr/ppermute | solution.py:10
  428.0 6.0 %scatter_fusion = f32[8,128,256]{2,1,0:T(8,128)S(1)} fusion(f32[8,128,256]{2,1,0:T(8,128)S(1)} %bitcast.55, s32[22]{0:T(128)S(1)} %fusion.26, f32[22,128,256]{2,1,0:T(8,128)} %convolution_select_fusion.2), kind=kCustom, calls=%fused_computation.2.clone.1 | custom fusion | flops 720896 | bytes 8650840 | tf_op jit(solution)/shard_map/while/body/eval_jaxpr/scatter-add | solution.py:26
  434.0 12.0 %collective-permute-done = bf16[1024,256]{1,0:T(8,128)(2,1)} collective-permute-done((bf16[1024,256]{1,0:T(8,128)(2,1)S(1)}, bf16[1024,256]{1,0:T(8,128)(2,1)}, u32[]{:S(2)}, u32[]{:S(2)}) %collective-permute-start) | collective-permute-done | bytes 524320 | tf_op jit(solution)/shard_map/while/body/eval_jaxpr/ppermute | solution.py:10
  454.6 6.0 %scatter_fusion.1 = f32[8,128,256]{2,1,0:T(8,128)S(1)} fusion(f32[8,128,256]{2,1,0:T(8,128)S(1)} %bitcast.57, s32[22]{0:T(128)S(1)} %fusion.18, f32[22,128,256]{2,1,0:T(8,128)} %copy.10), kind=kCustom, calls=%fused_computation.3 | custom fusion | flops 720896 | bytes 8650840 | tf_op jit(solution)/shard_map/scatter-add | solution.py:26
  461.5 96.4 %reduce-scatter.2.cloned.1.call-done = f32[256,256]{1,0:T(8,128)} async-done(((f32[1024,256]{1,0:T(8,128)}), f32[256,256]{1,0:T(8,128)}) %reduce-scatter.2.cloned.1.call-update) | async-done | bytes 262160 | tf_op jit(solution)/shard_map/reduce_scatter | solution.py:57
  (162 shorter events, 157.4 us)
Async XLA Ops:
  6.5 551.4 %copy-start = (bf16[256,256]{1,0:T(8,128)(2,1)S(1)}, bf16[256,256]{1,0:T(8,128)(2,1)}, u32[]{:S(2)}) copy-start(bf16[256,256]{1,0:T(8,128)(2,1)} %param.17) | copy-start | bytes 393220
  6.5 59.5 %copy-start.2 = (s32[1,1,16]{2,1,0:T(1,128)S(1)}, s32[1,1,16]{2,1,0:T(1,128)}, u32[]{:S(2)}) copy-start(s32[1,1,16]{2,1,0:T(1,128)} %param.16) | copy-start | bytes 196
  6.5 551.4 %reduce-scatter.2.cloned.1.call-start = ((), (), s32[]{:S(2)}) async-start(), calls=%async_computation.1 | async-start | bytes 1310720 | tf_op jit(solution)/shard_map/reduce_scatter | solution.py:57
  15.1 21.6 %collective-permute-start.1 = (bf16[1024,256]{1,0:T(8,128)(2,1)S(1)}, bf16[1024,256]{1,0:T(8,128)(2,1)S(1)}, u32[]{:S(2)}, u32[]{:S(2)}) collective-permute-start(bf16[1024,256]{1,0:T(8,128)(2,1)S(1)} %all_gather.3), channel_id=1, source_target_pairs={{252,0},{0,4},{4,8},{8,12},{12,16},{16,20},{20,24},{24,28},{28,32}... | collective-permute-start | bytes 1572872 | tf_op jit(solution)/shard_map/ppermute | solution.py:10
  36.7 28.4 %collective-permute-start.2 = (bf16[1024,256]{1,0:T(8,128)(2,1)S(1)}, bf16[1024,256]{1,0:T(8,128)(2,1)S(1)}, u32[]{:S(2)}, u32[]{:S(2)}) collective-permute-start(bf16[1024,256]{1,0:T(8,128)(2,1)S(1)} %broadcast_select_fusion), channel_id=1, source_target_pairs={{248,0},{252,4},{0,8},{4,12},{8,16},{12,20},{16,24},{20,28},{24,32... | collective-permute-start | bytes 1572872 | tf_op jit(solution)/shard_map/ppermute | solution.py:10
  67.1 30.0 %collective-permute-start = (bf16[1024,256]{1,0:T(8,128)(2,1)S(1)}, bf16[1024,256]{1,0:T(8,128)(2,1)}, u32[]{:S(2)}, u32[]{:S(2)}) collective-permute-start(bf16[1024,256]{1,0:T(8,128)(2,1)S(1)} %copy.18), channel_id=1, source_target_pairs={{240,0},{244,4},{248,8},{252,12},{0,16},{4,20},{8,24},{12,28},{16,... | collective-permute-start | bytes 1572872 | tf_op jit(solution)/shard_map/while/body/eval_jaxpr/ppermute | solution.py:10
  98.2 22.4 %collective-permute-start = (bf16[1024,256]{1,0:T(8,128)(2,1)S(1)}, bf16[1024,256]{1,0:T(8,128)(2,1)}, u32[]{:S(2)}, u32[]{:S(2)}) collective-permute-start(bf16[1024,256]{1,0:T(8,128)(2,1)S(1)} %copy.18), channel_id=1, source_target_pairs={{240,0},{244,4},{248,8},{252,12},{0,16},{4,20},{8,24},{12,28},{16,... | collective-permute-start | bytes 1572872 | tf_op jit(solution)/shard_map/while/body/eval_jaxpr/ppermute | solution.py:10
  121.6 25.3 %collective-permute-start = (bf16[1024,256]{1,0:T(8,128)(2,1)S(1)}, bf16[1024,256]{1,0:T(8,128)(2,1)}, u32[]{:S(2)}, u32[]{:S(2)}) collective-permute-start(bf16[1024,256]{1,0:T(8,128)(2,1)S(1)} %copy.18), channel_id=1, source_target_pairs={{240,0},{244,4},{248,8},{252,12},{0,16},{4,20},{8,24},{12,28},{16,... | collective-permute-start | bytes 1572872 | tf_op jit(solution)/shard_map/while/body/eval_jaxpr/ppermute | solution.py:10
  148.0 22.6 %collective-permute-start = (bf16[1024,256]{1,0:T(8,128)(2,1)S(1)}, bf16[1024,256]{1,0:T(8,128)(2,1)}, u32[]{:S(2)}, u32[]{:S(2)}) collective-permute-start(bf16[1024,256]{1,0:T(8,128)(2,1)S(1)} %copy.18), channel_id=1, source_target_pairs={{240,0},{244,4},{248,8},{252,12},{0,16},{4,20},{8,24},{12,28},{16,... | collective-permute-start | bytes 1572872 | tf_op jit(solution)/shard_map/while/body/eval_jaxpr/ppermute | solution.py:10
  171.6 25.1 %collective-permute-start = (bf16[1024,256]{1,0:T(8,128)(2,1)S(1)}, bf16[1024,256]{1,0:T(8,128)(2,1)}, u32[]{:S(2)}, u32[]{:S(2)}) collective-permute-start(bf16[1024,256]{1,0:T(8,128)(2,1)S(1)} %copy.18), channel_id=1, source_target_pairs={{240,0},{244,4},{248,8},{252,12},{0,16},{4,20},{8,24},{12,28},{16,... | collective-permute-start | bytes 1572872 | tf_op jit(solution)/shard_map/while/body/eval_jaxpr/ppermute | solution.py:10
  197.7 22.8 %collective-permute-start = (bf16[1024,256]{1,0:T(8,128)(2,1)S(1)}, bf16[1024,256]{1,0:T(8,128)(2,1)}, u32[]{:S(2)}, u32[]{:S(2)}) collective-permute-start(bf16[1024,256]{1,0:T(8,128)(2,1)S(1)} %copy.18), channel_id=1, source_target_pairs={{240,0},{244,4},{248,8},{252,12},{0,16},{4,20},{8,24},{12,28},{16,... | collective-permute-start | bytes 1572872 | tf_op jit(solution)/shard_map/while/body/eval_jaxpr/ppermute | solution.py:10
  221.6 25.0 %collective-permute-start = (bf16[1024,256]{1,0:T(8,128)(2,1)S(1)}, bf16[1024,256]{1,0:T(8,128)(2,1)}, u32[]{:S(2)}, u32[]{:S(2)}) collective-permute-start(bf16[1024,256]{1,0:T(8,128)(2,1)S(1)} %copy.18), channel_id=1, source_target_pairs={{240,0},{244,4},{248,8},{252,12},{0,16},{4,20},{8,24},{12,28},{16,... | collective-permute-start | bytes 1572872 | tf_op jit(solution)/shard_map/while/body/eval_jaxpr/ppermute | solution.py:10
  247.6 22.9 %collective-permute-start = (bf16[1024,256]{1,0:T(8,128)(2,1)S(1)}, bf16[1024,256]{1,0:T(8,128)(2,1)}, u32[]{:S(2)}, u32[]{:S(2)}) collective-permute-start(bf16[1024,256]{1,0:T(8,128)(2,1)S(1)} %copy.18), channel_id=1, source_target_pairs={{240,0},{244,4},{248,8},{252,12},{0,16},{4,20},{8,24},{12,28},{16,... | collective-permute-start | bytes 1572872 | tf_op jit(solution)/shard_map/while/body/eval_jaxpr/ppermute | solution.py:10
  271.5 24.9 %collective-permute-start = (bf16[1024,256]{1,0:T(8,128)(2,1)S(1)}, bf16[1024,256]{1,0:T(8,128)(2,1)}, u32[]{:S(2)}, u32[]{:S(2)}) collective-permute-start(bf16[1024,256]{1,0:T(8,128)(2,1)S(1)} %copy.18), channel_id=1, source_target_pairs={{240,0},{244,4},{248,8},{252,12},{0,16},{4,20},{8,24},{12,28},{16,... | collective-permute-start | bytes 1572872 | tf_op jit(solution)/shard_map/while/body/eval_jaxpr/ppermute | solution.py:10
  297.5 23.0 %collective-permute-start = (bf16[1024,256]{1,0:T(8,128)(2,1)S(1)}, bf16[1024,256]{1,0:T(8,128)(2,1)}, u32[]{:S(2)}, u32[]{:S(2)}) collective-permute-start(bf16[1024,256]{1,0:T(8,128)(2,1)S(1)} %copy.18), channel_id=1, source_target_pairs={{240,0},{244,4},{248,8},{252,12},{0,16},{4,20},{8,24},{12,28},{16,... | collective-permute-start | bytes 1572872 | tf_op jit(solution)/shard_map/while/body/eval_jaxpr/ppermute | solution.py:10
  321.5 24.9 %collective-permute-start = (bf16[1024,256]{1,0:T(8,128)(2,1)S(1)}, bf16[1024,256]{1,0:T(8,128)(2,1)}, u32[]{:S(2)}, u32[]{:S(2)}) collective-permute-start(bf16[1024,256]{1,0:T(8,128)(2,1)S(1)} %copy.18), channel_id=1, source_target_pairs={{240,0},{244,4},{248,8},{252,12},{0,16},{4,20},{8,24},{12,28},{16,... | collective-permute-start | bytes 1572872 | tf_op jit(solution)/shard_map/while/body/eval_jaxpr/ppermute | solution.py:10
  347.4 23.0 %collective-permute-start = (bf16[1024,256]{1,0:T(8,128)(2,1)S(1)}, bf16[1024,256]{1,0:T(8,128)(2,1)}, u32[]{:S(2)}, u32[]{:S(2)}) collective-permute-start(bf16[1024,256]{1,0:T(8,128)(2,1)S(1)} %copy.18), channel_id=1, source_target_pairs={{240,0},{244,4},{248,8},{252,12},{0,16},{4,20},{8,24},{12,28},{16,... | collective-permute-start | bytes 1572872 | tf_op jit(solution)/shard_map/while/body/eval_jaxpr/ppermute | solution.py:10
  371.4 24.8 %collective-permute-start = (bf16[1024,256]{1,0:T(8,128)(2,1)S(1)}, bf16[1024,256]{1,0:T(8,128)(2,1)}, u32[]{:S(2)}, u32[]{:S(2)}) collective-permute-start(bf16[1024,256]{1,0:T(8,128)(2,1)S(1)} %copy.18), channel_id=1, source_target_pairs={{240,0},{244,4},{248,8},{252,12},{0,16},{4,20},{8,24},{12,28},{16,... | collective-permute-start | bytes 1572872 | tf_op jit(solution)/shard_map/while/body/eval_jaxpr/ppermute | solution.py:10
  397.3 23.0 %collective-permute-start = (bf16[1024,256]{1,0:T(8,128)(2,1)S(1)}, bf16[1024,256]{1,0:T(8,128)(2,1)}, u32[]{:S(2)}, u32[]{:S(2)}) collective-permute-start(bf16[1024,256]{1,0:T(8,128)(2,1)S(1)} %copy.18), channel_id=1, source_target_pairs={{240,0},{244,4},{248,8},{252,12},{0,16},{4,20},{8,24},{12,28},{16,... | collective-permute-start | bytes 1572872 | tf_op jit(solution)/shard_map/while/body/eval_jaxpr/ppermute | solution.py:10
  421.4 24.6 %collective-permute-start = (bf16[1024,256]{1,0:T(8,128)(2,1)S(1)}, bf16[1024,256]{1,0:T(8,128)(2,1)}, u32[]{:S(2)}, u32[]{:S(2)}) collective-permute-start(bf16[1024,256]{1,0:T(8,128)(2,1)S(1)} %copy.18), channel_id=1, source_target_pairs={{240,0},{244,4},{248,8},{252,12},{0,16},{4,20},{8,24},{12,28},{16,... | collective-permute-start | bytes 1572872 | tf_op jit(solution)/shard_map/while/body/eval_jaxpr/ppermute | solution.py:10
  460.6 1.0 copy-start.1
Sparse Core Ops, SparseCore 0:
  461.7 96.2 reduce-scatter.1
where the time goes:
time: 573 us; the launch traced here: 567 us
  waiting for transfers between devices  317 us (55%)
  other arithmetic  131 us (23%)
  matrix products  54.7 us (10%)
  local copies, waits for them, and re-layouts  41.9 us (7%)
  between operations  13.5 us (2%)
  blocking collectives  6.78 us (1%)
    ppermute x17, waiting for transfers between devices, passed_along(): return lax.ppermute(block, axis, route)  220 us
    reduce_scatter x1, waiting for transfers between devices, local(): share = lax.psum_scatter(total, 'rep', scatter_dimension=0, tiled=True)  96.4 us
    scatter-add x16, other arithmetic, accumulate(): return shaped.at[dest].add(products).reshape(total.shape)  95.7 us
    dot_general x16, matrix products, accumulate(): jnp.einsum('sij,sjf->sif', slab, picked, preferred_element_type=jnp.float32)  52.8 us
    another operation x15, local copies, waits for them, and re-layouts  15.6 us
    and x16, other arithmetic, accumulate(): picked = jnp.take(blocks, source, axis=0)  11.8 us
  transfers between devices with their start and end apart: 18, of which 18 were waited for; matrix products, arithmetic and copies ran while one was open for 34% of the time, Pallas kernels for 0%

commit v1 on v0

v1 whole, which is shorter than its diff:
```python
import functools

import jax
import jax.numpy as jnp
import numpy as np
from jax import lax
from jax.experimental import pallas as pl
from jax.experimental.pallas import tpu as pltpu
from jax.sharding import PartitionSpec as P

AXES = ("row", "rep")
TILE = 128
SLOTS = 22
STEPS = 16
N_TILES = STEPS * SLOTS
LIST = 256


def home_shift(q):
    return (0, 1, 2, -1)[q]


def route(dh=0, dp=0, dy=0, home=False):
    out = []
    for h in range(2):
        for y in range(4):
            for z in range(8):
                for q in range(4):
                    hh, zz, qq = h, z, q
                    for _ in range(dp):
                        hh, zz, qq = hh + (qq == 3), zz + 1, (qq + 1) % 4
                    for _ in range(-dp):
                        hh, zz, qq = hh - (qq == 0), zz - 1, (qq - 1) % 4
                    if home:
                        zz -= home_shift(qq)
                    source = ((((hh + dh) % 2) * 4 + (y + dy) % 4) * 8 + zz % 8) * 4 + qq
                    out.append((source, ((h * 4 + y) * 8 + z) * 4 + q))
    return out


class Blocks:
    def __init__(self, rows, labels):
        self.rows, self.labels = rows, labels

    def __getitem__(self, blocks):
        first, last = blocks.start or 0, len(self.labels) if blocks.stop is None else blocks.stop
        return Blocks(lax.slice_in_dim(self.rows, first * TILE, last * TILE), self.labels[first:last])

    def moved(self, dh=0, dp=0, dy=0, home=False):
        rows = lax.ppermute(self.rows, AXES, route(dh, dp, dy, home))
        labels = [(t, (a + dh) % 2, (b + dp) % 8, (c + dy) % 4) for t, a, b, c in self.labels]
        return Blocks(rows, labels)


def joined(*parts):
    return Blocks(jnp.concatenate([p.rows for p in parts], 0), [label for p in parts for label in p.labels])


def gather(scaled):
    own = Blocks(scaled, [(0, 0, 0, 0), (1, 0, 0, 0)])
    near, far = own.moved(home=True), own.moved(dh=1, home=True)
    start = joined(near[0:1], far[0:1], near[1:2], far[1:2])
    found = [start]

    def along_y(blocks):
        got = [blocks.moved(dy=dy) for dy in (1, -1, 2)]
        found.extend(got)
        return got

    along = along_y(start)
    up, down = start.moved(dp=1), start.moved(dp=-1)
    found.extend((up, down))
    others = joined(*(a[2:4] for a in along))
    along_y(joined(up[0:2], down[0:2]))
    up, down = joined(up, others).moved(dp=1), joined(down, others).moved(dp=-1)
    found.extend((up, down))
    along_y(joined(up[0:2], down[0:2]))
    up, down = up.moved(dp=1), down.moved(dp=-1)
    found.extend((up, down))
    along_y(joined(up[0:2], down[0:2]))
    up, down = joined(up[0:1], up[2:3], up[4:10]).moved(dp=1), joined(down[1:2], down[3:4], down[4:10]).moved(dp=-1)
    found.extend((up, down))
    along_y(joined(up[0:1], down[0:1]))
    found.extend((up[2:5].moved(dp=1), down[5:8].moved(dp=-1)))
    return found


def list_kernel(live, coded, places, lists, counts):
    for b in range(8):
        counts[b] = 0

    def one_source(k, _):
        def one_slot(s, _):
            v = coded[k, s]
            b = v >> 7
            n = counts[b]
            lists[b, n] = (k * SLOTS + s) + (places[v & 127] << 10)
            counts[b] = n + 1
            return 0

        return lax.fori_loop(0, live[k], one_slot, 0)

    lax.fori_loop(0, STEPS, one_source, 0)
    for b in range(8):
        lists[b, counts[b]] = N_TILES


def slot_lists(live, coded, places):
    smem = pl.BlockSpec(memory_space=pltpu.SMEM)
    return pl.pallas_call(
        list_kernel,
        out_shape=(jax.ShapeDtypeStruct((8, LIST), jnp.int32), jax.ShapeDtypeStruct((8,), jnp.int32)),
        in_specs=[smem] * 3,
        out_specs=(smem, smem),
        cost_estimate=pl.CostEstimate(flops=0, bytes_accessed=20000, transcendentals=0),
    )(live, coded, places)


def product_kernel(sizes, place, lists, counts, tiles, *refs):
    sources, (keep, send, held, blocks, tile_sems, block_sems) = refs[: len(sizes)], refs[len(sizes) :]
    copies = [
        pltpu.make_async_copy(tiles.at[pl.ds(k * SLOTS, SLOTS)], held.at[pl.ds(k * SLOTS, SLOTS)], tile_sems.at[k])
        for k in range(STEPS)
    ]
    first = 0
    for i, size in enumerate(sizes):
        copies.append(pltpu.make_async_copy(sources[i], blocks.at[pl.ds(first, size)], block_sems.at[i]))
        first += size
    for copy in copies:
        copy.start()
    held[N_TILES] = jnp.zeros((TILE, TILE), jnp.bfloat16)
    for copy in copies:
        copy.wait()
    mine = place[0]
    for b in range(8):

        def pair(i, total):
            one, two = lists[b, 2 * i], lists[b, 2 * i + 1]
            left = jnp.concatenate([held[one & 1023], held[two & 1023]], axis=1)
            right = jnp.concatenate([blocks[one >> 10], blocks[two >> 10]], axis=0)
            return total + jnp.dot(left, right, preferred_element_type=jnp.float32)

        total = lax.fori_loop(0, (counts[b] + 1) >> 1, pair, jnp.zeros((TILE, 256), jnp.float32))
        other = (b >> 1) ^ mine
        rows = pl.ds((b & 1) * TILE, TILE)

        @pl.when((other & 1) == 0)
        def _():
            keep[other >> 1, rows, :] = total

        @pl.when((other & 1) == 1)
        def _():
            send[other >> 1, rows, :] = total


def products(place, lists, counts, tiles, found):
    smem, anywhere = pl.BlockSpec(memory_space=pltpu.SMEM), pl.BlockSpec(memory_space=pl.ANY)
    vmem = pl.BlockSpec(memory_space=pltpu.VMEM)
    sizes = tuple(len(f.labels) for f in found)
    half = jax.ShapeDtypeStruct((2, 256, 256), jnp.float32)
    return pl.pallas_call(
        functools.partial(product_kernel, sizes),
        out_shape=(half, half),
        in_specs=[smem] * 3 + [anywhere] * (1 + len(found)),
        out_specs=(vmem, vmem),
        scratch_shapes=[
            pltpu.VMEM((N_TILES + 1, TILE, TILE), jnp.bfloat16),
            pltpu.VMEM((sum(sizes), TILE, 256), jnp.bfloat16),
            pltpu.SemaphoreType.DMA((STEPS,)),
            pltpu.SemaphoreType.DMA((len(sizes),)),
        ],
        compiler_params=pltpu.CompilerParams(vmem_limit_bytes=40 << 20),
        cost_estimate=pl.CostEstimate(flops=3_000_000_000, bytes_accessed=20_000_000, transcendentals=0),
    )(place, lists, counts, tiles, *(f.rows.reshape(-1, TILE, 256) for f in found))


def local(features, degree, tiles, tile_rows, tile_cols, live, weight):
    row, mine = lax.axis_index("row"), lax.axis_index("rep")
    scale = lax.rsqrt(degree.astype(jnp.float32))
    scaled = (features.astype(jnp.float32) * scale[:, None]).astype(jnp.bfloat16)
    found = gather(scaled)

    cols, steps = tile_cols[0, 0], jnp.arange(STEPS, dtype=jnp.int32)[:, None]
    source = (row - mine - 4 * steps) & 63
    piece = cols >> 1
    shift = jnp.where(piece == 3, -1, piece)
    dp = ((source & 7) + shift - row) & 7
    dy = ((source >> 3) - (row >> 3)) & 3
    dh = ((source >> 5) - (row >> 5) - ((mine + dp) >> 2)) & 1
    coded = (((tile_rows[0, 0] * 2 + (cols & 1)) * 2 + dh) * 8 + dp) * 4 + dy
    places = np.zeros(128, np.int32)
    for n, (t, a, b, c) in enumerate(label for f in found for label in f.labels):
        places[((t * 2 + a) * 8 + b) * 4 + c] = n
    lists, counts = slot_lists(live[0, 0], coded, jnp.asarray(places))

    keep, send = products(mine[None], lists, counts, tiles.reshape(N_TILES, TILE, TILE), found)
    devices = range(256)
    halves = keep + lax.ppermute(send, AXES, [(i, i ^ 1) for i in devices])
    share = halves[0] + lax.ppermute(halves[1], AXES, [(i, i ^ 2) for i in devices])
    normed = share * scale[:, None]
    product = jnp.dot(normed, weight.astype(jnp.float32), precision=lax.Precision.HIGHEST)
    return jax.nn.relu(product).astype(jnp.bfloat16)


def solution(mesh):
    in_specs = (
        P(("row", "rep"), None),
        P(("row", "rep")),
        P("row", "rep", None, None, None, None),
        P("row", "rep", None, None),
        P("row", "rep", None, None),
        P("row", "rep", None),
        P(),
    )
    out_specs = P(("row", "rep"), None)
    return jax.shard_map(local, mesh=mesh, in_specs=in_specs, out_specs=out_specs, check_vma=False)
```

time: 573 us -> 175 us (0.31); the launches traced: 567 us -> 176 us
  waiting for transfers between devices: 317 us -> 65 us
  other arithmetic: 131 us -> 7.11 us
  matrix products: 54.7 us -> 0.97 us
  starting transfers between devices: 2.04 us -> 49.9 us
  Pallas kernels: 0 us -> 43.7 us
  local copies, waits for them, and re-layouts: 41.9 us -> 8.66 us
  between operations: 13.5 us -> 0.3 us
  blocking collectives: 6.78 us -> 0 us
    ppermute x17 -> x29, waiting for transfers between devices: 220 us -> 65 us  [the longest x27 54.7 us: moved(): rows = lax.ppermute(self.rows, AXES, route(dh, dp, dy, home))]
    reduce_scatter x1 -> x0, waiting for transfers between devices: 96.4 us -> none  [local(): share = lax.psum_scatter(total, 'rep', scatter_dimension=0, tiled=True)]
    scatter-add x16 -> x0, other arithmetic: 95.7 us -> none  [accumulate(): return shaped.at[dest].add(products).reshape(total.shape)]
    dot_general x16 -> x0, matrix products: 52.8 us -> none  [accumulate(): jnp.einsum('sij,sjf->sif', slab, picked, preferred_element_type=jnp.float32)]
    ppermute x17 -> x29, starting transfers between devices: 2.04 us -> 49.9 us  [the longest x27 49.7 us: moved(): rows = lax.ppermute(self.rows, AXES, route(dh, dp, dy, home))]
    pallas_call x0 -> x2, Pallas kernels: none -> 43.7 us  [the longest x1 36.7 us: products(): pl.pallas_call(functools.partial(product_kernel, sizes), out_shape=(half,...]
    another operation x15 -> x0, local copies, waits for them, and re-layouts: 15.6 us -> none
    select_n x18 -> x0, other arithmetic: 12.1 us -> none  [the longest x16 11.2 us: accumulate(): return shaped.at[dest].add(products).reshape(total.shape)]
  transfers between devices with their start and end apart: 18 -> 29, of which waited for: 18 -> 12; matrix products, arithmetic and copies ran while one was open for 34% -> 4% of each run, Pallas kernels for 0% -> 4%
where the time goes in v1:
time: 175 us; the launch traced here: 176 us
  waiting for transfers between devices  65 us (37%)
  starting transfers between devices  49.9 us (29%)
  Pallas kernels  43.7 us (25%)
  local copies, waits for them, and re-layouts  8.66 us (5%)
  other arithmetic  7.11 us (4%)
    ppermute x27, waiting for transfers between devices, moved(): rows = lax.ppermute(self.rows, AXES, route(dh, dp, dy, home))  54.7 us
    ppermute x27, starting transfers between devices, moved(): rows = lax.ppermute(self.rows, AXES, route(dh, dp, dy, home))  49.7 us
    pallas_call x1, Pallas kernels, products(): pl.pallas_call(functools.partial(product_kernel, sizes), out_shape=(half,...  36.7 us
    ppermute x1, waiting for transfers between devices, local(): lax.ppermute(halves[1], AXES, [(i, i ^ 2) for i in devices])  8.33 us
    unnamed x30, local copies, waits for them, and re-layouts  7.05 us
    pallas_call x1, Pallas kernels, slot_lists(): pl.pallas_call(list_kernel, out_shape=(jax.ShapeDtypeStruct((8, LIST), jn...  7 us
    concatenate x8, other arithmetic, joined(): jnp.concatenate([p.rows for p in parts], 0)  4.63 us
  transfers between devices with their start and end apart: 29, of which 12 were waited for; matrix products, arithmetic and copies ran while one was open for 4% of the time, Pallas kernels for 4%

profile of v1, /device:TPU:6, one launch (start us, length us, event | category | flops | bytes accessed | tf_op | source)
XLA Modules:
  0.0 175.5 jit_solution(5343903601928459409)
XLA Ops:
  0.7 1.0 multiply_convert_fusion
  1.7 4.2 %collective-permute-start.1 = (bf16[256,256]{1,0:T(8,128)(2,1)S(1)}, bf16[256,256]{1,0:T(8,128)(2,1)S(1)}, u32[]{:S(2)}, u32[]{:S(2)}) collective-permute-start(bf16[256,256]{1,0:T(8,128)(2,1)S(1)} %multiply_convert_fusion), channel_id=1, source_target_pairs={{128,0},{157,1},{154,2},{135,3},{132,4},{129,5},{158,6},{139,7},{1... | collective-permute-start | bytes 393224 | tf_op jit(solution)/shard_map/ppermute | solution.py:50
  5.9 6.4 %collective-permute-start = (bf16[256,256]{1,0:T(8,128)(2,1)S(1)}, bf16[256,256]{1,0:T(8,128)(2,1)S(1)}, u32[]{:S(2)}, u32[]{:S(2)}) collective-permute-start(bf16[256,256]{1,0:T(8,128)(2,1)S(1)} %multiply_convert_fusion), channel_id=1, source_target_pairs={{0,0},{29,1},{26,2},{7,3},{4,4},{1,5},{30,6},{11,7},{8,8},{5,9},{2... | collective-permute-start | bytes 393224 | tf_op jit(solution)/shard_map/ppermute | solution.py:50
  12.3 3.9 %collective-permute-done = bf16[256,256]{1,0:T(8,128)(2,1)S(1)} collective-permute-done((bf16[256,256]{1,0:T(8,128)(2,1)S(1)}, bf16[256,256]{1,0:T(8,128)(2,1)S(1)}, u32[]{:S(2)}, u32[]{:S(2)}) %collective-permute-start) | collective-permute-done | bytes 131104 | tf_op jit(solution)/shard_map/ppermute | solution.py:50
  16.3 3.3 %collective-permute-start.4 = (bf16[512,256]{1,0:T(8,128)(2,1)S(1)}, bf16[512,256]{1,0:T(8,128)(2,1)S(1)}, u32[]{:S(2)}, u32[]{:S(2)}) collective-permute-start(bf16[512,256]{1,0:T(8,128)(2,1)S(1)} %pad_maximum_fusion.8), channel_id=1, source_target_pairs={{64,0},{65,1},{66,2},{67,3},{68,4},{69,5},{70,6},{71,7},{72,8},{73... | collective-permute-start | bytes 786440 | tf_op jit(solution)/shard_map/ppermute | solution.py:50
  20.3 2.6 %collective-permute-start.2 = (bf16[512,256]{1,0:T(8,128)(2,1)S(1)}, bf16[512,256]{1,0:T(8,128)(2,1)S(1)}, u32[]{:S(2)}, u32[]{:S(2)}) collective-permute-start(bf16[512,256]{1,0:T(8,128)(2,1)S(1)} %pad_maximum_fusion.8), channel_id=1, source_target_pairs={{32,0},{33,1},{34,2},{35,3},{36,4},{37,5},{38,6},{39,7},{40,8},{41... | collective-permute-start | bytes 786440 | tf_op jit(solution)/shard_map/ppermute | solution.py:50
  22.9 3.9 %collective-permute-start.5 = (bf16[512,256]{1,0:T(8,128)(2,1)S(1)}, bf16[512,256]{1,0:T(8,128)(2,1)S(1)}, u32[]{:S(2)}, u32[]{:S(2)}) collective-permute-start(bf16[512,256]{1,0:T(8,128)(2,1)S(1)} %pad_maximum_fusion.8), channel_id=1, source_target_pairs={{5,0},{6,1},{7,2},{132,3},{9,4},{10,5},{11,6},{136,7},{13,8},{14,9... | collective-permute-start | bytes 786440 | tf_op jit(solution)/shard_map/ppermute | solution.py:50
  26.8 2.7 %collective-permute-done.3 = bf16[512,256]{1,0:T(8,128)(2,1)S(1)} collective-permute-done((bf16[512,256]{1,0:T(8,128)(2,1)S(1)}, bf16[512,256]{1,0:T(8,128)(2,1)S(1)}, u32[]{:S(2)}, u32[]{:S(2)}) %collective-permute-start.3) | collective-permute-done | bytes 262176 | tf_op jit(solution)/shard_map/ppermute | solution.py:50
  29.9 0.9 collective-permute-done.6
  31.5 4.1 %collective-permute-start.10 = (bf16[1280,256]{1,0:T(8,128)(2,1)S(1)}, bf16[1280,256]{1,0:T(8,128)(2,1)S(1)}, u32[]{:S(2)}, u32[]{:S(2)}) collective-permute-start(bf16[1280,256]{1,0:T(8,128)(2,1)S(1)} %get-tuple-element.16), channel_id=1, source_target_pairs={{5,0},{6,1},{7,2},{132,3},{9,4},{10,5},{11,6},{136,7},{13,8},{14,9... | collective-permute-start | bytes 1966088 | tf_op jit(solution)/shard_map/ppermute | solution.py:50
  35.6 15.2 %collective-permute-done.11 = bf16[1280,256]{1,0:T(8,128)(2,1)S(1)} collective-permute-done((bf16[1280,256]{1,0:T(8,128)(2,1)S(1)}, bf16[1280,256]{1,0:T(8,128)(2,1)S(1)}, u32[]{:S(2)}, u32[]{:S(2)}) %collective-permute-start.11) | collective-permute-done | bytes 655392 | tf_op jit(solution)/shard_map/ppermute | solution.py:50
  50.8 3.8 %collective-permute-start.15 = (bf16[1280,256]{1,0:T(8,128)(2,1)S(1)}, bf16[1280,256]{1,0:T(8,128)(2,1)S(1)}, u32[]{:S(2)}, u32[]{:S(2)}) collective-permute-start(bf16[1280,256]{1,0:T(8,128)(2,1)S(1)} %collective-permute-done.10), channel_id=1, source_target_pairs={{5,0},{6,1},{7,2},{132,3},{9,4},{10,5},{11,6},{136,7},{13,8},{14,9... | collective-permute-start | bytes 1966088 | tf_op jit(solution)/shard_map/ppermute | solution.py:50
  55.4 13.6 %collective-permute-done.16 = bf16[1280,256]{1,0:T(8,128)(2,1)S(1)} collective-permute-done((bf16[1280,256]{1,0:T(8,128)(2,1)S(1)}, bf16[1280,256]{1,0:T(8,128)(2,1)S(1)}, u32[]{:S(2)}, u32[]{:S(2)}) %collective-permute-start.16) | collective-permute-done | bytes 655392 | tf_op jit(solution)/shard_map/ppermute | solution.py:50
  70.8 3.9 %collective-permute-start.20 = (bf16[1024,256]{1,0:T(8,128)(2,1)}, bf16[1024,256]{1,0:T(8,128)(2,1)S(1)}, u32[]{:S(2)}, u32[]{:S(2)}) collective-permute-start(bf16[1024,256]{1,0:T(8,128)(2,1)} %pad_maximum_fusion.6), channel_id=1, source_target_pairs={{5,0},{6,1},{7,2},{132,3},{9,4},{10,5},{11,6},{136,7},{13,8},{14,9... | collective-permute-start | bytes 1572872 | tf_op jit(solution)/shard_map/ppermute | solution.py:50
  74.6 3.2 %collective-permute-start.7 = (bf16[512,256]{1,0:T(8,128)(2,1)}, bf16[512,256]{1,0:T(8,128)(2,1)}, u32[]{:S(2)}, u32[]{:S(2)}) collective-permute-start(bf16[512,256]{1,0:T(8,128)(2,1)} %pad_maximum_fusion.9), channel_id=1, source_target_pairs={{32,0},{33,1},{34,2},{35,3},{36,4},{37,5},{38,6},{39,7},{40,8},{41... | collective-permute-start | bytes 786440 | tf_op jit(solution)/shard_map/ppermute | solution.py:50
  80.1 12.5 %collective-permute-done.8 = bf16[512,256]{1,0:T(8,128)(2,1)} collective-permute-done((bf16[512,256]{1,0:T(8,128)(2,1)}, bf16[512,256]{1,0:T(8,128)(2,1)}, u32[]{:S(2)}, u32[]{:S(2)}) %collective-permute-start.8) | collective-permute-done | bytes 262176 | tf_op jit(solution)/shard_map/ppermute | solution.py:50
  92.7 3.2 %collective-permute-start.12 = (bf16[512,256]{1,0:T(8,128)(2,1)}, bf16[512,256]{1,0:T(8,128)(2,1)}, u32[]{:S(2)}, u32[]{:S(2)}) collective-permute-start(bf16[512,256]{1,0:T(8,128)(2,1)} %pad_maximum_fusion.10), channel_id=1, source_target_pairs={{32,0},{33,1},{34,2},{35,3},{36,4},{37,5},{38,6},{39,7},{40,8},{41... | collective-permute-start | bytes 786440 | tf_op jit(solution)/shard_map/ppermute | solution.py:50
  95.9 0.9 collective-permute-start.18
  96.9 2.4 %collective-permute-start.17 = (bf16[512,256]{1,0:T(8,128)(2,1)}, bf16[512,256]{1,0:T(8,128)(2,1)}, u32[]{:S(2)}, u32[]{:S(2)}) collective-permute-start(bf16[512,256]{1,0:T(8,128)(2,1)} %pad_maximum_fusion.11), channel_id=1, source_target_pairs={{32,0},{33,1},{34,2},{35,3},{36,4},{37,5},{38,6},{39,7},{40,8},{41... | collective-permute-start | bytes 786440 | tf_op jit(solution)/shard_map/ppermute | solution.py:50
  101.3 4.8 %collective-permute-done.13 = bf16[512,256]{1,0:T(8,128)(2,1)} collective-permute-done((bf16[512,256]{1,0:T(8,128)(2,1)}, bf16[512,256]{1,0:T(8,128)(2,1)}, u32[]{:S(2)}, u32[]{:S(2)}) %collective-permute-start.13) | collective-permute-done | bytes 262176 | tf_op jit(solution)/shard_map/ppermute | solution.py:50
  106.6 2.8 %collective-permute-start.22 = (bf16[256,256]{1,0:T(8,128)(2,1)}, bf16[256,256]{1,0:T(8,128)(2,1)}, u32[]{:S(2)}, u32[]{:S(2)}) collective-permute-start(bf16[256,256]{1,0:T(8,128)(2,1)} %pad_maximum_fusion.12), channel_id=1, source_target_pairs={{32,0},{33,1},{34,2},{35,3},{36,4},{37,5},{38,6},{39,7},{40,8},{41... | collective-permute-start | bytes 393224 | tf_op jit(solution)/shard_map/ppermute | solution.py:50
  109.5 3.9 %collective-permute-start.25 = (bf16[384,256]{1,0:T(8,128)(2,1)}, bf16[384,256]{1,0:T(8,128)(2,1)}, u32[]{:S(2)}, u32[]{:S(2)}) collective-permute-start(bf16[384,256]{1,0:T(8,128)(2,1)} %slice.118), channel_id=1, source_target_pairs={{5,0},{6,1},{7,2},{132,3},{9,4},{10,5},{11,6},{136,7},{13,8},{14,9... | collective-permute-start | bytes 589832 | tf_op jit(solution)/shard_map/ppermute | solution.py:50
  114.0 7.0 %shard_map.82 = (s32[8,256]{1,0:T(8,128)}, s32[8]{0:T(128)}) custom-call(s32[16]{0:T(128)} %bitcast.67, s32[16,22]{1,0:T(8,128)} %fusion.11.coded, s32[128]{0:T(128)} %constant.13.clone.places), custom_call_target="tpu_custom_call" | custom-call | bytes 20000 | tf_op jit(solution)/shard_map/pallas_call | solution.py:110
  121.1 1.1 copy-done.2
  122.1 1.1 copy-done.4
  123.2 0.9 copy-done.6
  124.2 0.9 copy-done.8
  125.1 0.9 copy-done.10
  127.4 36.7 %shard_map.83 = (f32[2,256,256]{2,1,0:T(8,128)S(1)}, f32[2,256,256]{2,1,0:T(8,128)S(1)}) custom-call(s32[1]{0:T(128)} %bitcast.place, s32[8,256]{1,0:T(8,128)S(1)} %copy-done.11, s32[8]{0:T(128)S(1)} %copy-done.12, bf16[352,128,128]{2,1,0:T(8,128)(2,1)} %bitcast.66, bf16[4,128,256]{2,1,0:T(8,128)(2,1)S(1)} %bitcast.59, bf16[4,128,256]{2,1,0:T(8,128)(2,1)S(1)} %bitcast.64, ...), custom_call_target="tpu_custom_call" | custom-call | flops 3000000000 | bytes 20000000 | tf_op jit(solution)/shard_map/pallas_call | solution.py:161
  164.1 1.9 %collective-permute-done.27 = f32[2,256,256]{2,1,0:T(8,128)S(1)} collective-permute-done((f32[2,256,256]{2,1,0:T(8,128)S(1)}, f32[2,256,256]{2,1,0:T(8,128)S(1)}, u32[]{:S(2)}, u32[]{:S(2)}) %collective-permute-start.27) | collective-permute-done | bytes 524320 | tf_op jit(solution)/shard_map/ppermute | solution.py:198
  166.2 8.3 %collective-permute-done.28 = f32[256,256]{1,0:T(8,128)S(1)} collective-permute-done((f32[256,256]{1,0:T(8,128)S(1)}, f32[256,256]{1,0:T(8,128)S(1)}, u32[]{:S(2)}, u32[]{:S(2)}) %collective-permute-start.28) | collective-permute-done | bytes 262176 | tf_op jit(solution)/shard_map/ppermute | solution.py:199
  174.6 1.0 fusion
  (93 shorter events, 12.1 us)
Async XLA Ops:
  0.0 174.6 %copy-start = (bf16[256,256]{1,0:T(8,128)(2,1)S(1)}, bf16[256,256]{1,0:T(8,128)(2,1)}, u32[]{:S(2)}) copy-start(bf16[256,256]{1,0:T(8,128)(2,1)} %param.14) | copy-start | bytes 393220
  1.7 10.6 %collective-permute-start.1 = (bf16[256,256]{1,0:T(8,128)(2,1)S(1)}, bf16[256,256]{1,0:T(8,128)(2,1)S(1)}, u32[]{:S(2)}, u32[]{:S(2)}) collective-permute-start(bf16[256,256]{1,0:T(8,128)(2,1)S(1)} %multiply_convert_fusion), channel_id=1, source_target_pairs={{128,0},{157,1},{154,2},{135,3},{132,4},{129,5},{158,6},{139,7},{1... | collective-permute-start | bytes 393224 | tf_op jit(solution)/shard_map/ppermute | solution.py:50
  5.9 10.4 %collective-permute-start = (bf16[256,256]{1,0:T(8,128)(2,1)S(1)}, bf16[256,256]{1,0:T(8,128)(2,1)S(1)}, u32[]{:S(2)}, u32[]{:S(2)}) collective-permute-start(bf16[256,256]{1,0:T(8,128)(2,1)S(1)} %multiply_convert_fusion), channel_id=1, source_target_pairs={{0,0},{29,1},{26,2},{7,3},{4,4},{1,5},{30,6},{11,7},{8,8},{5,9},{2... | collective-permute-start | bytes 393224 | tf_op jit(solution)/shard_map/ppermute | solution.py:50
  16.3 10.4 %collective-permute-start.4 = (bf16[512,256]{1,0:T(8,128)(2,1)S(1)}, bf16[512,256]{1,0:T(8,128)(2,1)S(1)}, u32[]{:S(2)}, u32[]{:S(2)}) collective-permute-start(bf16[512,256]{1,0:T(8,128)(2,1)S(1)} %pad_maximum_fusion.8), channel_id=1, source_target_pairs={{64,0},{65,1},{66,2},{67,3},{68,4},{69,5},{70,6},{71,7},{72,8},{73... | collective-permute-start | bytes 786440 | tf_op jit(solution)/shard_map/ppermute | solution.py:50
  19.6 9.9 %collective-permute-start.3 = (bf16[512,256]{1,0:T(8,128)(2,1)S(1)}, bf16[512,256]{1,0:T(8,128)(2,1)S(1)}, u32[]{:S(2)}, u32[]{:S(2)}) collective-permute-start(bf16[512,256]{1,0:T(8,128)(2,1)S(1)} %pad_maximum_fusion.8), channel_id=1, source_target_pairs={{96,0},{97,1},{98,2},{99,3},{100,4},{101,5},{102,6},{103,7},{104,8... | collective-permute-start | bytes 786440 | tf_op jit(solution)/shard_map/ppermute | solution.py:50
  20.3 9.6 %collective-permute-start.2 = (bf16[512,256]{1,0:T(8,128)(2,1)S(1)}, bf16[512,256]{1,0:T(8,128)(2,1)S(1)}, u32[]{:S(2)}, u32[]{:S(2)}) collective-permute-start(bf16[512,256]{1,0:T(8,128)(2,1)S(1)} %pad_maximum_fusion.8), channel_id=1, source_target_pairs={{32,0},{33,1},{34,2},{35,3},{36,4},{37,5},{38,6},{39,7},{40,8},{41... | collective-permute-start | bytes 786440 | tf_op jit(solution)/shard_map/ppermute | solution.py:50
  22.8 7.9 %collective-permute-start.6 = (bf16[512,256]{1,0:T(8,128)(2,1)S(1)}, bf16[512,256]{1,0:T(8,128)(2,1)S(1)}, u32[]{:S(2)}, u32[]{:S(2)}) collective-permute-start(bf16[512,256]{1,0:T(8,128)(2,1)S(1)} %pad_maximum_fusion.8), channel_id=1, source_target_pairs={{159,0},{28,1},{29,2},{30,3},{131,4},{0,5},{1,6},{2,7},{135,8},{4,... | collective-permute-start | bytes 786440 | tf_op jit(solution)/shard_map/ppermute | solution.py:50
  22.9 8.4 %collective-permute-start.5 = (bf16[512,256]{1,0:T(8,128)(2,1)S(1)}, bf16[512,256]{1,0:T(8,128)(2,1)S(1)}, u32[]{:S(2)}, u32[]{:S(2)}) collective-permute-start(bf16[512,256]{1,0:T(8,128)(2,1)S(1)} %pad_maximum_fusion.8), channel_id=1, source_target_pairs={{5,0},{6,1},{7,2},{132,3},{9,4},{10,5},{11,6},{136,7},{13,8},{14,9... | collective-permute-start | bytes 786440 | tf_op jit(solution)/shard_map/ppermute | solution.py:50
  31.4 19.4 %collective-permute-start.11 = (bf16[1280,256]{1,0:T(8,128)(2,1)S(1)}, bf16[1280,256]{1,0:T(8,128)(2,1)S(1)}, u32[]{:S(2)}, u32[]{:S(2)}) collective-permute-start(bf16[1280,256]{1,0:T(8,128)(2,1)S(1)} %get-tuple-element.15), channel_id=1, source_target_pairs={{159,0},{28,1},{29,2},{30,3},{131,4},{0,5},{1,6},{2,7},{135,8},{4,... | collective-permute-start | bytes 1966088 | tf_op jit(solution)/shard_map/ppermute | solution.py:50
  31.5 19.3 %collective-permute-start.10 = (bf16[1280,256]{1,0:T(8,128)(2,1)S(1)}, bf16[1280,256]{1,0:T(8,128)(2,1)S(1)}, u32[]{:S(2)}, u32[]{:S(2)}) collective-permute-start(bf16[1280,256]{1,0:T(8,128)(2,1)S(1)} %get-tuple-element.16), channel_id=1, source_target_pairs={{5,0},{6,1},{7,2},{132,3},{9,4},{10,5},{11,6},{136,7},{13,8},{14,9... | collective-permute-start | bytes 1966088 | tf_op jit(solution)/shard_map/ppermute | solution.py:50
  50.7 18.3 %collective-permute-start.16 = (bf16[1280,256]{1,0:T(8,128)(2,1)S(1)}, bf16[1280,256]{1,0:T(8,128)(2,1)S(1)}, u32[]{:S(2)}, u32[]{:S(2)}) collective-permute-start(bf16[1280,256]{1,0:T(8,128)(2,1)S(1)} %collective-permute-done.11), channel_id=1, source_target_pairs={{159,0},{28,1},{29,2},{30,3},{131,4},{0,5},{1,6},{2,7},{135,8},{4,... | collective-permute-start | bytes 1966088 | tf_op jit(solution)/shard_map/ppermute | solution.py:50
  50.8 27.1 %copy-start.3 = (bf16[1280,256]{1,0:T(8,128)(2,1)}, bf16[1280,256]{1,0:T(8,128)(2,1)S(1)}, u32[]{:S(2)}) copy-start(bf16[1280,256]{1,0:T(8,128)(2,1)S(1)} %collective-permute-done.10) | copy-start | bytes 1966084
  50.8 19.1 %collective-permute-start.15 = (bf16[1280,256]{1,0:T(8,128)(2,1)S(1)}, bf16[1280,256]{1,0:T(8,128)(2,1)S(1)}, u32[]{:S(2)}, u32[]{:S(2)}) collective-permute-start(bf16[1280,256]{1,0:T(8,128)(2,1)S(1)} %collective-permute-done.10), channel_id=1, source_target_pairs={{5,0},{6,1},{7,2},{132,3},{9,4},{10,5},{11,6},{136,7},{13,8},{14,9... | collective-permute-start | bytes 1966088 | tf_op jit(solution)/shard_map/ppermute | solution.py:50
  55.4 23.3 %collective-permute-start.9 = (bf16[512,256]{1,0:T(8,128)(2,1)}, bf16[512,256]{1,0:T(8,128)(2,1)S(1)}, u32[]{:S(2)}, u32[]{:S(2)}) collective-permute-start(bf16[512,256]{1,0:T(8,128)(2,1)} %pad_maximum_fusion.9), channel_id=1, source_target_pairs={{64,0},{65,1},{66,2},{67,3},{68,4},{69,5},{70,6},{71,7},{72,8},{73... | collective-permute-start | bytes 786440 | tf_op jit(solution)/shard_map/ppermute | solution.py:50
  69.9 26.0 %collective-permute-start.21 = (bf16[1024,256]{1,0:T(8,128)(2,1)}, bf16[1024,256]{1,0:T(8,128)(2,1)S(1)}, u32[]{:S(2)}, u32[]{:S(2)}) collective-permute-start(bf16[1024,256]{1,0:T(8,128)(2,1)} %pad_maximum_fusion.7), channel_id=1, source_target_pairs={{159,0},{28,1},{29,2},{30,3},{131,4},{0,5},{1,6},{2,7},{135,8},{4,... | collective-permute-start | bytes 1572872 | tf_op jit(solution)/shard_map/ppermute | solution.py:50
  70.8 26.1 %collective-permute-start.20 = (bf16[1024,256]{1,0:T(8,128)(2,1)}, bf16[1024,256]{1,0:T(8,128)(2,1)S(1)}, u32[]{:S(2)}, u32[]{:S(2)}) collective-permute-start(bf16[1024,256]{1,0:T(8,128)(2,1)} %pad_maximum_fusion.6), channel_id=1, source_target_pairs={{5,0},{6,1},{7,2},{132,3},{9,4},{10,5},{11,6},{136,7},{13,8},{14,9... | collective-permute-start | bytes 1572872 | tf_op jit(solution)/shard_map/ppermute | solution.py:50
  74.6 18.1 %collective-permute-start.8 = (bf16[512,256]{1,0:T(8,128)(2,1)}, bf16[512,256]{1,0:T(8,128)(2,1)}, u32[]{:S(2)}, u32[]{:S(2)}) collective-permute-start(bf16[512,256]{1,0:T(8,128)(2,1)} %pad_maximum_fusion.9), channel_id=1, source_target_pairs={{96,0},{97,1},{98,2},{99,3},{100,4},{101,5},{102,6},{103,7},{104,8... | collective-permute-start | bytes 786440 | tf_op jit(solution)/shard_map/ppermute | solution.py:50
  74.6 18.1 %collective-permute-start.7 = (bf16[512,256]{1,0:T(8,128)(2,1)}, bf16[512,256]{1,0:T(8,128)(2,1)}, u32[]{:S(2)}, u32[]{:S(2)}) collective-permute-start(bf16[512,256]{1,0:T(8,128)(2,1)} %pad_maximum_fusion.9), channel_id=1, source_target_pairs={{32,0},{33,1},{34,2},{35,3},{36,4},{37,5},{38,6},{39,7},{40,8},{41... | collective-permute-start | bytes 786440 | tf_op jit(solution)/shard_map/ppermute | solution.py:50
  78.7 34.7 %copy-start.13 = (s32[1,1,16,22]{3,2,1,0:T(8,128)S(1)}, s32[1,1,16,22]{3,2,1,0:T(8,128)}, u32[]{:S(2)}) copy-start(s32[1,1,16,22]{3,2,1,0:T(8,128)} %param.12) | copy-start | bytes 4228
  79.4 16.6 %collective-permute-start.14 = (bf16[512,256]{1,0:T(8,128)(2,1)}, bf16[512,256]{1,0:T(8,128)(2,1)}, u32[]{:S(2)}, u32[]{:S(2)}) collective-permute-start(bf16[512,256]{1,0:T(8,128)(2,1)} %pad_maximum_fusion.10), channel_id=1, source_target_pairs={{64,0},{65,1},{66,2},{67,3},{68,4},{69,5},{70,6},{71,7},{72,8},{73... | collective-permute-start | bytes 786440 | tf_op jit(solution)/shard_map/ppermute | solution.py:50
  92.7 13.5 %collective-permute-start.13 = (bf16[512,256]{1,0:T(8,128)(2,1)}, bf16[512,256]{1,0:T(8,128)(2,1)}, u32[]{:S(2)}, u32[]{:S(2)}) collective-permute-start(bf16[512,256]{1,0:T(8,128)(2,1)} %pad_maximum_fusion.10), channel_id=1, source_target_pairs={{96,0},{97,1},{98,2},{99,3},{100,4},{101,5},{102,6},{103,7},{104,8... | collective-permute-start | bytes 786440 | tf_op jit(solution)/shard_map/ppermute | solution.py:50
  92.7 13.5 %collective-permute-start.12 = (bf16[512,256]{1,0:T(8,128)(2,1)}, bf16[512,256]{1,0:T(8,128)(2,1)}, u32[]{:S(2)}, u32[]{:S(2)}) collective-permute-start(bf16[512,256]{1,0:T(8,128)(2,1)} %pad_maximum_fusion.10), channel_id=1, source_target_pairs={{32,0},{33,1},{34,2},{35,3},{36,4},{37,5},{38,6},{39,7},{40,8},{41... | collective-permute-start | bytes 786440 | tf_op jit(solution)/shard_map/ppermute | solution.py:50
  95.9 10.7 %collective-permute-start.19 = (bf16[512,256]{1,0:T(8,128)(2,1)}, bf16[512,256]{1,0:T(8,128)(2,1)}, u32[]{:S(2)}, u32[]{:S(2)}) collective-permute-start(bf16[512,256]{1,0:T(8,128)(2,1)} %pad_maximum_fusion.11), channel_id=1, source_target_pairs={{64,0},{65,1},{66,2},{67,3},{68,4},{69,5},{70,6},{71,7},{72,8},{73... | collective-permute-start | bytes 786440 | tf_op jit(solution)/shard_map/ppermute | solution.py:50
  95.9 13.5 %collective-permute-start.18 = (bf16[512,256]{1,0:T(8,128)(2,1)}, bf16[512,256]{1,0:T(8,128)(2,1)}, u32[]{:S(2)}, u32[]{:S(2)}) collective-permute-start(bf16[512,256]{1,0:T(8,128)(2,1)} %pad_maximum_fusion.11), channel_id=1, source_target_pairs={{96,0},{97,1},{98,2},{99,3},{100,4},{101,5},{102,6},{103,7},{104,8... | collective-permute-start | bytes 786440 | tf_op jit(solution)/shard_map/ppermute | solution.py:50
  96.9 12.6 %collective-permute-start.17 = (bf16[512,256]{1,0:T(8,128)(2,1)}, bf16[512,256]{1,0:T(8,128)(2,1)}, u32[]{:S(2)}, u32[]{:S(2)}) collective-permute-start(bf16[512,256]{1,0:T(8,128)(2,1)} %pad_maximum_fusion.11), channel_id=1, source_target_pairs={{32,0},{33,1},{34,2},{35,3},{36,4},{37,5},{38,6},{39,7},{40,8},{41... | collective-permute-start | bytes 786440 | tf_op jit(solution)/shard_map/ppermute | solution.py:50
  106.2 14.8 %collective-permute-start.24 = (bf16[256,256]{1,0:T(8,128)(2,1)}, bf16[256,256]{1,0:T(8,128)(2,1)}, u32[]{:S(2)}, u32[]{:S(2)}) collective-permute-start(bf16[256,256]{1,0:T(8,128)(2,1)} %pad_maximum_fusion.12), channel_id=1, source_target_pairs={{64,0},{65,1},{66,2},{67,3},{68,4},{69,5},{70,6},{71,7},{72,8},{73... | collective-permute-start | bytes 393224 | tf_op jit(solution)/shard_map/ppermute | solution.py:50
  106.2 14.8 %collective-permute-start.23 = (bf16[256,256]{1,0:T(8,128)(2,1)}, bf16[256,256]{1,0:T(8,128)(2,1)}, u32[]{:S(2)}, u32[]{:S(2)}) collective-permute-start(bf16[256,256]{1,0:T(8,128)(2,1)} %pad_maximum_fusion.12), channel_id=1, source_target_pairs={{96,0},{97,1},{98,2},{99,3},{100,4},{101,5},{102,6},{103,7},{104,8... | collective-permute-start | bytes 393224 | tf_op jit(solution)/shard_map/ppermute | solution.py:50
  106.6 14.4 %collective-permute-start.22 = (bf16[256,256]{1,0:T(8,128)(2,1)}, bf16[256,256]{1,0:T(8,128)(2,1)}, u32[]{:S(2)}, u32[]{:S(2)}) collective-permute-start(bf16[256,256]{1,0:T(8,128)(2,1)} %pad_maximum_fusion.12), channel_id=1, source_target_pairs={{32,0},{33,1},{34,2},{35,3},{36,4},{37,5},{38,6},{39,7},{40,8},{41... | collective-permute-start | bytes 393224 | tf_op jit(solution)/shard_map/ppermute | solution.py:50
  109.4 11.6 %collective-permute-start.26 = (bf16[384,256]{1,0:T(8,128)(2,1)}, bf16[384,256]{1,0:T(8,128)(2,1)}, u32[]{:S(2)}, u32[]{:S(2)}) collective-permute-start(bf16[384,256]{1,0:T(8,128)(2,1)} %slice.119), channel_id=1, source_target_pairs={{159,0},{28,1},{29,2},{30,3},{131,4},{0,5},{1,6},{2,7},{135,8},{4,... | collective-permute-start | bytes 589832 | tf_op jit(solution)/shard_map/ppermute | solution.py:50
  109.5 11.6 %collective-permute-start.25 = (bf16[384,256]{1,0:T(8,128)(2,1)}, bf16[384,256]{1,0:T(8,128)(2,1)}, u32[]{:S(2)}, u32[]{:S(2)}) collective-permute-start(bf16[384,256]{1,0:T(8,128)(2,1)} %slice.118), channel_id=1, source_target_pairs={{5,0},{6,1},{7,2},{132,3},{9,4},{10,5},{11,6},{136,7},{13,8},{14,9... | collective-permute-start | bytes 589832 | tf_op jit(solution)/shard_map/ppermute | solution.py:50
  164.0 2.0 %collective-permute-start.27 = (f32[2,256,256]{2,1,0:T(8,128)S(1)}, f32[2,256,256]{2,1,0:T(8,128)S(1)}, u32[]{:S(2)}, u32[]{:S(2)}) collective-permute-start(f32[2,256,256]{2,1,0:T(8,128)S(1)} %get-tuple-element.12), channel_id=1, source_target_pairs={{0,1},{1,0},{2,3},{3,2},{4,5},{5,4},{6,7},{7,6},{8,9},{9,8},{10,11... | collective-permute-start | bytes 1572872 | tf_op jit(solution)/shard_map/ppermute | solution.py:198
  166.1 8.4 %collective-permute-start.28 = (f32[256,256]{1,0:T(8,128)S(1)}, f32[256,256]{1,0:T(8,128)S(1)}, u32[]{:S(2)}, u32[]{:S(2)}) collective-permute-start(f32[256,256]{1,0:T(8,128)S(1)} %slice_bitcast_fusion), channel_id=1, source_target_pairs={{0,2},{1,3},{2,0},{3,1},{4,6},{5,7},{6,4},{7,5},{8,10},{9,11},{10,... | collective-permute-start | bytes 786440 | tf_op jit(solution)/shard_map/ppermute | solution.py:199
  (12 other events, 74.8 us)

commit v2 on v0

v2 whole, which is shorter than its diff:
```python
import functools

import jax
import jax.numpy as jnp
import numpy as np
from jax import lax
from jax.experimental import pallas as pl
from jax.experimental.pallas import tpu as pltpu
from jax.sharding import PartitionSpec as P

AXES = ("row", "rep")
TILE = 128
SLOTS = 22
STEPS = 16
N_TILES = STEPS * SLOTS
LIST = 128
BATCH = 4
PHASES = 5

HOME = (0, 1, 2, -1)


def member(h, y, z, q):
    return (((h % 2) * 4 + y % 4) * 8 + z % 8) * 4 + q % 4


def up(h, y, z, q):
    return member(h + (q == 3), y, z + 1, q + 1)


def down(h, y, z, q):
    return member(h - (q == 0), y, z - 1, q - 1)


MOVES = {
    "home": (lambda h, y, z, q: member(h, y, z - HOME[q], q), lambda t, h, p, e: (t, h, p, e)),
    "far": (lambda h, y, z, q: member(h + 1, y, z - HOME[q], q), lambda t, h, p, e: (t, 1 - h, p, e)),
    "z1": (lambda *d: down(*d) if d[3] % 2 else up(*d), lambda t, h, p, e: (t, h, (1 - p) % 8, e)),
    "z2": (lambda *d: up(*d) if d[3] % 2 else down(*d), lambda t, h, p, e: (t, h, (-1 - p) % 8, e)),
    "y1": (lambda h, y, z, q: member(h, y ^ (3 if q % 2 else 1), z, q), lambda t, h, p, e: (t, h, p, e ^ 1)),
    "y2": (lambda h, y, z, q: member(h, y ^ (1 if q % 2 else 3), z, q), lambda t, h, p, e: (t, h, p, e ^ 2)),
}


class Blocks:
    def __init__(self, rows, labels):
        self.rows, self.labels = rows, labels

    def __getitem__(self, blocks):
        first, last = blocks.start or 0, len(self.labels) if blocks.stop is None else blocks.stop
        return Blocks(lax.slice_in_dim(self.rows, first * TILE, last * TILE), self.labels[first:last])

    def moved(self, kind):
        sender, relabel = MOVES[kind]
        here = [(h, y, z, q) for h in range(2) for y in range(4) for z in range(8) for q in range(4)]
        rows = lax.ppermute(self.rows, AXES, [(sender(*d), member(*d)) for d in here])
        return Blocks(rows, [relabel(*label) for label in self.labels])

    def half(self, t):
        runs, first = [], 0
        for last in range(1, len(self.labels) + 1):
            if last == len(self.labels) or self.labels[last][0] != self.labels[first][0]:
                if self.labels[first][0] == t:
                    runs.append(self[first:last])
                first = last
        return joined(*runs)


def joined(*parts):
    return Blocks(jnp.concatenate([p.rows for p in parts], 0), [label for p in parts for label in p.labels])


def in_order(parts, *earlier):
    rows = lax.optimization_barrier(tuple(p.rows for p in parts) + earlier)
    return [Blocks(r, p.labels) for r, p in zip(rows, parts)]


def gather(scaled, first_ready, ready, add):
    own = Blocks(scaled, [(0, 0, 0, 0), (1, 0, 0, 0)])
    near, far = own.moved("home"), own.moved("far")
    (s0,) = in_order([joined(near[0:1], far[0:1], near[1:2], far[1:2])], first_ready)
    s1, e1 = s0.moved("z1"), s0.moved("y1")
    s2, e2 = joined(s0, s1).moved("z2"), joined(s0, e1).moved("y2")
    b0 = joined(e1.half(1), e2.half(1))
    z, y1 = in_order([joined(s2, b0), joined(s1.half(0), s2.half(0))], ready)
    z3, y1a = z.moved("z1"), y1.moved("y1")
    total = add(None, [s0, s1, e1, s2, e2])
    z, y = in_order([joined(z3[0:8], b0, z3[8:14]), joined(y1, y1a)], total)
    z4, y1b = z.moved("z2"), y.moved("y2")
    total = add(total, [z3, y1a])
    b, y2 = in_order([z4[8:20], joined(z3[0:8].half(0), z4[0:8].half(0))], total)
    b3, y2a = b.moved("z1"), y2.moved("y1")
    total = add(total, [z4, y1b])
    b, y = in_order([b3, joined(y2, y2a)], total)
    b4, y2b = b.moved("z2"), y.moved("y2")
    total = add(total, [b3, y2a])
    return add(total, [b4, y2b])


def phase_labels():
    found = []

    def traced(rows):
        return gather(rows, rows, rows, lambda _, parts: found.append([label for p in parts for label in p.labels]) or rows)

    jax.eval_shape(traced, jax.ShapeDtypeStruct((2 * TILE, 256), jnp.bfloat16))
    return found


def list_kernel(live, coded, tiles, lists, counts, held, sem):
    load = pltpu.make_async_copy(tiles, held, sem)
    load.start()
    for b in range(8 * PHASES):
        counts[b] = 0

    def one_source(k, _):
        def one_slot(s, _):
            v = coded[k, s]
            b = v >> 17
            n = counts[b]
            lists[b, n] = v & 0x1FFFF
            counts[b] = n + 1
            return 0

        return lax.fori_loop(0, live[k], one_slot, 0)

    lax.fori_loop(0, STEPS, one_source, 0)
    for b in range(8 * PHASES):
        for i in range(BATCH - 1):
            lists[b, counts[b] + i] = 0
    load.wait()


def slot_lists(live, coded, tiles):
    smem, vmem = pl.BlockSpec(memory_space=pltpu.SMEM), pl.BlockSpec(memory_space=pltpu.VMEM)
    return pl.pallas_call(
        list_kernel,
        out_shape=(
            jax.ShapeDtypeStruct((8 * PHASES, LIST), jnp.int32),
            jax.ShapeDtypeStruct((8 * PHASES,), jnp.int32),
            jax.ShapeDtypeStruct(tiles.shape, tiles.dtype),
        ),
        in_specs=[smem, smem, pl.BlockSpec(memory_space=pltpu.HBM)],
        out_specs=(smem, smem, vmem),
        scratch_shapes=[pltpu.SemaphoreType.DMA],
        compiler_params=pltpu.CompilerParams(vmem_limit_bytes=42 << 20),
        cost_estimate=pl.CostEstimate(flops=0, bytes_accessed=23_000_000, transcendentals=0),
    )(live, coded, tiles)


def product_kernel(buckets, first_bucket, more, lists, counts, tiles, blocks, *refs):
    before, total = refs if more else (None, refs[0])
    for b in range(buckets):

        def batch(i, total, b=b):
            at = [lists[first_bucket + b, i * BATCH + j] for j in range(BATCH)]
            left = jnp.concatenate([tiles[a & 1023] for a in at], axis=1)
            right = jnp.concatenate([blocks[a >> 10] for a in at], axis=0)
            return total + jnp.dot(left, right, preferred_element_type=jnp.float32)

        rows = pl.ds((b % 2) * TILE, TILE)
        start = before[b // 2, rows, :] if more else jnp.zeros((TILE, 256), jnp.float32)
        n = (counts[first_bucket + b] + (BATCH - 1)) // BATCH
        total[b // 2, rows, :] = lax.fori_loop(0, n, batch, start)


def products(lists, counts, first_bucket, buckets, tiles, blocks, before=None):
    smem, vmem = pl.BlockSpec(memory_space=pltpu.SMEM), pl.BlockSpec(memory_space=pltpu.VMEM)
    more = before is not None
    slots = blocks.shape[0] * 3 * buckets // 8
    return pl.pallas_call(
        functools.partial(product_kernel, buckets, first_bucket, more),
        out_shape=jax.ShapeDtypeStruct((buckets // 2, 256, 256), jnp.float32),
        in_specs=[smem] * 2 + [vmem] * (2 + more),
        out_specs=vmem,
        compiler_params=pltpu.CompilerParams(vmem_limit_bytes=2 << 20),
        cost_estimate=pl.CostEstimate(flops=slots * 8_400_000, bytes_accessed=slots * 150_000, transcendentals=0),
    )(lists, counts, tiles, blocks, *([before] if more else []))


def local(features, degree, tiles, tile_rows, tile_cols, live, weight):
    row, mine = lax.axis_index("row"), lax.axis_index("rep")
    scale = lax.rsqrt(degree.astype(jnp.float32))
    scaled = (features.astype(jnp.float32) * scale[:, None]).astype(jnp.bfloat16)

    cols, steps = tile_cols[0, 0], jnp.arange(STEPS, dtype=jnp.int32)[:, None]
    source = (row - mine - 4 * steps) & 63
    piece, t = cols >> 1, cols & 1
    p = ((source & 7) + jnp.where(piece == 3, -1, piece) - row) & 7
    h = ((source >> 5) - (row >> 5) - ((mine + p) >> 2)) & 1
    core = mine & 1
    p = jnp.where(core == 1, -p & 7, p)
    y = ((source >> 3) ^ (row >> 3)) & 3
    swapped = jnp.where(t == 0, core, piece & 1)
    e = jnp.where(y == 2, 3, jnp.where(y == 0, 0, jnp.where(y == 1, 1 + swapped, 2 - swapped)))
    dest = tile_rows[0, 0]
    bucket = ((((dest >> 1) ^ mine) ^ 2) << 1) + (dest & 1)
    label = (((t * 2 + h) * 8 + p) * 4 + e)[..., None]
    places = np.zeros(128, np.int32)
    for n, found in enumerate(phase_labels()):
        for i, (t, h, p, e) in enumerate(found):
            places[((t * 2 + h) * 8 + p) * 4 + e] = ((8 * n) << 17) + ((i + 1) << 10)
    place = jnp.sum(jnp.where(label == jnp.arange(128, dtype=jnp.int32), jnp.asarray(places), 0), axis=-1)
    coded = place + (bucket << 17) + steps * SLOTS + jnp.arange(SLOTS, dtype=jnp.int32)
    lists, counts, held = slot_lists(live[0, 0], coded, tiles.reshape(N_TILES, TILE, TILE))
    devices = range(256)
    nothing = jnp.zeros((TILE, 256), jnp.bfloat16)
    n = 0

    def add(total, found):
        nonlocal n
        first, n = 8 * n, n + 1
        blocks = jnp.concatenate([nothing] + [f.rows for f in found], 0).reshape(-1, TILE, 256)
        if n < PHASES:
            return products(lists, counts, first, 8, held, blocks, total)
        theirs = to_owner_core(products(lists, counts, first, 4, held, blocks, total[0:2]))
        theirs, total = lax.optimization_barrier((theirs, total))
        theirs = lax.ppermute(theirs, AXES, [(i, i ^ 2) for i in devices])
        return to_owner_core(products(lists, counts, first + 4, 4, held, blocks, total[2:4])), theirs

    def to_owner_core(part):
        return part[0] + lax.ppermute(part[1], AXES, [(i, i ^ 1) for i in devices])

    def weighted(share):
        return jnp.dot(share * scale[:, None], weight.astype(jnp.float32), precision=lax.Precision.HIGHEST)

    ours, theirs = gather(scaled, coded, counts, add)
    return jax.nn.relu(weighted(ours) + weighted(theirs)).astype(jnp.bfloat16)


def solution(mesh):
    in_specs = (
        P(("row", "rep"), None),
        P(("row", "rep")),
        P("row", "rep", None, None, None, None),
        P("row", "rep", None, None),
        P("row", "rep", None, None),
        P("row", "rep", None),
        P(),
    )
    out_specs = P(("row", "rep"), None)
    return jax.shard_map(local, mesh=mesh, in_specs=in_specs, out_specs=out_specs, check_vma=False)
```

time: 573 us -> 113 us (0.20)
  the two profiles are of different devices: /device:TPU:6 before, /device:TPU:1 now
where the time goes in v2:
time: 113 us
  waiting for transfers between devices  50.6 us (45%)
  starting transfers between devices  30.8 us (27%)
  Pallas kernels  23.9 us (21%)
  other arithmetic  5.34 us (5%)
  matrix products  1.29 us (1%)
    ppermute x14, waiting for transfers between devices, moved(): lax.ppermute(self.rows, AXES, [(sender(*d), member(*d)) for d in here])  44.9 us
    ppermute x14, starting transfers between devices, moved(): lax.ppermute(self.rows, AXES, [(sender(*d), member(*d)) for d in here])  29.4 us
    pallas_call x6, Pallas kernels, products(): pl.pallas_call(functools.partial(product_kernel, buckets, first_bucket, m...  18 us
    pallas_call x1, Pallas kernels, slot_lists(): pl.pallas_call(list_kernel, out_shape=(jax.ShapeDtypeStruct((8 * PHASES,...  5.88 us
    ppermute x1, waiting for transfers between devices, add(): theirs = lax.ppermute(theirs, AXES, [(i, i ^ 2) for i in devices])  4.5 us
  transfers between devices with their start and end apart: 17, of which 14 were waited for; matrix products, arithmetic and copies ran while one was open for 4% of the time, Pallas kernels for 19%

profile of v2, /device:TPU:1, one launch (start us, length us, event | category | flops | bytes accessed | tf_op | source)
XLA Modules:
  0.0 113.1 jit_solution(14592583548645534952)
XLA Ops:
  0.7 1.0 multiply_convert_fusion
  1.8 5.0 %collective-permute-start.1 = (bf16[256,256]{1,0:T(8,128)(2,1)S(1)}, bf16[256,256]{1,0:T(8,128)(2,1)S(1)}, u32[]{:S(2)}, u32[]{:S(2)}) collective-permute-start(bf16[256,256]{1,0:T(8,128)(2,1)S(1)} %multiply_convert_fusion), channel_id=1, source_target_pairs={{128,0},{157,1},{154,2},{135,3},{132,4},{129,5},{158,6},{139,7},{1... | collective-permute-start | bytes 393224 | tf_op jit(solution)/shard_map/ppermute | solution.py:56
  6.8 3.5 %collective-permute-start = (bf16[256,256]{1,0:T(8,128)(2,1)S(1)}, bf16[256,256]{1,0:T(8,128)(2,1)S(1)}, u32[]{:S(2)}, u32[]{:S(2)}) collective-permute-start(bf16[256,256]{1,0:T(8,128)(2,1)S(1)} %multiply_convert_fusion), channel_id=1, source_target_pairs={{0,0},{29,1},{26,2},{7,3},{4,4},{1,5},{30,6},{11,7},{8,8},{5,9},{2... | collective-permute-start | bytes 393224 | tf_op jit(solution)/shard_map/ppermute | solution.py:56
  11.2 1.2 %select_reduce_fusion = s32[16,22]{0,1:T(8,128)S(1)} fusion(s32[128]{0:T(128)} %constant.12.clone, s32[16,22]{0,1:T(8,128)S(1)} %copy.9), kind=kLoop, calls=%fused_computation.29 | loop fusion | flops 134816 | bytes 3328 | tf_op jit(solution)/shard_map/reduce_sum | solution.py:203
  13.7 2.8 %collective-permute-start.4 = (bf16[512,256]{1,0:T(8,128)(2,1)S(1)}, bf16[512,256]{1,0:T(8,128)(2,1)S(1)}, u32[]{:S(2)}, u32[]{:S(2)}) collective-permute-start(bf16[512,256]{1,0:T(8,128)(2,1)S(1)} %pad_maximum_fusion.11), channel_id=1, source_target_pairs={{32,0},{97,1},{34,2},{99,3},{36,4},{101,5},{38,6},{103,7},{40,8},{... | collective-permute-start | bytes 786440 | tf_op jit(solution)/shard_map/ppermute | solution.py:56
  16.5 1.6 %collective-permute-start.2 = (bf16[512,256]{1,0:T(8,128)(2,1)S(1)}, bf16[512,256]{1,0:T(8,128)(2,1)S(1)}, u32[]{:S(2)}, u32[]{:S(2)}) collective-permute-start(bf16[512,256]{1,0:T(8,128)(2,1)S(1)} %pad_maximum_fusion.11), channel_id=1, source_target_pairs={{5,0},{28,1},{7,2},{30,3},{9,4},{0,5},{11,6},{2,7},{13,8},{4,9},{1... | collective-permute-start | bytes 786440 | tf_op jit(solution)/shard_map/ppermute | solution.py:56
  18.2 2.1 %collective-permute-done.4 = bf16[512,256]{1,0:T(8,128)(2,1)S(1)} collective-permute-done((bf16[512,256]{1,0:T(8,128)(2,1)S(1)}, bf16[512,256]{1,0:T(8,128)(2,1)S(1)}, u32[]{:S(2)}, u32[]{:S(2)}) %collective-permute-start.4) | collective-permute-done | bytes 262176 | tf_op jit(solution)/shard_map/ppermute | solution.py:56
  20.3 3.2 %collective-permute-done.2 = bf16[512,256]{1,0:T(8,128)(2,1)S(1)} collective-permute-done((bf16[512,256]{1,0:T(8,128)(2,1)S(1)}, bf16[512,256]{1,0:T(8,128)(2,1)S(1)}, u32[]{:S(2)}, u32[]{:S(2)}) %collective-permute-start.2) | collective-permute-done | bytes 262176 | tf_op jit(solution)/shard_map/ppermute | solution.py:56
  23.6 4.3 %collective-permute-start.3 = (bf16[1024,256]{1,0:T(8,128)(2,1)S(1)}, bf16[1024,256]{1,0:T(8,128)(2,1)S(1)}, u32[]{:S(2)}, u32[]{:S(2)}) collective-permute-start(bf16[1024,256]{1,0:T(8,128)(2,1)S(1)} %get-tuple-element.41), channel_id=1, source_target_pairs={{159,0},{6,1},{29,2},{132,3},{131,4},{10,5},{1,6},{136,7},{135,8},... | collective-permute-start | bytes 1572872 | tf_op jit(solution)/shard_map/ppermute | solution.py:56
  28.2 5.9 %shard_map.82 = (s32[40,128]{1,0:T(8,128)S(1)}, s32[40]{0:T(128)S(1)}, bf16[352,128,128]{2,1,0:T(8,128)(2,1)S(1)}) custom-call(s32[16]{0:T(128)S(1)} %bitcast.67, s32[16,22]{1,0:T(8,128)S(1)} %fusion.16.coded, bf16[352,128,128]{2,1,0:T(8,128)(2,1)} %bitcast.68), custom_call_target="tpu_custom_call" | custom-call | bytes 23000000 | tf_op jit(solution)/shard_map/pallas_call | solution.py:136
  34.1 0.9 collective-permute-done.3
  35.1 1.1 collective-permute-done.5
  36.3 4.9 %collective-permute-start.6 = (bf16[1792,256]{1,0:T(8,128)(2,1)S(1)}, bf16[1792,256]{1,0:T(8,128)(2,1)S(1)}, u32[]{:S(2)}, u32[]{:S(2)}) collective-permute-start(bf16[1792,256]{1,0:T(8,128)(2,1)S(1)} %pad_maximum_fusion.5), channel_id=1, source_target_pairs={{5,0},{28,1},{7,2},{30,3},{9,4},{0,5},{11,6},{2,7},{13,8},{4,9},{1... | collective-permute-start | bytes 2752520 | tf_op jit(solution)/shard_map/ppermute | solution.py:56
  41.2 2.0 %collective-permute-start.7 = (bf16[768,256]{1,0:T(8,128)(2,1)S(1)}, bf16[768,256]{1,0:T(8,128)(2,1)S(1)}, u32[]{:S(2)}, u32[]{:S(2)}) collective-permute-start(bf16[768,256]{1,0:T(8,128)(2,1)S(1)} %pad_maximum_fusion.10), channel_id=1, source_target_pairs={{32,0},{97,1},{34,2},{99,3},{36,4},{101,5},{38,6},{103,7},{40,8},{... | collective-permute-start | bytes 1179656 | tf_op jit(solution)/shard_map/ppermute | solution.py:56
  43.3 3.2 %shard_map.83.refs_0_ = f32[4,256,256]{2,1,0:T(8,128)S(1)} custom-call(s32[40,128]{1,0:T(8,128)S(1)} %get-tuple-element.19.lists, s32[40]{0:T(128)S(1)} %get-tuple-element.20.counts, bf16[352,128,128]{2,1,0:T(8,128)(2,1)S(1)} %get-tuple-element.21.tiles, bf16[29,128,256]{2,1,0:T(8,128)(2,1)S(1)} %bitcast.66), custom_call_target="tpu_custom_call" | custom-call | flops 730800000 | bytes 13050000 | tf_op jit(solution)/shard_map/pallas_call | solution.py:171
  46.5 2.6 %collective-permute-done.7 = bf16[768,256]{1,0:T(8,128)(2,1)S(1)} collective-permute-done((bf16[768,256]{1,0:T(8,128)(2,1)S(1)}, bf16[768,256]{1,0:T(8,128)(2,1)S(1)}, u32[]{:S(2)}, u32[]{:S(2)}) %collective-permute-start.7) | collective-permute-done | bytes 393248 | tf_op jit(solution)/shard_map/ppermute | solution.py:56
  49.2 3.0 %collective-permute-done.6 = bf16[1792,256]{1,0:T(8,128)(2,1)S(1)} collective-permute-done((bf16[1792,256]{1,0:T(8,128)(2,1)S(1)}, bf16[1792,256]{1,0:T(8,128)(2,1)S(1)}, u32[]{:S(2)}, u32[]{:S(2)}) %collective-permute-start.6) | collective-permute-done | bytes 917536 | tf_op jit(solution)/shard_map/ppermute | solution.py:56
  52.7 2.8 %shard_map.84.refs_0_ = f32[4,256,256]{2,1,0:T(8,128)S(1)} custom-call(s32[40,128]{1,0:T(8,128)S(1)} %get-tuple-element.19.lists, s32[40]{0:T(128)S(1)} %get-tuple-element.20.counts, bf16[352,128,128]{2,1,0:T(8,128)(2,1)S(1)} %get-tuple-element.21.tiles, bf16[21,128,256]{2,1,0:T(8,128)(2,1)S(1)} %bitcast.64, f32[4,256,256]{2,1,0:T(8,128)S(1)} %shard_map.83.refs_0_), custom_call_target="tpu_custom_call" | custom-call | flops 529200000 | bytes 9450000 | tf_op jit(solution)/shard_map/pallas_call | solution.py:171
  55.5 15.2 %collective-permute-done.8 = bf16[2560,256]{1,0:T(8,128)(2,1)S(1)} collective-permute-done((bf16[2560,256]{1,0:T(8,128)(2,1)S(1)}, bf16[2560,256]{1,0:T(8,128)(2,1)S(1)}, u32[]{:S(2)}, u32[]{:S(2)}) %collective-permute-start.8) | collective-permute-done | bytes 1310752 | tf_op jit(solution)/shard_map/ppermute | solution.py:56
  70.8 2.0 %collective-permute-start.10 = (bf16[1024,256]{1,0:T(8,128)(2,1)S(1)}, bf16[1024,256]{1,0:T(8,128)(2,1)S(1)}, u32[]{:S(2)}, u32[]{:S(2)}) collective-permute-start(bf16[1024,256]{1,0:T(8,128)(2,1)S(1)} %pad_maximum_fusion.9), channel_id=1, source_target_pairs={{32,0},{97,1},{34,2},{99,3},{36,4},{101,5},{38,6},{103,7},{40,8},{... | collective-permute-start | bytes 1572872 | tf_op jit(solution)/shard_map/ppermute | solution.py:56
  72.8 2.1 %collective-permute-start.9 = (bf16[1536,256]{1,0:T(8,128)(2,1)S(1)}, bf16[1536,256]{1,0:T(8,128)(2,1)S(1)}, u32[]{:S(2)}, u32[]{:S(2)}) collective-permute-start(bf16[1536,256]{1,0:T(8,128)(2,1)S(1)} %slice.110), channel_id=1, source_target_pairs={{5,0},{28,1},{7,2},{30,3},{9,4},{0,5},{11,6},{2,7},{13,8},{4,9},{1... | collective-permute-start | bytes 2359304 | tf_op jit(solution)/shard_map/ppermute | solution.py:56
  75.0 3.9 %shard_map.85.refs_0_ = f32[4,256,256]{2,1,0:T(8,128)S(1)} custom-call(s32[40,128]{1,0:T(8,128)S(1)} %get-tuple-element.19.lists, s32[40]{0:T(128)S(1)} %get-tuple-element.20.counts, bf16[352,128,128]{2,1,0:T(8,128)(2,1)S(1)} %get-tuple-element.21.tiles, bf16[33,128,256]{2,1,0:T(8,128)(2,1)S(1)} %bitcast.63, f32[4,256,256]{2,1,0:T(8,128)S(1)} %shard_map.84.refs_0_), custom_call_target="tpu_custom_call" | custom-call | flops 831600000 | bytes 14850000 | tf_op jit(solution)/shard_map/pallas_call | solution.py:171
  79.0 1.2 %collective-permute-done.10 = bf16[1024,256]{1,0:T(8,128)(2,1)S(1)} collective-permute-done((bf16[1024,256]{1,0:T(8,128)(2,1)S(1)}, bf16[1024,256]{1,0:T(8,128)(2,1)S(1)}, u32[]{:S(2)}, u32[]{:S(2)}) %collective-permute-start.10) | collective-permute-done | bytes 524320 | tf_op jit(solution)/shard_map/ppermute | solution.py:56
  80.2 5.2 %collective-permute-done.9 = bf16[1536,256]{1,0:T(8,128)(2,1)S(1)} collective-permute-done((bf16[1536,256]{1,0:T(8,128)(2,1)S(1)}, bf16[1536,256]{1,0:T(8,128)(2,1)S(1)}, u32[]{:S(2)}, u32[]{:S(2)}) %collective-permute-start.9) | collective-permute-done | bytes 786464 | tf_op jit(solution)/shard_map/ppermute | solution.py:56
  86.3 3.2 %shard_map.86 = f32[4,256,256]{2,1,0:T(8,128)S(1)} custom-call(s32[40,128]{1,0:T(8,128)S(1)} %get-tuple-element.19.lists, s32[40]{0:T(128)S(1)} %get-tuple-element.20.counts, bf16[352,128,128]{2,1,0:T(8,128)(2,1)S(1)} %get-tuple-element.21.tiles, bf16[21,128,256]{2,1,0:T(8,128)(2,1)S(1)} %bitcast.65, f32[4,256,256]{2,1,0:T(8,128)S(1)} %shard_map.85.refs_0_), custom_call_target="tpu_custom_call" | custom-call | flops 529200000 | bytes 9450000 | tf_op jit(solution)/shard_map/pallas_call | solution.py:171
  89.5 9.3 %collective-permute-done.12 = bf16[1536,256]{1,0:T(8,128)(2,1)S(1)} collective-permute-done((bf16[1536,256]{1,0:T(8,128)(2,1)S(1)}, bf16[1536,256]{1,0:T(8,128)(2,1)S(1)}, u32[]{:S(2)}, u32[]{:S(2)}) %collective-permute-start.12) | collective-permute-done | bytes 786464 | tf_op jit(solution)/shard_map/ppermute | solution.py:56
  99.5 2.5 %shard_map.87 = f32[2,256,256]{2,1,0:T(8,128)S(1)} custom-call(s32[40,128]{1,0:T(8,128)S(1)} %get-tuple-element.19.lists, s32[40]{0:T(128)S(1)} %get-tuple-element.20.counts, bf16[352,128,128]{2,1,0:T(8,128)(2,1)S(1)} %get-tuple-element.21.tiles, bf16[29,128,256]{2,1,0:T(8,128)(2,1)S(1)} %bitcast.61, f32[2,256,256]{2,1,0:T(8,128)S(1)} %slice.115.refs_0_), custom_call_target="tpu_custom_call" | custom-call | flops 361200000 | bytes 6450000 | tf_op jit(solution)/shard_map/pallas_call | solution.py:171
  102.0 0.9 collective-permute-start.14
  102.9 1.2 %collective-permute-done.14 = f32[256,256]{1,0:T(8,128)S(1)} collective-permute-done((f32[256,256]{1,0:T(8,128)S(1)}, f32[256,256]{1,0:T(8,128)S(1)}, u32[]{:S(2)}, u32[]{:S(2)}) %collective-permute-start.14) | collective-permute-done | bytes 262176 | tf_op jit(solution)/shard_map/ppermute | solution.py:222
  104.3 2.5 %shard_map.88 = f32[2,256,256]{2,1,0:T(8,128)S(1)} custom-call(s32[40,128]{1,0:T(8,128)S(1)} %get-tuple-element.19.lists, s32[40]{0:T(128)S(1)} %get-tuple-element.20.counts, bf16[352,128,128]{2,1,0:T(8,128)(2,1)S(1)} %get-tuple-element.21.tiles, bf16[29,128,256]{2,1,0:T(8,128)(2,1)S(1)} %bitcast.62, f32[2,256,256]{2,1,0:T(8,128)S(1)} %slice.95.refs_0_), custom_call_target="tpu_custom_call" | custom-call | flops 361200000 | bytes 6450000 | tf_op jit(solution)/shard_map/pallas_call | solution.py:171
  107.3 4.5 %collective-permute-done.16 = f32[256,256]{1,0:T(8,128)S(1)} collective-permute-done((f32[256,256]{1,0:T(8,128)S(1)}, f32[256,256]{1,0:T(8,128)S(1)}, u32[]{:S(2)}, u32[]{:S(2)}) %collective-permute-start.16) | collective-permute-done | bytes 262176 | tf_op jit(solution)/shard_map/ppermute | solution.py:218
  112.1 1.0 fusion.3
  (68 shorter events, 6.9 us)
Async XLA Ops:
  0.0 111.8 %copy-start = (bf16[256,256]{1,0:T(8,128)(2,1)S(1)}, bf16[256,256]{1,0:T(8,128)(2,1)}, u32[]{:S(2)}) copy-start(bf16[256,256]{1,0:T(8,128)(2,1)} %param.14) | copy-start | bytes 393220
  0.0 28.2 %copy-start.1 = (s32[1,1,16]{2,1,0:T(1,128)S(1)}, s32[1,1,16]{2,1,0:T(1,128)}, u32[]{:S(2)}) copy-start(s32[1,1,16]{2,1,0:T(1,128)} %param.13) | copy-start | bytes 196
  1.8 11.5 %collective-permute-start.1 = (bf16[256,256]{1,0:T(8,128)(2,1)S(1)}, bf16[256,256]{1,0:T(8,128)(2,1)S(1)}, u32[]{:S(2)}, u32[]{:S(2)}) collective-permute-start(bf16[256,256]{1,0:T(8,128)(2,1)S(1)} %multiply_convert_fusion), channel_id=1, source_target_pairs={{128,0},{157,1},{154,2},{135,3},{132,4},{129,5},{158,6},{139,7},{1... | collective-permute-start | bytes 393224 | tf_op jit(solution)/shard_map/ppermute | solution.py:56
  6.8 6.9 %collective-permute-start = (bf16[256,256]{1,0:T(8,128)(2,1)S(1)}, bf16[256,256]{1,0:T(8,128)(2,1)S(1)}, u32[]{:S(2)}, u32[]{:S(2)}) collective-permute-start(bf16[256,256]{1,0:T(8,128)(2,1)S(1)} %multiply_convert_fusion), channel_id=1, source_target_pairs={{0,0},{29,1},{26,2},{7,3},{4,4},{1,5},{30,6},{11,7},{8,8},{5,9},{2... | collective-permute-start | bytes 393224 | tf_op jit(solution)/shard_map/ppermute | solution.py:56
  13.7 6.6 %collective-permute-start.4 = (bf16[512,256]{1,0:T(8,128)(2,1)S(1)}, bf16[512,256]{1,0:T(8,128)(2,1)S(1)}, u32[]{:S(2)}, u32[]{:S(2)}) collective-permute-start(bf16[512,256]{1,0:T(8,128)(2,1)S(1)} %pad_maximum_fusion.11), channel_id=1, source_target_pairs={{32,0},{97,1},{34,2},{99,3},{36,4},{101,5},{38,6},{103,7},{40,8},{... | collective-permute-start | bytes 786440 | tf_op jit(solution)/shard_map/ppermute | solution.py:56
  16.5 7.0 %collective-permute-start.2 = (bf16[512,256]{1,0:T(8,128)(2,1)S(1)}, bf16[512,256]{1,0:T(8,128)(2,1)S(1)}, u32[]{:S(2)}, u32[]{:S(2)}) collective-permute-start(bf16[512,256]{1,0:T(8,128)(2,1)S(1)} %pad_maximum_fusion.11), channel_id=1, source_target_pairs={{5,0},{28,1},{7,2},{30,3},{9,4},{0,5},{11,6},{2,7},{13,8},{4,9},{1... | collective-permute-start | bytes 786440 | tf_op jit(solution)/shard_map/ppermute | solution.py:56
  20.3 13.8 %copy-start.2 = (bf16[512,256]{1,0:T(8,128)(2,1)}, bf16[512,256]{1,0:T(8,128)(2,1)S(1)}, u32[]{:S(2)}) copy-start(bf16[512,256]{1,0:T(8,128)(2,1)S(1)} %collective-permute-done.4) | copy-start | bytes 786436
  23.6 11.4 %collective-permute-start.3 = (bf16[1024,256]{1,0:T(8,128)(2,1)S(1)}, bf16[1024,256]{1,0:T(8,128)(2,1)S(1)}, u32[]{:S(2)}, u32[]{:S(2)}) collective-permute-start(bf16[1024,256]{1,0:T(8,128)(2,1)S(1)} %get-tuple-element.41), channel_id=1, source_target_pairs={{159,0},{6,1},{29,2},{132,3},{131,4},{10,5},{1,6},{136,7},{135,8},... | collective-permute-start | bytes 1572872 | tf_op jit(solution)/shard_map/ppermute | solution.py:56
  27.9 8.3 %collective-permute-start.5 = (bf16[1024,256]{1,0:T(8,128)(2,1)S(1)}, bf16[1024,256]{1,0:T(8,128)(2,1)S(1)}, u32[]{:S(2)}, u32[]{:S(2)}) collective-permute-start(bf16[1024,256]{1,0:T(8,128)(2,1)S(1)} %get-tuple-element.42), channel_id=1, source_target_pairs={{96,0},{33,1},{98,2},{35,3},{100,4},{37,5},{102,6},{39,7},{104,8},... | collective-permute-start | bytes 1572872 | tf_op jit(solution)/shard_map/ppermute | solution.py:56
  34.1 2.1 %slice-start = ((bf16[512,256]{1,0:T(8,128)(2,1)}), bf16[256,256]{1,0:T(8,128)(2,1)S(1)}, s32[]{:S(2)}) async-start(bf16[512,256]{1,0:T(8,128)(2,1)} %copy-done.2), calls=%async_computation | async-start | bytes 262144 | tf_op jit(solution)/shard_map/slice | solution.py:51
  35.1 8.1 %copy-start.3 = (bf16[512,256]{1,0:T(8,128)(2,1)S(1)}, bf16[512,256]{1,0:T(8,128)(2,1)}, u32[]{:S(2)}) copy-start(bf16[512,256]{1,0:T(8,128)(2,1)} %copy-done.2) | copy-start | bytes 786436
  36.3 15.9 %collective-permute-start.6 = (bf16[1792,256]{1,0:T(8,128)(2,1)S(1)}, bf16[1792,256]{1,0:T(8,128)(2,1)S(1)}, u32[]{:S(2)}, u32[]{:S(2)}) collective-permute-start(bf16[1792,256]{1,0:T(8,128)(2,1)S(1)} %pad_maximum_fusion.5), channel_id=1, source_target_pairs={{5,0},{28,1},{7,2},{30,3},{9,4},{0,5},{11,6},{2,7},{13,8},{4,9},{1... | collective-permute-start | bytes 2752520 | tf_op jit(solution)/shard_map/ppermute | solution.py:56
  41.2 7.9 %collective-permute-start.7 = (bf16[768,256]{1,0:T(8,128)(2,1)S(1)}, bf16[768,256]{1,0:T(8,128)(2,1)S(1)}, u32[]{:S(2)}, u32[]{:S(2)}) collective-permute-start(bf16[768,256]{1,0:T(8,128)(2,1)S(1)} %pad_maximum_fusion.10), channel_id=1, source_target_pairs={{32,0},{97,1},{34,2},{99,3},{36,4},{101,5},{38,6},{103,7},{40,8},{... | collective-permute-start | bytes 1179656 | tf_op jit(solution)/shard_map/ppermute | solution.py:56
  52.4 18.3 %collective-permute-start.8 = (bf16[2560,256]{1,0:T(8,128)(2,1)S(1)}, bf16[2560,256]{1,0:T(8,128)(2,1)S(1)}, u32[]{:S(2)}, u32[]{:S(2)}) collective-permute-start(bf16[2560,256]{1,0:T(8,128)(2,1)S(1)} %slice_dynamic-update-slice_fusion.1), channel_id=1, source_target_pairs={{159,0},{6,1},{29,2},{132,3},{131,4},{10,5},{1,6},{136,7},{135,8},... | collective-permute-start | bytes 3932168 | tf_op jit(solution)/shard_map/ppermute | solution.py:56
  52.5 22.4 %collective-permute-start.11 = (bf16[1536,256]{1,0:T(8,128)(2,1)S(1)}, bf16[1536,256]{1,0:T(8,128)(2,1)S(1)}, u32[]{:S(2)}, u32[]{:S(2)}) collective-permute-start(bf16[1536,256]{1,0:T(8,128)(2,1)S(1)} %pad_maximum_fusion.6), channel_id=1, source_target_pairs={{96,0},{33,1},{98,2},{35,3},{100,4},{37,5},{102,6},{39,7},{104,8},... | collective-permute-start | bytes 2359304 | tf_op jit(solution)/shard_map/ppermute | solution.py:56
  70.8 9.3 %collective-permute-start.10 = (bf16[1024,256]{1,0:T(8,128)(2,1)S(1)}, bf16[1024,256]{1,0:T(8,128)(2,1)S(1)}, u32[]{:S(2)}, u32[]{:S(2)}) collective-permute-start(bf16[1024,256]{1,0:T(8,128)(2,1)S(1)} %pad_maximum_fusion.9), channel_id=1, source_target_pairs={{32,0},{97,1},{34,2},{99,3},{36,4},{101,5},{38,6},{103,7},{40,8},{... | collective-permute-start | bytes 1572872 | tf_op jit(solution)/shard_map/ppermute | solution.py:56
  72.8 12.6 %collective-permute-start.9 = (bf16[1536,256]{1,0:T(8,128)(2,1)S(1)}, bf16[1536,256]{1,0:T(8,128)(2,1)S(1)}, u32[]{:S(2)}, u32[]{:S(2)}) collective-permute-start(bf16[1536,256]{1,0:T(8,128)(2,1)S(1)} %slice.110), channel_id=1, source_target_pairs={{5,0},{28,1},{7,2},{30,3},{9,4},{0,5},{11,6},{2,7},{13,8},{4,9},{1... | collective-permute-start | bytes 2359304 | tf_op jit(solution)/shard_map/ppermute | solution.py:56
  85.4 13.9 %collective-permute-start.13 = (bf16[2048,256]{1,0:T(8,128)(2,1)S(1)}, bf16[2048,256]{1,0:T(8,128)(2,1)S(1)}, u32[]{:S(2)}, u32[]{:S(2)}) collective-permute-start(bf16[2048,256]{1,0:T(8,128)(2,1)S(1)} %pad_maximum_fusion.4), channel_id=1, source_target_pairs={{96,0},{33,1},{98,2},{35,3},{100,4},{37,5},{102,6},{39,7},{104,8},... | collective-permute-start | bytes 3145736 | tf_op jit(solution)/shard_map/ppermute | solution.py:56
  86.2 12.6 %collective-permute-start.12 = (bf16[1536,256]{1,0:T(8,128)(2,1)S(1)}, bf16[1536,256]{1,0:T(8,128)(2,1)S(1)}, u32[]{:S(2)}, u32[]{:S(2)}) collective-permute-start(bf16[1536,256]{1,0:T(8,128)(2,1)S(1)} %collective-permute-done.9), channel_id=1, source_target_pairs={{159,0},{6,1},{29,2},{132,3},{131,4},{10,5},{1,6},{136,7},{135,8},... | collective-permute-start | bytes 2359304 | tf_op jit(solution)/shard_map/ppermute | solution.py:56
  102.0 2.0 %collective-permute-start.14 = (f32[256,256]{1,0:T(8,128)S(1)}, f32[256,256]{1,0:T(8,128)S(1)}, u32[]{:S(2)}, u32[]{:S(2)}) collective-permute-start(f32[256,256]{1,0:T(8,128)S(1)} %slice_bitcast_fusion.2), channel_id=1, source_target_pairs={{0,1},{1,0},{2,3},{3,2},{4,5},{5,4},{6,7},{7,6},{8,9},{9,8},{10,11... | collective-permute-start | bytes 786440 | tf_op jit(solution)/shard_map/ppermute | solution.py:222
  104.2 7.6 %collective-permute-start.16 = (f32[256,256]{1,0:T(8,128)S(1)}, f32[256,256]{1,0:T(8,128)S(1)}, u32[]{:S(2)}, u32[]{:S(2)}) collective-permute-start(f32[256,256]{1,0:T(8,128)S(1)} %fusion.7), channel_id=1, source_target_pairs={{0,2},{1,3},{2,0},{3,1},{4,6},{5,7},{6,4},{7,5},{8,10},{9,11},{10,... | collective-permute-start | bytes 786440 | tf_op jit(solution)/shard_map/ppermute | solution.py:218
  106.8 5.3 %collective-permute-start.15 = (f32[256,256]{1,0:T(8,128)S(1)}, f32[256,256]{1,0:T(8,128)S(1)}, u32[]{:S(2)}, u32[]{:S(2)}) collective-permute-start(f32[256,256]{1,0:T(8,128)S(1)} %slice_bitcast_fusion), channel_id=1, source_target_pairs={{0,1},{1,0},{2,3},{3,2},{4,5},{5,4},{6,7},{7,6},{8,9},{9,8},{10,11... | collective-permute-start | bytes 786440 | tf_op jit(solution)/shard_map/ppermute | solution.py:222

commit v3 on v2

--- a/solution.py
+++ b/solution.py
@@ -15,6 +15,7 @@
 N_TILES = STEPS * SLOTS
 LIST = 128
 BATCH = 4
+AT_ONCE = 3
 PHASES = 5
 
 HOME = (0, 1, 2, -1)
@@ -75,33 +76,36 @@
     return [Blocks(r, p.labels) for r, p in zip(rows, parts)]
 
 
-def gather(scaled, first_ready, ready, add):
+def gather(scaled, first_ready, prepare, add):
     own = Blocks(scaled, [(0, 0, 0, 0), (1, 0, 0, 0)])
     near, far = own.moved("home"), own.moved("far")
     (s0,) = in_order([joined(near[0:1], far[0:1], near[1:2], far[1:2])], first_ready)
-    s1, e1 = s0.moved("z1"), s0.moved("y1")
-    s2, e2 = joined(s0, s1).moved("z2"), joined(s0, e1).moved("y2")
+    s1, e1 = in_order([s0.moved("z1"), s0.moved("y1")])
+    ready = prepare(s1.rows)
+    s2, e2 = in_order([joined(s0, s1).moved("z2"), joined(s0, e1).moved("y2")], ready)
     b0 = joined(e1.half(1), e2.half(1))
-    z, y1 = in_order([joined(s2, b0), joined(s1.half(0), s2.half(0))], ready)
-    z3, y1a = z.moved("z1"), y1.moved("y1")
+    y12 = joined(s1.half(0), s2.half(0))
+    z3, y3 = joined(s2, b0).moved("z1"), y12.moved("y1")
     total = add(None, [s0, s1, e1, s2, e2])
-    z, y = in_order([joined(z3[0:8], b0, z3[8:14]), joined(y1, y1a)], total)
-    z4, y1b = z.moved("z2"), y.moved("y2")
-    total = add(total, [z3, y1a])
-    b, y2 = in_order([z4[8:20], joined(z3[0:8].half(0), z4[0:8].half(0))], total)
-    b3, y2a = b.moved("z1"), y2.moved("y1")
-    total = add(total, [z4, y1b])
-    b, y = in_order([b3, joined(y2, y2a)], total)
-    b4, y2b = b.moved("z2"), y.moved("y2")
-    total = add(total, [b3, y2a])
-    return add(total, [b4, y2b])
+    s3 = z3[0:8].half(0)
+    z, y = in_order([joined(z3[0:8], b0, z3[8:14]), joined(y12, y3, s3)], total)
+    z4, y4 = z.moved("z2"), y.moved("y2")
+    total = add(total, [z3, y3])
+    s4 = z4[0:8].half(0)
+    z, y = in_order([z4[8:20], joined(s3, y4[12:16], s4)], total)
+    z5, y5 = z.moved("z1"), y.moved("y1")
+    total = add(total, [z4])
+    z, y = in_order([z5, joined(s4, y5[8:12])], total)
+    z6, y6 = z.moved("z2"), y.moved("y2")
+    total = add(total, [y4, z5, y5])
+    return add(total, [z6, y6])
 
 
 def phase_labels():
     found = []
 
     def traced(rows):
-        return gather(rows, rows, rows, lambda _, parts: found.append([label for p in parts for label in p.labels]) or rows)
+        return gather(rows, rows, lambda _: rows, lambda _, parts: found.append([label for p in parts for label in p.labels]) or rows)
 
     jax.eval_shape(traced, jax.ShapeDtypeStruct((2 * TILE, 256), jnp.bfloat16))
     return found
@@ -114,20 +118,25 @@
         counts[b] = 0
 
     def one_source(k, _):
-        def one_slot(s, _):
-            v = coded[k, s]
-            b = v >> 17
-            n = counts[b]
-            lists[b, n] = v & 0x1FFFF
-            counts[b] = n + 1
-            return 0
-
-        return lax.fori_loop(0, live[k], one_slot, 0)
+        used = live[k]
+        for s in range(SLOTS):
+
+            @pl.when(s < used)
+            def _(s=s):
+                v = coded[k, s]
+                b = v >> 17
+                n = counts[b]
+                lists[b, n] = v & 0x1FFFF
+                counts[b] = n + 1
+
+        return 0
 
     lax.fori_loop(0, STEPS, one_source, 0)
     for b in range(8 * PHASES):
         for i in range(BATCH - 1):
             lists[b, counts[b] + i] = 0
+    for i in range(BATCH):
+        lists[8 * PHASES, i] = 0
     load.wait()
 
 
@@ -136,7 +145,7 @@
     return pl.pallas_call(
         list_kernel,
         out_shape=(
-            jax.ShapeDtypeStruct((8 * PHASES, LIST), jnp.int32),
+            jax.ShapeDtypeStruct((8 * PHASES + 1, LIST), jnp.int32),
             jax.ShapeDtypeStruct((8 * PHASES,), jnp.int32),
             jax.ShapeDtypeStruct(tiles.shape, tiles.dtype),
         ),
@@ -149,30 +158,44 @@
 
 
 def product_kernel(buckets, first_bucket, more, lists, counts, tiles, blocks, *refs):
-    before, total = refs if more else (None, refs[0])
+    before, total, order = refs if more else (None, *refs)
+    total[...] = before[...] if more else jnp.zeros_like(total)
+    end = 0
     for b in range(buckets):
 
-        def batch(i, total, b=b):
-            at = [lists[first_bucket + b, i * BATCH + j] for j in range(BATCH)]
+        def note(i, end, b=b):
+            order[end] = (b << 16) + ((first_bucket + b) << 8) + i
+            return end + 1
+
+        end = lax.fori_loop(0, (counts[first_bucket + b] + (BATCH - 1)) // BATCH, note, end)
+    for i in range(AT_ONCE - 1):
+        order[end + i] = (8 * PHASES) << 8
+
+    def batches(g, _):
+        found = []
+        for i in range(AT_ONCE):
+            v = order[g * AT_ONCE + i]
+            at = [lists[(v >> 8) & 255, (v & 255) * BATCH + j] for j in range(BATCH)]
             left = jnp.concatenate([tiles[a & 1023] for a in at], axis=1)
             right = jnp.concatenate([blocks[a >> 10] for a in at], axis=0)
-            return total + jnp.dot(left, right, preferred_element_type=jnp.float32)
-
-        rows = pl.ds((b % 2) * TILE, TILE)
-        start = before[b // 2, rows, :] if more else jnp.zeros((TILE, 256), jnp.float32)
-        n = (counts[first_bucket + b] + (BATCH - 1)) // BATCH
-        total[b // 2, rows, :] = lax.fori_loop(0, n, batch, start)
+            found.append((v >> 16, jnp.dot(left, right, preferred_element_type=jnp.float32)))
+        for b, product in found:
+            total[b >> 1, pl.ds((b & 1) * TILE, TILE), :] += product
+        return 0
+
+    lax.fori_loop(0, (end + (AT_ONCE - 1)) // AT_ONCE, batches, 0)
 
 
 def products(lists, counts, first_bucket, buckets, tiles, blocks, before=None):
     smem, vmem = pl.BlockSpec(memory_space=pltpu.SMEM), pl.BlockSpec(memory_space=pltpu.VMEM)
     more = before is not None
-    slots = blocks.shape[0] * 3 * buckets // 8
+    slots = blocks.shape[0] * 3 * buckets // (8 if buckets < 8 else 32)
     return pl.pallas_call(
         functools.partial(product_kernel, buckets, first_bucket, more),
         out_shape=jax.ShapeDtypeStruct((buckets // 2, 256, 256), jnp.float32),
         in_specs=[smem] * 2 + [vmem] * (2 + more),
         out_specs=vmem,
+        scratch_shapes=[pltpu.SMEM((N_TILES // BATCH + 8 + AT_ONCE,), jnp.int32)],
         compiler_params=pltpu.CompilerParams(vmem_limit_bytes=2 << 20),
         cost_estimate=pl.CostEstimate(flops=slots * 8_400_000, bytes_accessed=slots * 150_000, transcendentals=0),
     )(lists, counts, tiles, blocks, *([before] if more else []))
@@ -180,8 +203,9 @@
 
 def local(features, degree, tiles, tile_rows, tile_cols, live, weight):
     row, mine = lax.axis_index("row"), lax.axis_index("rep")
-    scale = lax.rsqrt(degree.astype(jnp.float32))
-    scaled = (features.astype(jnp.float32) * scale[:, None]).astype(jnp.bfloat16)
+    scale = lax.rsqrt(lax.optimization_barrier(degree).astype(jnp.float32))
+    first_scale = lax.rsqrt(degree.astype(jnp.float32))
+    scaled = (features.astype(jnp.float32) * first_scale[:, None]).astype(jnp.bfloat16)
 
     cols, steps = tile_cols[0, 0], jnp.arange(STEPS, dtype=jnp.int32)[:, None]
     source = (row - mine - 4 * steps) & 63
@@ -202,10 +226,16 @@
             places[((t * 2 + h) * 8 + p) * 4 + e] = ((8 * n) << 17) + ((i + 1) << 10)
     place = jnp.sum(jnp.where(label == jnp.arange(128, dtype=jnp.int32), jnp.asarray(places), 0), axis=-1)
     coded = place + (bucket << 17) + steps * SLOTS + jnp.arange(SLOTS, dtype=jnp.int32)
-    lists, counts, held = slot_lists(live[0, 0], coded, tiles.reshape(N_TILES, TILE, TILE))
+    lists, counts, held = None, None, None
     devices = range(256)
     nothing = jnp.zeros((TILE, 256), jnp.bfloat16)
     n = 0
+
+    def prepare(earlier):
+        nonlocal lists, counts, held
+        now, _ = lax.optimization_barrier((coded, earlier))
+        lists, counts, held = slot_lists(live[0, 0], now, tiles.reshape(N_TILES, TILE, TILE))
+        return counts
 
     def add(total, found):
         nonlocal n
@@ -216,15 +246,18 @@
         theirs = to_owner_core(products(lists, counts, first, 4, held, blocks, total[0:2]))
         theirs, total = lax.optimization_barrier((theirs, total))
         theirs = lax.ppermute(theirs, AXES, [(i, i ^ 2) for i in devices])
-        return to_owner_core(products(lists, counts, first + 4, 4, held, blocks, total[2:4])), theirs
-
-    def to_owner_core(part):
-        return part[0] + lax.ppermute(part[1], AXES, [(i, i ^ 1) for i in devices])
+        return to_owner_core(products(lists, counts, first + 4, 4, held, blocks, total[2:4]), 2), theirs
+
+    def to_owner_core(part, pieces=1):
+        size = part.shape[1] // pieces
+        sent = [part[1, i * size : (i + 1) * size] for i in range(pieces)]
+        got = [lax.ppermute(x, AXES, [(i, i ^ 1) for i in devices]) for x in sent]
+        return part[0] + jnp.concatenate(got, 0)
 
     def weighted(share):
         return jnp.dot(share * scale[:, None], weight.astype(jnp.float32), precision=lax.Precision.HIGHEST)
 
-    ours, theirs = gather(scaled, coded, counts, add)
+    ours, theirs = gather(scaled, coded, prepare, add)
     return jax.nn.relu(weighted(ours) + weighted(theirs)).astype(jnp.bfloat16)
 
 

time: 113 us -> 112 us (level)
  the two profiles are of different devices: /device:TPU:1 before, /device:TPU:6 now
where the time goes in v3:
time: 112 us
  waiting for transfers between devices  55.4 us (49%)
  starting transfers between devices  24.5 us (22%)
  Pallas kernels  23.7 us (21%)
  other arithmetic  5.43 us (5%)
  matrix products  1.3 us (1%)
    ppermute x14, waiting for transfers between devices, moved(): lax.ppermute(self.rows, AXES, [(sender(*d), member(*d)) for d in here])  48.6 us
    ppermute x14, starting transfers between devices, moved(): lax.ppermute(self.rows, AXES, [(sender(*d), member(*d)) for d in here])  20.5 us
    pallas_call x6, Pallas kernels, products(): pl.pallas_call(functools.partial(product_kernel, buckets, first_bucket, m...  17.8 us
    pallas_call x1, Pallas kernels, slot_lists(): pl.pallas_call(list_kernel, out_shape=(jax.ShapeDtypeStruct((8 * PHASES +...  5.95 us
    ppermute x1, waiting for transfers between devices, add(): theirs = lax.ppermute(theirs, AXES, [(i, i ^ 2) for i in devices])  5.63 us
    ppermute x3, starting transfers between devices, to_owner_core(): got = [lax.ppermute(x, AXES, [(i, i ^ 1) for i in devices]) for x in sent]  3.94 us
  transfers between devices with their start and end apart: 18, of which 14 were waited for; matrix products, arithmetic and copies ran while one was open for 4% of the time, Pallas kernels for 20%

profile of v3, /device:TPU:6, one launch (start us, length us, event | category | flops | bytes accessed | tf_op | source)
XLA Modules:
  0.0 111.8 jit_solution(2578002824035999850)
XLA Ops:
  0.7 1.0 multiply_convert_fusion
  1.7 4.2 %collective-permute-start.1 = (bf16[256,256]{1,0:T(8,128)(2,1)S(1)}, bf16[256,256]{1,0:T(8,128)(2,1)S(1)}, u32[]{:S(2)}, u32[]{:S(2)}) collective-permute-start(bf16[256,256]{1,0:T(8,128)(2,1)S(1)} %multiply_convert_fusion), channel_id=1, source_target_pairs={{128,0},{157,1},{154,2},{135,3},{132,4},{129,5},{158,6},{139,7},{1... | collective-permute-start | bytes 393224 | tf_op jit(solution)/shard_map/ppermute | solution.py:57
  5.9 6.4 %collective-permute-start = (bf16[256,256]{1,0:T(8,128)(2,1)S(1)}, bf16[256,256]{1,0:T(8,128)(2,1)S(1)}, u32[]{:S(2)}, u32[]{:S(2)}) collective-permute-start(bf16[256,256]{1,0:T(8,128)(2,1)S(1)} %multiply_convert_fusion), channel_id=1, source_target_pairs={{0,0},{29,1},{26,2},{7,3},{4,4},{1,5},{30,6},{11,7},{8,8},{5,9},{2... | collective-permute-start | bytes 393224 | tf_op jit(solution)/shard_map/ppermute | solution.py:57
  12.4 0.8 fusion.24
  13.3 1.2 %select_reduce_fusion = s32[16,22]{0,1:T(8,128)S(1)} fusion(s32[128]{0:T(128)} %constant.12.clone, s32[16,22]{0,1:T(8,128)S(1)} %copy.9), kind=kLoop, calls=%fused_computation.29 | loop fusion | flops 134816 | bytes 3328 | tf_op jit(solution)/shard_map/reduce_sum | solution.py:227
  15.3 1.0 collective-permute-done
  16.3 1.7 %collective-permute-start.3 = (bf16[512,256]{1,0:T(8,128)(2,1)S(1)}, bf16[512,256]{1,0:T(8,128)(2,1)S(1)}, u32[]{:S(2)}, u32[]{:S(2)}) collective-permute-start(bf16[512,256]{1,0:T(8,128)(2,1)S(1)} %pad_maximum_fusion.8), channel_id=1, source_target_pairs={{32,0},{97,1},{34,2},{99,3},{36,4},{101,5},{38,6},{103,7},{40,8},{... | collective-permute-start | bytes 786440 | tf_op jit(solution)/shard_map/ppermute | solution.py:57
  18.0 4.8 %collective-permute-done.3 = bf16[512,256]{1,0:T(8,128)(2,1)S(1)} collective-permute-done((bf16[512,256]{1,0:T(8,128)(2,1)S(1)}, bf16[512,256]{1,0:T(8,128)(2,1)S(1)}, u32[]{:S(2)}, u32[]{:S(2)}) %collective-permute-start.3) | collective-permute-done | bytes 262176 | tf_op jit(solution)/shard_map/ppermute | solution.py:57
  22.8 1.0 collective-permute-done.2
  23.9 2.3 %collective-permute-start.5 = (bf16[1024,256]{1,0:T(8,128)(2,1)S(1)}, bf16[1024,256]{1,0:T(8,128)(2,1)S(1)}, u32[]{:S(2)}, u32[]{:S(2)}) collective-permute-start(bf16[1024,256]{1,0:T(8,128)(2,1)S(1)} %get-tuple-element.55), channel_id=1, source_target_pairs={{96,0},{33,1},{98,2},{35,3},{100,4},{37,5},{102,6},{39,7},{104,8},... | collective-permute-start | bytes 1572872 | tf_op jit(solution)/shard_map/ppermute | solution.py:57
  26.2 6.0 %shard_map.82 = (s32[41,128]{1,0:T(8,128)S(1)}, s32[40]{0:T(128)S(1)}, bf16[352,128,128]{2,1,0:T(8,128)(2,1)S(1)}) custom-call(s32[16]{0:T(128)S(1)} %bitcast.69, s32[16,22]{1,0:T(8,128)S(1)} %fusion.19.coded, bf16[352,128,128]{2,1,0:T(8,128)(2,1)} %bitcast.70), custom_call_target="tpu_custom_call" | custom-call | bytes 23000000 | tf_op jit(solution)/shard_map/pallas_call | solution.py:145
  32.2 2.1 %collective-permute-done.5 = bf16[1024,256]{1,0:T(8,128)(2,1)S(1)} collective-permute-done((bf16[1024,256]{1,0:T(8,128)(2,1)S(1)}, bf16[1024,256]{1,0:T(8,128)(2,1)S(1)}, u32[]{:S(2)}, u32[]{:S(2)}) %collective-permute-start.5) | collective-permute-done | bytes 524320 | tf_op jit(solution)/shard_map/ppermute | solution.py:57
  34.3 2.5 %collective-permute-done.4 = bf16[1024,256]{1,0:T(8,128)(2,1)S(1)} collective-permute-done((bf16[1024,256]{1,0:T(8,128)(2,1)S(1)}, bf16[1024,256]{1,0:T(8,128)(2,1)S(1)}, u32[]{:S(2)}, u32[]{:S(2)}) %collective-permute-start.4) | collective-permute-done | bytes 524320 | tf_op jit(solution)/shard_map/ppermute | solution.py:57
  38.0 3.6 %shard_map.83.refs_0_ = f32[4,256,256]{2,1,0:T(8,128)S(1)} custom-call(s32[41,128]{1,0:T(8,128)S(1)} %get-tuple-element.25.lists, s32[40]{0:T(128)S(1)} %get-tuple-element.26.counts, bf16[352,128,128]{2,1,0:T(8,128)(2,1)S(1)} %get-tuple-element.27.tiles, bf16[29,128,256]{2,1,0:T(8,128)(2,1)S(1)} %bitcast.68), custom_call_target="tpu_custom_call" | custom-call | flops 176400000 | bytes 3150000 | tf_op jit(solution)/shard_map/pallas_call | solution.py:193
  41.5 3.4 %collective-permute-done.7 = bf16[768,256]{1,0:T(8,128)(2,1)S(1)} collective-permute-done((bf16[768,256]{1,0:T(8,128)(2,1)S(1)}, bf16[768,256]{1,0:T(8,128)(2,1)S(1)}, u32[]{:S(2)}, u32[]{:S(2)}) %collective-permute-start.7) | collective-permute-done | bytes 393248 | tf_op jit(solution)/shard_map/ppermute | solution.py:57
  45.0 4.8 %collective-permute-done.6 = bf16[1792,256]{1,0:T(8,128)(2,1)S(1)} collective-permute-done((bf16[1792,256]{1,0:T(8,128)(2,1)S(1)}, bf16[1792,256]{1,0:T(8,128)(2,1)S(1)}, u32[]{:S(2)}, u32[]{:S(2)}) %collective-permute-start.6) | collective-permute-done | bytes 917536 | tf_op jit(solution)/shard_map/ppermute | solution.py:57
  50.4 1.2 %collective-permute-start.9 = (bf16[2048,256]{1,0:T(8,128)(2,1)S(1)}, bf16[2048,256]{1,0:T(8,128)(2,1)S(1)}, u32[]{:S(2)}, u32[]{:S(2)}) collective-permute-start(bf16[2048,256]{1,0:T(8,128)(2,1)S(1)} %get-tuple-element.32), channel_id=1, source_target_pairs={{96,0},{33,1},{98,2},{35,3},{100,4},{37,5},{102,6},{39,7},{104,8},... | collective-permute-start | bytes 3145736 | tf_op jit(solution)/shard_map/ppermute | solution.py:57
  51.7 2.9 %shard_map.84.refs_0_ = f32[4,256,256]{2,1,0:T(8,128)S(1)} custom-call(s32[41,128]{1,0:T(8,128)S(1)} %get-tuple-element.25.lists, s32[40]{0:T(128)S(1)} %get-tuple-element.26.counts, bf16[352,128,128]{2,1,0:T(8,128)(2,1)S(1)} %get-tuple-element.27.tiles, bf16[21,128,256]{2,1,0:T(8,128)(2,1)S(1)} %bitcast.66, f32[4,256,256]{2,1,0:T(8,128)S(1)} %shard_map.83.refs_0_), custom_call_target="tpu_custom_call" | custom-call | flops 126000000 | bytes 2250000 | tf_op jit(solution)/shard_map/pallas_call | solution.py:193
  54.6 11.8 %collective-permute-done.9 = bf16[2048,256]{1,0:T(8,128)(2,1)S(1)} collective-permute-done((bf16[2048,256]{1,0:T(8,128)(2,1)S(1)}, bf16[2048,256]{1,0:T(8,128)(2,1)S(1)}, u32[]{:S(2)}, u32[]{:S(2)}) %collective-permute-start.9) | collective-permute-done | bytes 1048608 | tf_op jit(solution)/shard_map/ppermute | solution.py:57
  66.4 2.9 %collective-permute-done.8 = bf16[2560,256]{1,0:T(8,128)(2,1)S(1)} collective-permute-done((bf16[2560,256]{1,0:T(8,128)(2,1)S(1)}, bf16[2560,256]{1,0:T(8,128)(2,1)S(1)}, u32[]{:S(2)}, u32[]{:S(2)}) %collective-permute-start.8) | collective-permute-done | bytes 1310752 | tf_op jit(solution)/shard_map/ppermute | solution.py:57
  70.6 2.9 %shard_map.85.refs_0_ = f32[4,256,256]{2,1,0:T(8,128)S(1)} custom-call(s32[41,128]{1,0:T(8,128)S(1)} %get-tuple-element.25.lists, s32[40]{0:T(128)S(1)} %get-tuple-element.26.counts, bf16[352,128,128]{2,1,0:T(8,128)(2,1)S(1)} %get-tuple-element.27.tiles, bf16[21,128,256]{2,1,0:T(8,128)(2,1)S(1)} %bitcast.67, f32[4,256,256]{2,1,0:T(8,128)S(1)} %shard_map.84.refs_0_), custom_call_target="tpu_custom_call" | custom-call | flops 126000000 | bytes 2250000 | tf_op jit(solution)/shard_map/pallas_call | solution.py:193
  73.5 7.9 %collective-permute-done.11 = bf16[1536,256]{1,0:T(8,128)(2,1)S(1)} collective-permute-done((bf16[1536,256]{1,0:T(8,128)(2,1)S(1)}, bf16[1536,256]{1,0:T(8,128)(2,1)S(1)}, u32[]{:S(2)}, u32[]{:S(2)}) %collective-permute-start.11) | collective-permute-done | bytes 786464 | tf_op jit(solution)/shard_map/ppermute | solution.py:57
  82.0 2.0 %collective-permute-start.13 = (bf16[1024,256]{1,0:T(8,128)(2,1)S(1)}, bf16[1024,256]{1,0:T(8,128)(2,1)S(1)}, u32[]{:S(2)}, u32[]{:S(2)}) collective-permute-start(bf16[1024,256]{1,0:T(8,128)(2,1)S(1)} %pad_maximum_fusion.6), channel_id=1, source_target_pairs={{96,0},{33,1},{98,2},{35,3},{100,4},{37,5},{102,6},{39,7},{104,8},... | collective-permute-start | bytes 1572872 | tf_op jit(solution)/shard_map/ppermute | solution.py:57
  84.6 4.2 %shard_map.86 = f32[4,256,256]{2,1,0:T(8,128)S(1)} custom-call(s32[41,128]{1,0:T(8,128)S(1)} %get-tuple-element.25.lists, s32[40]{0:T(128)S(1)} %get-tuple-element.26.counts, bf16[352,128,128]{2,1,0:T(8,128)(2,1)S(1)} %get-tuple-element.27.tiles, bf16[41,128,256]{2,1,0:T(8,128)(2,1)S(1)} %bitcast.65, f32[4,256,256]{2,1,0:T(8,128)S(1)} %shard_map.85.refs_0_), custom_call_target="tpu_custom_call" | custom-call | flops 252000000 | bytes 4500000 | tf_op jit(solution)/shard_map/pallas_call | solution.py:193
  88.8 3.6 %collective-permute-done.13 = bf16[1024,256]{1,0:T(8,128)(2,1)S(1)} collective-permute-done((bf16[1024,256]{1,0:T(8,128)(2,1)S(1)}, bf16[1024,256]{1,0:T(8,128)(2,1)S(1)}, u32[]{:S(2)}, u32[]{:S(2)}) %collective-permute-start.13) | collective-permute-done | bytes 524320 | tf_op jit(solution)/shard_map/ppermute | solution.py:57
  92.4 2.7 %collective-permute-done.12 = bf16[1536,256]{1,0:T(8,128)(2,1)S(1)} collective-permute-done((bf16[1536,256]{1,0:T(8,128)(2,1)S(1)}, bf16[1536,256]{1,0:T(8,128)(2,1)S(1)}, u32[]{:S(2)}, u32[]{:S(2)}) %collective-permute-start.12) | collective-permute-done | bytes 786464 | tf_op jit(solution)/shard_map/ppermute | solution.py:57
  95.2 1.9 %shard_map.87 = f32[2,256,256]{2,1,0:T(8,128)S(1)} custom-call(s32[41,128]{1,0:T(8,128)S(1)} %get-tuple-element.25.lists, s32[40]{0:T(128)S(1)} %get-tuple-element.26.counts, bf16[352,128,128]{2,1,0:T(8,128)(2,1)S(1)} %get-tuple-element.27.tiles, bf16[21,128,256]{2,1,0:T(8,128)(2,1)S(1)} %bitcast.63, f32[2,256,256]{2,1,0:T(8,128)S(1)} %slice.123.refs_0_), custom_call_target="tpu_custom_call" | custom-call | flops 260400000 | bytes 4650000 | tf_op jit(solution)/shard_map/pallas_call | solution.py:193
  97.2 3.3 %collective-permute-start.14 = (f32[256,256]{1,0:T(8,128)S(1)}, f32[256,256]{1,0:T(8,128)S(1)}, u32[]{:S(2)}, u32[]{:S(2)}) collective-permute-start(f32[256,256]{1,0:T(8,128)S(1)} %slice_bitcast_fusion.1), channel_id=1, source_target_pairs={{0,1},{1,0},{2,3},{3,2},{4,5},{5,4},{6,7},{7,6},{8,9},{9,8},{10,11... | collective-permute-start | bytes 786440 | tf_op jit(solution)/shard_map/ppermute | solution.py:254
  100.6 1.2 %collective-permute-done.14 = f32[256,256]{1,0:T(8,128)S(1)} collective-permute-done((f32[256,256]{1,0:T(8,128)S(1)}, f32[256,256]{1,0:T(8,128)S(1)}, u32[]{:S(2)}, u32[]{:S(2)}) %collective-permute-start.14) | collective-permute-done | bytes 262176 | tf_op jit(solution)/shard_map/ppermute | solution.py:254
  101.9 2.2 %shard_map.88 = f32[2,256,256]{2,1,0:T(8,128)S(1)} custom-call(s32[41,128]{1,0:T(8,128)S(1)} %get-tuple-element.25.lists, s32[40]{0:T(128)S(1)} %get-tuple-element.26.counts, bf16[352,128,128]{2,1,0:T(8,128)(2,1)S(1)} %get-tuple-element.27.tiles, bf16[21,128,256]{2,1,0:T(8,128)(2,1)S(1)} %bitcast.64, f32[2,256,256]{2,1,0:T(8,128)S(1)} %slice.106.refs_0_), custom_call_target="tpu_custom_call" | custom-call | flops 260400000 | bytes 4650000 | tf_op jit(solution)/shard_map/pallas_call | solution.py:193
  104.8 5.6 %collective-permute-done.17 = f32[256,256]{1,0:T(8,128)S(1)} collective-permute-done((f32[256,256]{1,0:T(8,128)S(1)}, f32[256,256]{1,0:T(8,128)S(1)}, u32[]{:S(2)}, u32[]{:S(2)}) %collective-permute-start.17) | collective-permute-done | bytes 262176 | tf_op jit(solution)/shard_map/ppermute | solution.py:248
  110.8 1.0 fusion.3
  (72 shorter events, 7.2 us)
Async XLA Ops:
  0.0 110.4 %copy-start = (bf16[256,256]{1,0:T(8,128)(2,1)S(1)}, bf16[256,256]{1,0:T(8,128)(2,1)}, u32[]{:S(2)}) copy-start(bf16[256,256]{1,0:T(8,128)(2,1)} %param.14) | copy-start | bytes 393220
  1.7 13.6 %collective-permute-start.1 = (bf16[256,256]{1,0:T(8,128)(2,1)S(1)}, bf16[256,256]{1,0:T(8,128)(2,1)S(1)}, u32[]{:S(2)}, u32[]{:S(2)}) collective-permute-start(bf16[256,256]{1,0:T(8,128)(2,1)S(1)} %multiply_convert_fusion), channel_id=1, source_target_pairs={{128,0},{157,1},{154,2},{135,3},{132,4},{129,5},{158,6},{139,7},{1... | collective-permute-start | bytes 393224 | tf_op jit(solution)/shard_map/ppermute | solution.py:57
  5.9 10.4 %collective-permute-start = (bf16[256,256]{1,0:T(8,128)(2,1)S(1)}, bf16[256,256]{1,0:T(8,128)(2,1)S(1)}, u32[]{:S(2)}, u32[]{:S(2)}) collective-permute-start(bf16[256,256]{1,0:T(8,128)(2,1)S(1)} %multiply_convert_fusion), channel_id=1, source_target_pairs={{0,0},{29,1},{26,2},{7,3},{4,4},{1,5},{30,6},{11,7},{8,8},{5,9},{2... | collective-permute-start | bytes 393224 | tf_op jit(solution)/shard_map/ppermute | solution.py:57
  14.5 11.7 %copy-start.1 = (s32[1,1,16]{2,1,0:T(1,128)S(1)}, s32[1,1,16]{2,1,0:T(1,128)}, u32[]{:S(2)}) copy-start(s32[1,1,16]{2,1,0:T(1,128)} %param.13) | copy-start | bytes 196
  16.3 6.5 %collective-permute-start.3 = (bf16[512,256]{1,0:T(8,128)(2,1)S(1)}, bf16[512,256]{1,0:T(8,128)(2,1)S(1)}, u32[]{:S(2)}, u32[]{:S(2)}) collective-permute-start(bf16[512,256]{1,0:T(8,128)(2,1)S(1)} %pad_maximum_fusion.8), channel_id=1, source_target_pairs={{32,0},{97,1},{34,2},{99,3},{36,4},{101,5},{38,6},{103,7},{40,8},{... | collective-permute-start | bytes 786440 | tf_op jit(solution)/shard_map/ppermute | solution.py:57
  18.0 5.8 %collective-permute-start.2 = (bf16[512,256]{1,0:T(8,128)(2,1)S(1)}, bf16[512,256]{1,0:T(8,128)(2,1)S(1)}, u32[]{:S(2)}, u32[]{:S(2)}) collective-permute-start(bf16[512,256]{1,0:T(8,128)(2,1)S(1)} %pad_maximum_fusion.8), channel_id=1, source_target_pairs={{5,0},{28,1},{7,2},{30,3},{9,4},{0,5},{11,6},{2,7},{13,8},{4,9},{1... | collective-permute-start | bytes 786440 | tf_op jit(solution)/shard_map/ppermute | solution.py:57
  23.9 10.5 %collective-permute-start.5 = (bf16[1024,256]{1,0:T(8,128)(2,1)S(1)}, bf16[1024,256]{1,0:T(8,128)(2,1)S(1)}, u32[]{:S(2)}, u32[]{:S(2)}) collective-permute-start(bf16[1024,256]{1,0:T(8,128)(2,1)S(1)} %get-tuple-element.55), channel_id=1, source_target_pairs={{96,0},{33,1},{98,2},{35,3},{100,4},{37,5},{102,6},{39,7},{104,8},... | collective-permute-start | bytes 1572872 | tf_op jit(solution)/shard_map/ppermute | solution.py:57
  26.1 10.7 %collective-permute-start.4 = (bf16[1024,256]{1,0:T(8,128)(2,1)S(1)}, bf16[1024,256]{1,0:T(8,128)(2,1)S(1)}, u32[]{:S(2)}, u32[]{:S(2)}) collective-permute-start(bf16[1024,256]{1,0:T(8,128)(2,1)S(1)} %get-tuple-element.56), channel_id=1, source_target_pairs={{159,0},{6,1},{29,2},{132,3},{131,4},{10,5},{1,6},{136,7},{135,8},... | collective-permute-start | bytes 1572872 | tf_op jit(solution)/shard_map/ppermute | solution.py:57
  36.9 12.9 %collective-permute-start.6 = (bf16[1792,256]{1,0:T(8,128)(2,1)S(1)}, bf16[1792,256]{1,0:T(8,128)(2,1)S(1)}, u32[]{:S(2)}, u32[]{:S(2)}) collective-permute-start(bf16[1792,256]{1,0:T(8,128)(2,1)S(1)} %pad_maximum_fusion.3), channel_id=1, source_target_pairs={{5,0},{28,1},{7,2},{30,3},{9,4},{0,5},{11,6},{2,7},{13,8},{4,9},{1... | collective-permute-start | bytes 2752520 | tf_op jit(solution)/shard_map/ppermute | solution.py:57
  37.1 7.9 %collective-permute-start.7 = (bf16[768,256]{1,0:T(8,128)(2,1)S(1)}, bf16[768,256]{1,0:T(8,128)(2,1)S(1)}, u32[]{:S(2)}, u32[]{:S(2)}) collective-permute-start(bf16[768,256]{1,0:T(8,128)(2,1)S(1)} %pad_maximum_fusion.7), channel_id=1, source_target_pairs={{32,0},{97,1},{34,2},{99,3},{36,4},{101,5},{38,6},{103,7},{40,8},{... | collective-permute-start | bytes 1179656 | tf_op jit(solution)/shard_map/ppermute | solution.py:57
  50.0 19.2 %collective-permute-start.8 = (bf16[2560,256]{1,0:T(8,128)(2,1)S(1)}, bf16[2560,256]{1,0:T(8,128)(2,1)S(1)}, u32[]{:S(2)}, u32[]{:S(2)}) collective-permute-start(bf16[2560,256]{1,0:T(8,128)(2,1)S(1)} %slice_dynamic-update-slice_fusion.1), channel_id=1, source_target_pairs={{159,0},{6,1},{29,2},{132,3},{131,4},{10,5},{1,6},{136,7},{135,8},... | collective-permute-start | bytes 3932168 | tf_op jit(solution)/shard_map/ppermute | solution.py:57
  50.4 16.0 %collective-permute-start.9 = (bf16[2048,256]{1,0:T(8,128)(2,1)S(1)}, bf16[2048,256]{1,0:T(8,128)(2,1)S(1)}, u32[]{:S(2)}, u32[]{:S(2)}) collective-permute-start(bf16[2048,256]{1,0:T(8,128)(2,1)S(1)} %get-tuple-element.32), channel_id=1, source_target_pairs={{96,0},{33,1},{98,2},{35,3},{100,4},{37,5},{102,6},{39,7},{104,8},... | collective-permute-start | bytes 3145736 | tf_op jit(solution)/shard_map/ppermute | solution.py:57
  69.4 12.1 %collective-permute-start.11 = (bf16[1536,256]{1,0:T(8,128)(2,1)S(1)}, bf16[1536,256]{1,0:T(8,128)(2,1)S(1)}, u32[]{:S(2)}, u32[]{:S(2)}) collective-permute-start(bf16[1536,256]{1,0:T(8,128)(2,1)S(1)} %constant_dynamic-update-slice_fusion.13), channel_id=1, source_target_pairs={{32,0},{97,1},{34,2},{99,3},{36,4},{101,5},{38,6},{103,7},{40,8},{... | collective-permute-start | bytes 2359304 | tf_op jit(solution)/shard_map/ppermute | solution.py:57
  70.1 11.4 %collective-permute-start.10 = (bf16[1536,256]{1,0:T(8,128)(2,1)S(1)}, bf16[1536,256]{1,0:T(8,128)(2,1)S(1)}, u32[]{:S(2)}, u32[]{:S(2)}) collective-permute-start(bf16[1536,256]{1,0:T(8,128)(2,1)S(1)} %slice.118), channel_id=1, source_target_pairs={{5,0},{28,1},{7,2},{30,3},{9,4},{0,5},{11,6},{2,7},{13,8},{4,9},{1... | collective-permute-start | bytes 2359304 | tf_op jit(solution)/shard_map/ppermute | solution.py:57
  81.6 13.6 %collective-permute-start.12 = (bf16[1536,256]{1,0:T(8,128)(2,1)S(1)}, bf16[1536,256]{1,0:T(8,128)(2,1)S(1)}, u32[]{:S(2)}, u32[]{:S(2)}) collective-permute-start(bf16[1536,256]{1,0:T(8,128)(2,1)S(1)} %collective-permute-done.10), channel_id=1, source_target_pairs={{159,0},{6,1},{29,2},{132,3},{131,4},{10,5},{1,6},{136,7},{135,8},... | collective-permute-start | bytes 2359304 | tf_op jit(solution)/shard_map/ppermute | solution.py:57
  82.0 10.4 %collective-permute-start.13 = (bf16[1024,256]{1,0:T(8,128)(2,1)S(1)}, bf16[1024,256]{1,0:T(8,128)(2,1)S(1)}, u32[]{:S(2)}, u32[]{:S(2)}) collective-permute-start(bf16[1024,256]{1,0:T(8,128)(2,1)S(1)} %pad_maximum_fusion.6), channel_id=1, source_target_pairs={{96,0},{33,1},{98,2},{35,3},{100,4},{37,5},{102,6},{39,7},{104,8},... | collective-permute-start | bytes 1572872 | tf_op jit(solution)/shard_map/ppermute | solution.py:57
  95.2 6.6 %copy-start.2 = (s32[256]{0:T(256)S(1)}, s32[256]{0:T(256)}, u32[]{:S(2)}) copy-start(s32[256]{0:T(256)} %param.9) | copy-start | bytes 3076
  97.2 4.5 %collective-permute-start.14 = (f32[256,256]{1,0:T(8,128)S(1)}, f32[256,256]{1,0:T(8,128)S(1)}, u32[]{:S(2)}, u32[]{:S(2)}) collective-permute-start(f32[256,256]{1,0:T(8,128)S(1)} %slice_bitcast_fusion.1), channel_id=1, source_target_pairs={{0,1},{1,0},{2,3},{3,2},{4,5},{5,4},{6,7},{7,6},{8,9},{9,8},{10,11... | collective-permute-start | bytes 786440 | tf_op jit(solution)/shard_map/ppermute | solution.py:254
  101.8 8.7 %collective-permute-start.17 = (f32[256,256]{1,0:T(8,128)S(1)}, f32[256,256]{1,0:T(8,128)S(1)}, u32[]{:S(2)}, u32[]{:S(2)}) collective-permute-start(f32[256,256]{1,0:T(8,128)S(1)} %fusion.7), channel_id=1, source_target_pairs={{0,2},{1,3},{2,0},{3,1},{4,6},{5,7},{6,4},{7,5},{8,10},{9,11},{10,... | collective-permute-start | bytes 786440 | tf_op jit(solution)/shard_map/ppermute | solution.py:248
  104.2 6.6 %collective-permute-start.15 = (f32[128,256]{1,0:T(8,128)S(1)}, f32[128,256]{1,0:T(8,128)S(1)}, u32[]{:S(2)}, u32[]{:S(2)}) collective-permute-start(f32[128,256]{1,0:T(8,128)S(1)} %get-tuple-element.46), channel_id=1, source_target_pairs={{0,1},{1,0},{2,3},{3,2},{4,5},{5,4},{6,7},{7,6},{8,9},{9,8},{10,11... | collective-permute-start | bytes 393224 | tf_op jit(solution)/shard_map/ppermute | solution.py:254
  104.4 6.4 %collective-permute-start.16 = (f32[128,256]{1,0:T(8,128)S(1)}, f32[128,256]{1,0:T(8,128)S(1)}, u32[]{:S(2)}, u32[]{:S(2)}) collective-permute-start(f32[128,256]{1,0:T(8,128)S(1)} %get-tuple-element.47), channel_id=1, source_target_pairs={{0,1},{1,0},{2,3},{3,2},{4,5},{5,4},{6,7},{7,6},{8,9},{9,8},{10,11... | collective-permute-start | bytes 393224 | tf_op jit(solution)/shard_map/ppermute | solution.py:254

commit v4 on v3

--- a/solution.py
+++ b/solution.py
@@ -19,6 +19,7 @@
 PHASES = 5
 
 HOME = (0, 1, 2, -1)
+PIECE = (1, 2, 0, 3)
 
 
 def member(h, y, z, q):
@@ -34,8 +35,8 @@
 
 
 MOVES = {
-    "home": (lambda h, y, z, q: member(h, y, z - HOME[q], q), lambda t, h, p, e: (t, h, p, e)),
-    "far": (lambda h, y, z, q: member(h + 1, y, z - HOME[q], q), lambda t, h, p, e: (t, 1 - h, p, e)),
+    "home": (lambda h, y, z, q: member(h, y, z - HOME[q], PIECE[q]), lambda t, h, p, e: (t, h, p, e)),
+    "far": (lambda h, y, z, q: member(h + 1, y, z - HOME[q], PIECE[q]), lambda t, h, p, e: (t, 1 - h, p, e)),
     "z1": (lambda *d: down(*d) if d[3] % 2 else up(*d), lambda t, h, p, e: (t, h, (1 - p) % 8, e)),
     "z2": (lambda *d: up(*d) if d[3] % 2 else down(*d), lambda t, h, p, e: (t, h, (-1 - p) % 8, e)),
     "y1": (lambda h, y, z, q: member(h, y ^ (3 if q % 2 else 1), z, q), lambda t, h, p, e: (t, h, p, e ^ 1)),
@@ -210,12 +211,13 @@
     cols, steps = tile_cols[0, 0], jnp.arange(STEPS, dtype=jnp.int32)[:, None]
     source = (row - mine - 4 * steps) & 63
     piece, t = cols >> 1, cols & 1
-    p = ((source & 7) + jnp.where(piece == 3, -1, piece) - row) & 7
+    home = sum(jnp.where(piece == PIECE[i], i, 0) for i in range(4))
+    p = ((source & 7) + jnp.where(home == 3, -1, home) - row) & 7
     h = ((source >> 5) - (row >> 5) - ((mine + p) >> 2)) & 1
     core = mine & 1
     p = jnp.where(core == 1, -p & 7, p)
     y = ((source >> 3) ^ (row >> 3)) & 3
-    swapped = jnp.where(t == 0, core, piece & 1)
+    swapped = jnp.where(t == 0, core, home & 1)
     e = jnp.where(y == 2, 3, jnp.where(y == 0, 0, jnp.where(y == 1, 1 + swapped, 2 - swapped)))
     dest = tile_rows[0, 0]
     bucket = ((((dest >> 1) ^ mine) ^ 2) << 1) + (dest & 1)

time: 112 us -> 111 us (level)
  Pallas kernels: 23.7 us -> 18.4 us
  starting transfers between devices: 24.5 us -> 28.2 us
  waiting for transfers between devices: 55.4 us -> 56.6 us
    pallas_call x6, Pallas kernels: 17.8 us -> 12.4 us  [products(): pl.pallas_call(functools.partial(product_kernel, buckets, first_bucket, m...]
    ppermute x3, starting transfers between devices: 3.94 us -> 6.48 us  [to_owner_core(): got = [lax.ppermute(x, AXES, [(i, i ^ 1) for i in devices]) for x in sent]]
    ppermute x14, starting transfers between devices: 20.5 us -> 21.7 us  [moved(): lax.ppermute(self.rows, AXES, [(sender(*d), member(*d)) for d in here])]
  transfers between devices with their start and end apart: 18 -> 18, of which waited for: 14 -> 15; matrix products, arithmetic and copies ran while one was open for 4% -> 4% of each run, Pallas kernels for 20% -> 15%
where the time goes in v4:
time: 111 us
  waiting for transfers between devices  56.6 us (51%)
  starting transfers between devices  28.2 us (25%)
  Pallas kernels  18.4 us (17%)
  other arithmetic  5.42 us (5%)
  matrix products  1.3 us (1%)
    ppermute x14, waiting for transfers between devices, moved(): lax.ppermute(self.rows, AXES, [(sender(*d), member(*d)) for d in here])  49.2 us
    ppermute x14, starting transfers between devices, moved(): lax.ppermute(self.rows, AXES, [(sender(*d), member(*d)) for d in here])  21.7 us
    pallas_call x6, Pallas kernels, products(): pl.pallas_call(functools.partial(product_kernel, buckets, first_bucket, m...  12.4 us
    ppermute x3, starting transfers between devices, to_owner_core(): got = [lax.ppermute(x, AXES, [(i, i ^ 1) for i in devices]) for x in sent]  6.48 us
    ppermute x1, waiting for transfers between devices, add(): theirs = lax.ppermute(theirs, AXES, [(i, i ^ 2) for i in devices])  6.25 us
    pallas_call x1, Pallas kernels, slot_lists(): pl.pallas_call(list_kernel, out_shape=(jax.ShapeDtypeStruct((8 * PHASES +...  5.95 us
  transfers between devices with their start and end apart: 18, of which 15 were waited for; matrix products, arithmetic and copies ran while one was open for 4% of the time, Pallas kernels for 15%

profile of v4, /device:TPU:6, one launch (start us, length us, event | category | flops | bytes accessed | tf_op | source)
XLA Modules:
  0.0 111.3 jit_solution(16394783317702023982)
XLA Ops:
  1.7 1.4 %collective-permute-start.1 = (bf16[256,256]{1,0:T(8,128)(2,1)S(1)}, bf16[256,256]{1,0:T(8,128)(2,1)S(1)}, u32[]{:S(2)}, u32[]{:S(2)}) collective-permute-start(bf16[256,256]{1,0:T(8,128)(2,1)S(1)} %multiply_convert_fusion), channel_id=1, source_target_pairs={{129,0},{158,1},{152,2},{135,3},{133,4},{130,5},{156,6},{139,7},{1... | collective-permute-start | bytes 393224 | tf_op jit(solution)/shard_map/ppermute | solution.py:58
  3.1 1.1 %collective-permute-start = (bf16[256,256]{1,0:T(8,128)(2,1)S(1)}, bf16[256,256]{1,0:T(8,128)(2,1)S(1)}, u32[]{:S(2)}, u32[]{:S(2)}) collective-permute-start(bf16[256,256]{1,0:T(8,128)(2,1)S(1)} %multiply_convert_fusion), channel_id=1, source_target_pairs={{1,0},{30,1},{24,2},{7,3},{5,4},{2,5},{28,6},{11,7},{9,8},{6,9},{0... | collective-permute-start | bytes 393224 | tf_op jit(solution)/shard_map/ppermute | solution.py:58
  5.2 1.2 %select_reduce_fusion = s32[16,22]{0,1:T(8,128)S(1)} fusion(s32[128]{0:T(128)} %constant.11.clone, s32[16,22]{0,1:T(8,128)S(1)} %copy.9), kind=kLoop, calls=%fused_computation.29 | loop fusion | flops 134816 | bytes 3328 | tf_op jit(solution)/shard_map/reduce_sum | solution.py:229
  7.2 3.9 %collective-permute-done.1 = bf16[256,256]{1,0:T(8,128)(2,1)S(1)} collective-permute-done((bf16[256,256]{1,0:T(8,128)(2,1)S(1)}, bf16[256,256]{1,0:T(8,128)(2,1)S(1)}, u32[]{:S(2)}, u32[]{:S(2)}) %collective-permute-start.1) | collective-permute-done | bytes 131104 | tf_op jit(solution)/shard_map/ppermute | solution.py:58
  11.1 2.2 %collective-permute-done = bf16[256,256]{1,0:T(8,128)(2,1)S(1)} collective-permute-done((bf16[256,256]{1,0:T(8,128)(2,1)S(1)}, bf16[256,256]{1,0:T(8,128)(2,1)S(1)}, u32[]{:S(2)}, u32[]{:S(2)}) %collective-permute-start) | collective-permute-done | bytes 131104 | tf_op jit(solution)/shard_map/ppermute | solution.py:58
  13.4 1.7 %collective-permute-start.3 = (bf16[512,256]{1,0:T(8,128)(2,1)S(1)}, bf16[512,256]{1,0:T(8,128)(2,1)S(1)}, u32[]{:S(2)}, u32[]{:S(2)}) collective-permute-start(bf16[512,256]{1,0:T(8,128)(2,1)S(1)} %pad_maximum_fusion.8), channel_id=1, source_target_pairs={{32,0},{97,1},{34,2},{99,3},{36,4},{101,5},{38,6},{103,7},{40,8},{... | collective-permute-start | bytes 786440 | tf_op jit(solution)/shard_map/ppermute | solution.py:58
  15.3 4.5 %collective-permute-done.3 = bf16[512,256]{1,0:T(8,128)(2,1)S(1)} collective-permute-done((bf16[512,256]{1,0:T(8,128)(2,1)S(1)}, bf16[512,256]{1,0:T(8,128)(2,1)S(1)}, u32[]{:S(2)}, u32[]{:S(2)}) %collective-permute-start.3) | collective-permute-done | bytes 262176 | tf_op jit(solution)/shard_map/ppermute | solution.py:58
  20.9 2.3 %collective-permute-start.5 = (bf16[1024,256]{1,0:T(8,128)(2,1)S(1)}, bf16[1024,256]{1,0:T(8,128)(2,1)S(1)}, u32[]{:S(2)}, u32[]{:S(2)}) collective-permute-start(bf16[1024,256]{1,0:T(8,128)(2,1)S(1)} %get-tuple-element.55), channel_id=1, source_target_pairs={{96,0},{33,1},{98,2},{35,3},{100,4},{37,5},{102,6},{39,7},{104,8},... | collective-permute-start | bytes 1572872 | tf_op jit(solution)/shard_map/ppermute | solution.py:58
  24.3 6.0 %shard_map.82 = (s32[41,128]{1,0:T(8,128)S(1)}, s32[40]{0:T(128)S(1)}, bf16[352,128,128]{2,1,0:T(8,128)(2,1)S(1)}) custom-call(s32[16]{0:T(128)S(1)} %bitcast.69, s32[16,22]{1,0:T(8,128)S(1)} %fusion.19.coded, bf16[352,128,128]{2,1,0:T(8,128)(2,1)} %bitcast.70), custom_call_target="tpu_custom_call" | custom-call | bytes 23000000 | tf_op jit(solution)/shard_map/pallas_call | solution.py:146
  30.3 1.1 collective-permute-done.5
  31.4 2.5 %collective-permute-done.4 = bf16[1024,256]{1,0:T(8,128)(2,1)S(1)} collective-permute-done((bf16[1024,256]{1,0:T(8,128)(2,1)S(1)}, bf16[1024,256]{1,0:T(8,128)(2,1)S(1)}, u32[]{:S(2)}, u32[]{:S(2)}) %collective-permute-start.4) | collective-permute-done | bytes 524320 | tf_op jit(solution)/shard_map/ppermute | solution.py:58
  34.0 1.5 %collective-permute-start.6 = (bf16[1792,256]{1,0:T(8,128)(2,1)S(1)}, bf16[1792,256]{1,0:T(8,128)(2,1)S(1)}, u32[]{:S(2)}, u32[]{:S(2)}) collective-permute-start(bf16[1792,256]{1,0:T(8,128)(2,1)S(1)} %pad_maximum_fusion.3), channel_id=1, source_target_pairs={{5,0},{28,1},{7,2},{30,3},{9,4},{0,5},{11,6},{2,7},{13,8},{4,9},{1... | collective-permute-start | bytes 2752520 | tf_op jit(solution)/shard_map/ppermute | solution.py:58
  36.4 2.3 %shard_map.83.refs_0_ = f32[4,256,256]{2,1,0:T(8,128)S(1)} custom-call(s32[41,128]{1,0:T(8,128)S(1)} %get-tuple-element.25.lists, s32[40]{0:T(128)S(1)} %get-tuple-element.26.counts, bf16[352,128,128]{2,1,0:T(8,128)(2,1)S(1)} %get-tuple-element.27.tiles, bf16[29,128,256]{2,1,0:T(8,128)(2,1)S(1)} %bitcast.68), custom_call_target="tpu_custom_call" | custom-call | flops 176400000 | bytes 3150000 | tf_op jit(solution)/shard_map/pallas_call | solution.py:194
  38.7 4.7 %collective-permute-done.7 = bf16[768,256]{1,0:T(8,128)(2,1)S(1)} collective-permute-done((bf16[768,256]{1,0:T(8,128)(2,1)S(1)}, bf16[768,256]{1,0:T(8,128)(2,1)S(1)}, u32[]{:S(2)}, u32[]{:S(2)}) %collective-permute-start.7) | collective-permute-done | bytes 393248 | tf_op jit(solution)/shard_map/ppermute | solution.py:58
  43.4 3.5 %collective-permute-done.6 = bf16[1792,256]{1,0:T(8,128)(2,1)S(1)} collective-permute-done((bf16[1792,256]{1,0:T(8,128)(2,1)S(1)}, bf16[1792,256]{1,0:T(8,128)(2,1)S(1)}, u32[]{:S(2)}, u32[]{:S(2)}) %collective-permute-start.6) | collective-permute-done | bytes 917536 | tf_op jit(solution)/shard_map/ppermute | solution.py:58
  47.1 1.6 %collective-permute-start.8 = (bf16[2560,256]{1,0:T(8,128)(2,1)S(1)}, bf16[2560,256]{1,0:T(8,128)(2,1)S(1)}, u32[]{:S(2)}, u32[]{:S(2)}) collective-permute-start(bf16[2560,256]{1,0:T(8,128)(2,1)S(1)} %slice_dynamic-update-slice_fusion.1), channel_id=1, source_target_pairs={{159,0},{6,1},{29,2},{132,3},{131,4},{10,5},{1,6},{136,7},{135,8},... | collective-permute-start | bytes 3932168 | tf_op jit(solution)/shard_map/ppermute | solution.py:58
  48.7 2.9 %collective-permute-start.9 = (bf16[2048,256]{1,0:T(8,128)(2,1)S(1)}, bf16[2048,256]{1,0:T(8,128)(2,1)S(1)}, u32[]{:S(2)}, u32[]{:S(2)}) collective-permute-start(bf16[2048,256]{1,0:T(8,128)(2,1)S(1)} %get-tuple-element.32), channel_id=1, source_target_pairs={{96,0},{33,1},{98,2},{35,3},{100,4},{37,5},{102,6},{39,7},{104,8},... | collective-permute-start | bytes 3145736 | tf_op jit(solution)/shard_map/ppermute | solution.py:58
  51.6 2.0 %shard_map.84.refs_0_ = f32[4,256,256]{2,1,0:T(8,128)S(1)} custom-call(s32[41,128]{1,0:T(8,128)S(1)} %get-tuple-element.25.lists, s32[40]{0:T(128)S(1)} %get-tuple-element.26.counts, bf16[352,128,128]{2,1,0:T(8,128)(2,1)S(1)} %get-tuple-element.27.tiles, bf16[21,128,256]{2,1,0:T(8,128)(2,1)S(1)} %bitcast.66, f32[4,256,256]{2,1,0:T(8,128)S(1)} %shard_map.83.refs_0_), custom_call_target="tpu_custom_call" | custom-call | flops 126000000 | bytes 2250000 | tf_op jit(solution)/shard_map/pallas_call | solution.py:194
  53.6 11.0 %collective-permute-done.9 = bf16[2048,256]{1,0:T(8,128)(2,1)S(1)} collective-permute-done((bf16[2048,256]{1,0:T(8,128)(2,1)S(1)}, bf16[2048,256]{1,0:T(8,128)(2,1)S(1)}, u32[]{:S(2)}, u32[]{:S(2)}) %collective-permute-start.9) | collective-permute-done | bytes 1048608 | tf_op jit(solution)/shard_map/ppermute | solution.py:58
  64.7 1.6 %collective-permute-done.8 = bf16[2560,256]{1,0:T(8,128)(2,1)S(1)} collective-permute-done((bf16[2560,256]{1,0:T(8,128)(2,1)S(1)}, bf16[2560,256]{1,0:T(8,128)(2,1)S(1)}, u32[]{:S(2)}, u32[]{:S(2)}) %collective-permute-start.8) | collective-permute-done | bytes 1310752 | tf_op jit(solution)/shard_map/ppermute | solution.py:58
  67.2 1.8 %collective-permute-start.10 = (bf16[1536,256]{1,0:T(8,128)(2,1)S(1)}, bf16[1536,256]{1,0:T(8,128)(2,1)S(1)}, u32[]{:S(2)}, u32[]{:S(2)}) collective-permute-start(bf16[1536,256]{1,0:T(8,128)(2,1)S(1)} %slice.118), channel_id=1, source_target_pairs={{5,0},{28,1},{7,2},{30,3},{9,4},{0,5},{11,6},{2,7},{13,8},{4,9},{1... | collective-permute-start | bytes 2359304 | tf_op jit(solution)/shard_map/ppermute | solution.py:58
  69.1 2.0 %shard_map.85.refs_0_ = f32[4,256,256]{2,1,0:T(8,128)S(1)} custom-call(s32[41,128]{1,0:T(8,128)S(1)} %get-tuple-element.25.lists, s32[40]{0:T(128)S(1)} %get-tuple-element.26.counts, bf16[352,128,128]{2,1,0:T(8,128)(2,1)S(1)} %get-tuple-element.27.tiles, bf16[21,128,256]{2,1,0:T(8,128)(2,1)S(1)} %bitcast.67, f32[4,256,256]{2,1,0:T(8,128)S(1)} %shard_map.84.refs_0_), custom_call_target="tpu_custom_call" | custom-call | flops 126000000 | bytes 2250000 | tf_op jit(solution)/shard_map/pallas_call | solution.py:194
  71.1 7.4 %collective-permute-done.11 = bf16[1536,256]{1,0:T(8,128)(2,1)S(1)} collective-permute-done((bf16[1536,256]{1,0:T(8,128)(2,1)S(1)}, bf16[1536,256]{1,0:T(8,128)(2,1)S(1)}, u32[]{:S(2)}, u32[]{:S(2)}) %collective-permute-start.11) | collective-permute-done | bytes 786464 | tf_op jit(solution)/shard_map/ppermute | solution.py:58
  78.6 3.4 %collective-permute-start.12 = (bf16[1536,256]{1,0:T(8,128)(2,1)S(1)}, bf16[1536,256]{1,0:T(8,128)(2,1)S(1)}, u32[]{:S(2)}, u32[]{:S(2)}) collective-permute-start(bf16[1536,256]{1,0:T(8,128)(2,1)S(1)} %collective-permute-done.10), channel_id=1, source_target_pairs={{159,0},{6,1},{29,2},{132,3},{131,4},{10,5},{1,6},{136,7},{135,8},... | collective-permute-start | bytes 2359304 | tf_op jit(solution)/shard_map/ppermute | solution.py:58
  82.0 1.4 %collective-permute-start.13 = (bf16[1024,256]{1,0:T(8,128)(2,1)S(1)}, bf16[1024,256]{1,0:T(8,128)(2,1)S(1)}, u32[]{:S(2)}, u32[]{:S(2)}) collective-permute-start(bf16[1024,256]{1,0:T(8,128)(2,1)S(1)} %pad_maximum_fusion.6), channel_id=1, source_target_pairs={{96,0},{33,1},{98,2},{35,3},{100,4},{37,5},{102,6},{39,7},{104,8},... | collective-permute-start | bytes 1572872 | tf_op jit(solution)/shard_map/ppermute | solution.py:58
  83.9 2.8 %shard_map.86 = f32[4,256,256]{2,1,0:T(8,128)S(1)} custom-call(s32[41,128]{1,0:T(8,128)S(1)} %get-tuple-element.25.lists, s32[40]{0:T(128)S(1)} %get-tuple-element.26.counts, bf16[352,128,128]{2,1,0:T(8,128)(2,1)S(1)} %get-tuple-element.27.tiles, bf16[41,128,256]{2,1,0:T(8,128)(2,1)S(1)} %bitcast.65, f32[4,256,256]{2,1,0:T(8,128)S(1)} %shard_map.85.refs_0_), custom_call_target="tpu_custom_call" | custom-call | flops 252000000 | bytes 4500000 | tf_op jit(solution)/shard_map/pallas_call | solution.py:194
  86.7 5.7 %collective-permute-done.13 = bf16[1024,256]{1,0:T(8,128)(2,1)S(1)} collective-permute-done((bf16[1024,256]{1,0:T(8,128)(2,1)S(1)}, bf16[1024,256]{1,0:T(8,128)(2,1)S(1)}, u32[]{:S(2)}, u32[]{:S(2)}) %collective-permute-start.13) | collective-permute-done | bytes 524320 | tf_op jit(solution)/shard_map/ppermute | solution.py:58
  92.5 1.6 %shard_map.87 = f32[2,256,256]{2,1,0:T(8,128)S(1)} custom-call(s32[41,128]{1,0:T(8,128)S(1)} %get-tuple-element.25.lists, s32[40]{0:T(128)S(1)} %get-tuple-element.26.counts, bf16[352,128,128]{2,1,0:T(8,128)(2,1)S(1)} %get-tuple-element.27.tiles, bf16[21,128,256]{2,1,0:T(8,128)(2,1)S(1)} %bitcast.63, f32[2,256,256]{2,1,0:T(8,128)S(1)} %slice.123.refs_0_), custom_call_target="tpu_custom_call" | custom-call | flops 260400000 | bytes 4650000 | tf_op jit(solution)/shard_map/pallas_call | solution.py:194
  94.2 5.9 %collective-permute-start.14 = (f32[256,256]{1,0:T(8,128)S(1)}, f32[256,256]{1,0:T(8,128)S(1)}, u32[]{:S(2)}, u32[]{:S(2)}) collective-permute-start(f32[256,256]{1,0:T(8,128)S(1)} %slice_bitcast_fusion.1), channel_id=1, source_target_pairs={{0,1},{1,0},{2,3},{3,2},{4,5},{5,4},{6,7},{7,6},{8,9},{9,8},{10,11... | collective-permute-start | bytes 786440 | tf_op jit(solution)/shard_map/ppermute | solution.py:256
  100.1 1.2 %collective-permute-done.14 = f32[256,256]{1,0:T(8,128)S(1)} collective-permute-done((f32[256,256]{1,0:T(8,128)S(1)}, f32[256,256]{1,0:T(8,128)S(1)}, u32[]{:S(2)}, u32[]{:S(2)}) %collective-permute-start.14) | collective-permute-done | bytes 262176 | tf_op jit(solution)/shard_map/ppermute | solution.py:256
  101.4 1.6 %shard_map.88 = f32[2,256,256]{2,1,0:T(8,128)S(1)} custom-call(s32[41,128]{1,0:T(8,128)S(1)} %get-tuple-element.25.lists, s32[40]{0:T(128)S(1)} %get-tuple-element.26.counts, bf16[352,128,128]{2,1,0:T(8,128)(2,1)S(1)} %get-tuple-element.27.tiles, bf16[21,128,256]{2,1,0:T(8,128)(2,1)S(1)} %bitcast.64, f32[2,256,256]{2,1,0:T(8,128)S(1)} %slice.106.refs_0_), custom_call_target="tpu_custom_call" | custom-call | flops 260400000 | bytes 4650000 | tf_op jit(solution)/shard_map/pallas_call | solution.py:194
  103.7 6.2 %collective-permute-done.17 = f32[256,256]{1,0:T(8,128)S(1)} collective-permute-done((f32[256,256]{1,0:T(8,128)S(1)}, f32[256,256]{1,0:T(8,128)S(1)}, u32[]{:S(2)}, u32[]{:S(2)}) %collective-permute-start.17) | collective-permute-done | bytes 262176 | tf_op jit(solution)/shard_map/ppermute | solution.py:250
  (72 shorter events, 11.0 us)
Async XLA Ops:
  0.0 109.9 %copy-start = (bf16[256,256]{1,0:T(8,128)(2,1)S(1)}, bf16[256,256]{1,0:T(8,128)(2,1)}, u32[]{:S(2)}) copy-start(bf16[256,256]{1,0:T(8,128)(2,1)} %param.14) | copy-start | bytes 393220
  1.7 9.4 %collective-permute-start.1 = (bf16[256,256]{1,0:T(8,128)(2,1)S(1)}, bf16[256,256]{1,0:T(8,128)(2,1)S(1)}, u32[]{:S(2)}, u32[]{:S(2)}) collective-permute-start(bf16[256,256]{1,0:T(8,128)(2,1)S(1)} %multiply_convert_fusion), channel_id=1, source_target_pairs={{129,0},{158,1},{152,2},{135,3},{133,4},{130,5},{156,6},{139,7},{1... | collective-permute-start | bytes 393224 | tf_op jit(solution)/shard_map/ppermute | solution.py:58
  3.1 10.2 %collective-permute-start = (bf16[256,256]{1,0:T(8,128)(2,1)S(1)}, bf16[256,256]{1,0:T(8,128)(2,1)S(1)}, u32[]{:S(2)}, u32[]{:S(2)}) collective-permute-start(bf16[256,256]{1,0:T(8,128)(2,1)S(1)} %multiply_convert_fusion), channel_id=1, source_target_pairs={{1,0},{30,1},{24,2},{7,3},{5,4},{2,5},{28,6},{11,7},{9,8},{6,9},{0... | collective-permute-start | bytes 393224 | tf_op jit(solution)/shard_map/ppermute | solution.py:58
  6.3 17.9 %copy-start.1 = (s32[1,1,16]{2,1,0:T(1,128)S(1)}, s32[1,1,16]{2,1,0:T(1,128)}, u32[]{:S(2)}) copy-start(s32[1,1,16]{2,1,0:T(1,128)} %param.13) | copy-start | bytes 196
  13.4 6.5 %collective-permute-start.3 = (bf16[512,256]{1,0:T(8,128)(2,1)S(1)}, bf16[512,256]{1,0:T(8,128)(2,1)S(1)}, u32[]{:S(2)}, u32[]{:S(2)}) collective-permute-start(bf16[512,256]{1,0:T(8,128)(2,1)S(1)} %pad_maximum_fusion.8), channel_id=1, source_target_pairs={{32,0},{97,1},{34,2},{99,3},{36,4},{101,5},{38,6},{103,7},{40,8},{... | collective-permute-start | bytes 786440 | tf_op jit(solution)/shard_map/ppermute | solution.py:58
  15.0 5.8 %collective-permute-start.2 = (bf16[512,256]{1,0:T(8,128)(2,1)S(1)}, bf16[512,256]{1,0:T(8,128)(2,1)S(1)}, u32[]{:S(2)}, u32[]{:S(2)}) collective-permute-start(bf16[512,256]{1,0:T(8,128)(2,1)S(1)} %pad_maximum_fusion.8), channel_id=1, source_target_pairs={{5,0},{28,1},{7,2},{30,3},{9,4},{0,5},{11,6},{2,7},{13,8},{4,9},{1... | collective-permute-start | bytes 786440 | tf_op jit(solution)/shard_map/ppermute | solution.py:58
  20.9 10.5 %collective-permute-start.5 = (bf16[1024,256]{1,0:T(8,128)(2,1)S(1)}, bf16[1024,256]{1,0:T(8,128)(2,1)S(1)}, u32[]{:S(2)}, u32[]{:S(2)}) collective-permute-start(bf16[1024,256]{1,0:T(8,128)(2,1)S(1)} %get-tuple-element.55), channel_id=1, source_target_pairs={{96,0},{33,1},{98,2},{35,3},{100,4},{37,5},{102,6},{39,7},{104,8},... | collective-permute-start | bytes 1572872 | tf_op jit(solution)/shard_map/ppermute | solution.py:58
  23.2 10.7 %collective-permute-start.4 = (bf16[1024,256]{1,0:T(8,128)(2,1)S(1)}, bf16[1024,256]{1,0:T(8,128)(2,1)S(1)}, u32[]{:S(2)}, u32[]{:S(2)}) collective-permute-start(bf16[1024,256]{1,0:T(8,128)(2,1)S(1)} %get-tuple-element.56), channel_id=1, source_target_pairs={{159,0},{6,1},{29,2},{132,3},{131,4},{10,5},{1,6},{136,7},{135,8},... | collective-permute-start | bytes 1572872 | tf_op jit(solution)/shard_map/ppermute | solution.py:58
  34.0 12.9 %collective-permute-start.6 = (bf16[1792,256]{1,0:T(8,128)(2,1)S(1)}, bf16[1792,256]{1,0:T(8,128)(2,1)S(1)}, u32[]{:S(2)}, u32[]{:S(2)}) collective-permute-start(bf16[1792,256]{1,0:T(8,128)(2,1)S(1)} %pad_maximum_fusion.3), channel_id=1, source_target_pairs={{5,0},{28,1},{7,2},{30,3},{9,4},{0,5},{11,6},{2,7},{13,8},{4,9},{1... | collective-permute-start | bytes 2752520 | tf_op jit(solution)/shard_map/ppermute | solution.py:58
  35.5 7.9 %collective-permute-start.7 = (bf16[768,256]{1,0:T(8,128)(2,1)S(1)}, bf16[768,256]{1,0:T(8,128)(2,1)S(1)}, u32[]{:S(2)}, u32[]{:S(2)}) collective-permute-start(bf16[768,256]{1,0:T(8,128)(2,1)S(1)} %pad_maximum_fusion.7), channel_id=1, source_target_pairs={{32,0},{97,1},{34,2},{99,3},{36,4},{101,5},{38,6},{103,7},{40,8},{... | collective-permute-start | bytes 1179656 | tf_op jit(solution)/shard_map/ppermute | solution.py:58
  47.1 19.2 %collective-permute-start.8 = (bf16[2560,256]{1,0:T(8,128)(2,1)S(1)}, bf16[2560,256]{1,0:T(8,128)(2,1)S(1)}, u32[]{:S(2)}, u32[]{:S(2)}) collective-permute-start(bf16[2560,256]{1,0:T(8,128)(2,1)S(1)} %slice_dynamic-update-slice_fusion.1), channel_id=1, source_target_pairs={{159,0},{6,1},{29,2},{132,3},{131,4},{10,5},{1,6},{136,7},{135,8},... | collective-permute-start | bytes 3932168 | tf_op jit(solution)/shard_map/ppermute | solution.py:58
  48.7 16.0 %collective-permute-start.9 = (bf16[2048,256]{1,0:T(8,128)(2,1)S(1)}, bf16[2048,256]{1,0:T(8,128)(2,1)S(1)}, u32[]{:S(2)}, u32[]{:S(2)}) collective-permute-start(bf16[2048,256]{1,0:T(8,128)(2,1)S(1)} %get-tuple-element.32), channel_id=1, source_target_pairs={{96,0},{33,1},{98,2},{35,3},{100,4},{37,5},{102,6},{39,7},{104,8},... | collective-permute-start | bytes 3145736 | tf_op jit(solution)/shard_map/ppermute | solution.py:58
  66.4 12.1 %collective-permute-start.11 = (bf16[1536,256]{1,0:T(8,128)(2,1)S(1)}, bf16[1536,256]{1,0:T(8,128)(2,1)S(1)}, u32[]{:S(2)}, u32[]{:S(2)}) collective-permute-start(bf16[1536,256]{1,0:T(8,128)(2,1)S(1)} %constant_dynamic-update-slice_fusion.13), channel_id=1, source_target_pairs={{32,0},{97,1},{34,2},{99,3},{36,4},{101,5},{38,6},{103,7},{40,8},{... | collective-permute-start | bytes 2359304 | tf_op jit(solution)/shard_map/ppermute | solution.py:58
  67.2 11.4 %collective-permute-start.10 = (bf16[1536,256]{1,0:T(8,128)(2,1)S(1)}, bf16[1536,256]{1,0:T(8,128)(2,1)S(1)}, u32[]{:S(2)}, u32[]{:S(2)}) collective-permute-start(bf16[1536,256]{1,0:T(8,128)(2,1)S(1)} %slice.118), channel_id=1, source_target_pairs={{5,0},{28,1},{7,2},{30,3},{9,4},{0,5},{11,6},{2,7},{13,8},{4,9},{1... | collective-permute-start | bytes 2359304 | tf_op jit(solution)/shard_map/ppermute | solution.py:58
  78.6 13.8 %collective-permute-start.12 = (bf16[1536,256]{1,0:T(8,128)(2,1)S(1)}, bf16[1536,256]{1,0:T(8,128)(2,1)S(1)}, u32[]{:S(2)}, u32[]{:S(2)}) collective-permute-start(bf16[1536,256]{1,0:T(8,128)(2,1)S(1)} %collective-permute-done.10), channel_id=1, source_target_pairs={{159,0},{6,1},{29,2},{132,3},{131,4},{10,5},{1,6},{136,7},{135,8},... | collective-permute-start | bytes 2359304 | tf_op jit(solution)/shard_map/ppermute | solution.py:58
  82.0 10.4 %collective-permute-start.13 = (bf16[1024,256]{1,0:T(8,128)(2,1)S(1)}, bf16[1024,256]{1,0:T(8,128)(2,1)S(1)}, u32[]{:S(2)}, u32[]{:S(2)}) collective-permute-start(bf16[1024,256]{1,0:T(8,128)(2,1)S(1)} %pad_maximum_fusion.6), channel_id=1, source_target_pairs={{96,0},{33,1},{98,2},{35,3},{100,4},{37,5},{102,6},{39,7},{104,8},... | collective-permute-start | bytes 1572872 | tf_op jit(solution)/shard_map/ppermute | solution.py:58
  92.5 8.9 %copy-start.2 = (s32[256]{0:T(256)S(1)}, s32[256]{0:T(256)}, u32[]{:S(2)}) copy-start(s32[256]{0:T(256)} %param.9) | copy-start | bytes 3076
  94.2 7.0 %collective-permute-start.14 = (f32[256,256]{1,0:T(8,128)S(1)}, f32[256,256]{1,0:T(8,128)S(1)}, u32[]{:S(2)}, u32[]{:S(2)}) collective-permute-start(f32[256,256]{1,0:T(8,128)S(1)} %slice_bitcast_fusion.1), channel_id=1, source_target_pairs={{0,1},{1,0},{2,3},{3,2},{4,5},{5,4},{6,7},{7,6},{8,9},{9,8},{10,11... | collective-permute-start | bytes 786440 | tf_op jit(solution)/shard_map/ppermute | solution.py:256
  101.3 8.7 %collective-permute-start.17 = (f32[256,256]{1,0:T(8,128)S(1)}, f32[256,256]{1,0:T(8,128)S(1)}, u32[]{:S(2)}, u32[]{:S(2)}) collective-permute-start(f32[256,256]{1,0:T(8,128)S(1)} %fusion.7), channel_id=1, source_target_pairs={{0,2},{1,3},{2,0},{3,1},{4,6},{5,7},{6,4},{7,5},{8,10},{9,11},{10,... | collective-permute-start | bytes 786440 | tf_op jit(solution)/shard_map/ppermute | solution.py:250
  103.1 7.2 %collective-permute-start.15 = (f32[128,256]{1,0:T(8,128)S(1)}, f32[128,256]{1,0:T(8,128)S(1)}, u32[]{:S(2)}, u32[]{:S(2)}) collective-permute-start(f32[128,256]{1,0:T(8,128)S(1)} %get-tuple-element.46), channel_id=1, source_target_pairs={{0,1},{1,0},{2,3},{3,2},{4,5},{5,4},{6,7},{7,6},{8,9},{9,8},{10,11... | collective-permute-start | bytes 393224 | tf_op jit(solution)/shard_map/ppermute | solution.py:256
  103.5 6.7 %collective-permute-start.16 = (f32[128,256]{1,0:T(8,128)S(1)}, f32[128,256]{1,0:T(8,128)S(1)}, u32[]{:S(2)}, u32[]{:S(2)}) collective-permute-start(f32[128,256]{1,0:T(8,128)S(1)} %get-tuple-element.47), channel_id=1, source_target_pairs={{0,1},{1,0},{2,3},{3,2},{4,5},{5,4},{6,7},{7,6},{8,9},{9,8},{10,11... | collective-permute-start | bytes 393224 | tf_op jit(solution)/shard_map/ppermute | solution.py:256

commit v5 on v4

--- a/solution.py
+++ b/solution.py
@@ -19,7 +19,7 @@
 PHASES = 5
 
 HOME = (0, 1, 2, -1)
-PIECE = (1, 2, 0, 3)
+PIECE = (0, 2, 1, 3)
 
 
 def member(h, y, z, q):

time: 111 us -> 111 us (level)
  waiting for transfers between devices: 56.6 us -> 51.6 us
  starting transfers between devices: 28.2 us -> 32.7 us
    ppermute x14, starting transfers between devices: 21.7 us -> 27.1 us  [moved(): lax.ppermute(self.rows, AXES, [(sender(*d), member(*d)) for d in here])]
    ppermute x14, waiting for transfers between devices: 49.2 us -> 44.2 us  [moved(): lax.ppermute(self.rows, AXES, [(sender(*d), member(*d)) for d in here])]
where the time goes in v5:
time: 111 us
  waiting for transfers between devices  51.6 us (46%)
  starting transfers between devices  32.7 us (29%)
  Pallas kernels  18.2 us (16%)
  other arithmetic  5.43 us (5%)
  matrix products  1.3 us (1%)
    ppermute x14, waiting for transfers between devices, moved(): lax.ppermute(self.rows, AXES, [(sender(*d), member(*d)) for d in here])  44.2 us
    ppermute x14, starting transfers between devices, moved(): lax.ppermute(self.rows, AXES, [(sender(*d), member(*d)) for d in here])  27.1 us
    pallas_call x6, Pallas kernels, products(): pl.pallas_call(functools.partial(product_kernel, buckets, first_bucket, m...  12.3 us
    ppermute x1, waiting for transfers between devices, add(): theirs = lax.ppermute(theirs, AXES, [(i, i ^ 2) for i in devices])  6.25 us
    pallas_call x1, Pallas kernels, slot_lists(): pl.pallas_call(list_kernel, out_shape=(jax.ShapeDtypeStruct((8 * PHASES +...  5.95 us
    ppermute x3, starting transfers between devices, to_owner_core(): got = [lax.ppermute(x, AXES, [(i, i ^ 1) for i in devices]) for x in sent]  5.44 us
  transfers between devices with their start and end apart: 18, of which 15 were waited for; matrix products, arithmetic and copies ran while one was open for 4% of the time, Pallas kernels for 15%

profile of v5, /device:TPU:6, one launch (start us, length us, event | category | flops | bytes accessed | tf_op | source)
XLA Modules:
  0.0 110.6 jit_solution(16158163059967772927)
XLA Ops:
  1.7 1.3 %collective-permute-start.1 = (bf16[256,256]{1,0:T(8,128)(2,1)S(1)}, bf16[256,256]{1,0:T(8,128)(2,1)S(1)}, u32[]{:S(2)}, u32[]{:S(2)}) collective-permute-start(bf16[256,256]{1,0:T(8,128)(2,1)S(1)} %multiply_convert_fusion), channel_id=1, source_target_pairs={{128,0},{158,1},{153,2},{135,3},{132,4},{130,5},{157,6},{139,7},{1... | collective-permute-start | bytes 393224 | tf_op jit(solution)/shard_map/ppermute | solution.py:58
  3.1 5.8 %collective-permute-start = (bf16[256,256]{1,0:T(8,128)(2,1)S(1)}, bf16[256,256]{1,0:T(8,128)(2,1)S(1)}, u32[]{:S(2)}, u32[]{:S(2)}) collective-permute-start(bf16[256,256]{1,0:T(8,128)(2,1)S(1)} %multiply_convert_fusion), channel_id=1, source_target_pairs={{0,0},{30,1},{25,2},{7,3},{4,4},{2,5},{29,6},{11,7},{8,8},{6,9},{1... | collective-permute-start | bytes 393224 | tf_op jit(solution)/shard_map/ppermute | solution.py:58
  9.8 1.2 %select_reduce_fusion = s32[16,22]{0,1:T(8,128)S(1)} fusion(s32[128]{0:T(128)} %constant.11.clone, s32[16,22]{0,1:T(8,128)S(1)} %copy.9), kind=kLoop, calls=%fused_computation.29 | loop fusion | flops 134816 | bytes 3328 | tf_op jit(solution)/shard_map/reduce_sum | solution.py:229
  13.1 1.7 %collective-permute-start.3 = (bf16[512,256]{1,0:T(8,128)(2,1)S(1)}, bf16[512,256]{1,0:T(8,128)(2,1)S(1)}, u32[]{:S(2)}, u32[]{:S(2)}) collective-permute-start(bf16[512,256]{1,0:T(8,128)(2,1)S(1)} %pad_maximum_fusion.8), channel_id=1, source_target_pairs={{32,0},{97,1},{34,2},{99,3},{36,4},{101,5},{38,6},{103,7},{40,8},{... | collective-permute-start | bytes 786440 | tf_op jit(solution)/shard_map/ppermute | solution.py:58
  14.7 2.5 %collective-permute-start.2 = (bf16[512,256]{1,0:T(8,128)(2,1)S(1)}, bf16[512,256]{1,0:T(8,128)(2,1)S(1)}, u32[]{:S(2)}, u32[]{:S(2)}) collective-permute-start(bf16[512,256]{1,0:T(8,128)(2,1)S(1)} %pad_maximum_fusion.8), channel_id=1, source_target_pairs={{5,0},{28,1},{7,2},{30,3},{9,4},{0,5},{11,6},{2,7},{13,8},{4,9},{1... | collective-permute-start | bytes 786440 | tf_op jit(solution)/shard_map/ppermute | solution.py:58
  17.2 2.3 %collective-permute-done.3 = bf16[512,256]{1,0:T(8,128)(2,1)S(1)} collective-permute-done((bf16[512,256]{1,0:T(8,128)(2,1)S(1)}, bf16[512,256]{1,0:T(8,128)(2,1)S(1)}, u32[]{:S(2)}, u32[]{:S(2)}) %collective-permute-start.3) | collective-permute-done | bytes 262176 | tf_op jit(solution)/shard_map/ppermute | solution.py:58
  19.5 1.8 %collective-permute-done.2 = bf16[512,256]{1,0:T(8,128)(2,1)S(1)} collective-permute-done((bf16[512,256]{1,0:T(8,128)(2,1)S(1)}, bf16[512,256]{1,0:T(8,128)(2,1)S(1)}, u32[]{:S(2)}, u32[]{:S(2)}) %collective-permute-start.2) | collective-permute-done | bytes 262176 | tf_op jit(solution)/shard_map/ppermute | solution.py:58
  21.3 1.5 %collective-permute-start.5 = (bf16[1024,256]{1,0:T(8,128)(2,1)S(1)}, bf16[1024,256]{1,0:T(8,128)(2,1)S(1)}, u32[]{:S(2)}, u32[]{:S(2)}) collective-permute-start(bf16[1024,256]{1,0:T(8,128)(2,1)S(1)} %get-tuple-element.55), channel_id=1, source_target_pairs={{96,0},{33,1},{98,2},{35,3},{100,4},{37,5},{102,6},{39,7},{104,8},... | collective-permute-start | bytes 1572872 | tf_op jit(solution)/shard_map/ppermute | solution.py:58
  22.9 1.3 %collective-permute-start.4 = (bf16[1024,256]{1,0:T(8,128)(2,1)S(1)}, bf16[1024,256]{1,0:T(8,128)(2,1)S(1)}, u32[]{:S(2)}, u32[]{:S(2)}) collective-permute-start(bf16[1024,256]{1,0:T(8,128)(2,1)S(1)} %get-tuple-element.56), channel_id=1, source_target_pairs={{159,0},{6,1},{29,2},{132,3},{131,4},{10,5},{1,6},{136,7},{135,8},... | collective-permute-start | bytes 1572872 | tf_op jit(solution)/shard_map/ppermute | solution.py:58
  24.2 6.0 %shard_map.82 = (s32[41,128]{1,0:T(8,128)S(1)}, s32[40]{0:T(128)S(1)}, bf16[352,128,128]{2,1,0:T(8,128)(2,1)S(1)}) custom-call(s32[16]{0:T(128)S(1)} %bitcast.69, s32[16,22]{1,0:T(8,128)S(1)} %fusion.19.coded, bf16[352,128,128]{2,1,0:T(8,128)(2,1)} %bitcast.70), custom_call_target="tpu_custom_call" | custom-call | bytes 23000000 | tf_op jit(solution)/shard_map/pallas_call | solution.py:146
  30.3 1.5 %collective-permute-done.5 = bf16[1024,256]{1,0:T(8,128)(2,1)S(1)} collective-permute-done((bf16[1024,256]{1,0:T(8,128)(2,1)S(1)}, bf16[1024,256]{1,0:T(8,128)(2,1)S(1)}, u32[]{:S(2)}, u32[]{:S(2)}) %collective-permute-start.5) | collective-permute-done | bytes 524320 | tf_op jit(solution)/shard_map/ppermute | solution.py:58
  31.8 1.7 %collective-permute-done.4 = bf16[1024,256]{1,0:T(8,128)(2,1)S(1)} collective-permute-done((bf16[1024,256]{1,0:T(8,128)(2,1)S(1)}, bf16[1024,256]{1,0:T(8,128)(2,1)S(1)}, u32[]{:S(2)}, u32[]{:S(2)}) %collective-permute-start.4) | collective-permute-done | bytes 524320 | tf_op jit(solution)/shard_map/ppermute | solution.py:58
  34.4 1.5 %collective-permute-start.7 = (bf16[768,256]{1,0:T(8,128)(2,1)S(1)}, bf16[768,256]{1,0:T(8,128)(2,1)S(1)}, u32[]{:S(2)}, u32[]{:S(2)}) collective-permute-start(bf16[768,256]{1,0:T(8,128)(2,1)S(1)} %pad_maximum_fusion.7), channel_id=1, source_target_pairs={{32,0},{97,1},{34,2},{99,3},{36,4},{101,5},{38,6},{103,7},{40,8},{... | collective-permute-start | bytes 1179656 | tf_op jit(solution)/shard_map/ppermute | solution.py:58
  36.1 2.3 %shard_map.83.refs_0_ = f32[4,256,256]{2,1,0:T(8,128)S(1)} custom-call(s32[41,128]{1,0:T(8,128)S(1)} %get-tuple-element.25.lists, s32[40]{0:T(128)S(1)} %get-tuple-element.26.counts, bf16[352,128,128]{2,1,0:T(8,128)(2,1)S(1)} %get-tuple-element.27.tiles, bf16[29,128,256]{2,1,0:T(8,128)(2,1)S(1)} %bitcast.68), custom_call_target="tpu_custom_call" | custom-call | flops 176400000 | bytes 3150000 | tf_op jit(solution)/shard_map/pallas_call | solution.py:194
  38.4 3.9 %collective-permute-done.7 = bf16[768,256]{1,0:T(8,128)(2,1)S(1)} collective-permute-done((bf16[768,256]{1,0:T(8,128)(2,1)S(1)}, bf16[768,256]{1,0:T(8,128)(2,1)S(1)}, u32[]{:S(2)}, u32[]{:S(2)}) %collective-permute-start.7) | collective-permute-done | bytes 393248 | tf_op jit(solution)/shard_map/ppermute | solution.py:58
  42.3 4.2 %collective-permute-done.6 = bf16[1792,256]{1,0:T(8,128)(2,1)S(1)} collective-permute-done((bf16[1792,256]{1,0:T(8,128)(2,1)S(1)}, bf16[1792,256]{1,0:T(8,128)(2,1)S(1)}, u32[]{:S(2)}, u32[]{:S(2)}) %collective-permute-start.6) | collective-permute-done | bytes 917536 | tf_op jit(solution)/shard_map/ppermute | solution.py:58
  46.8 1.7 %collective-permute-start.8 = (bf16[2560,256]{1,0:T(8,128)(2,1)S(1)}, bf16[2560,256]{1,0:T(8,128)(2,1)S(1)}, u32[]{:S(2)}, u32[]{:S(2)}) collective-permute-start(bf16[2560,256]{1,0:T(8,128)(2,1)S(1)} %slice_dynamic-update-slice_fusion.1), channel_id=1, source_target_pairs={{159,0},{6,1},{29,2},{132,3},{131,4},{10,5},{1,6},{136,7},{135,8},... | collective-permute-start | bytes 3932168 | tf_op jit(solution)/shard_map/ppermute | solution.py:58
  48.5 2.2 %collective-permute-start.9 = (bf16[2048,256]{1,0:T(8,128)(2,1)S(1)}, bf16[2048,256]{1,0:T(8,128)(2,1)S(1)}, u32[]{:S(2)}, u32[]{:S(2)}) collective-permute-start(bf16[2048,256]{1,0:T(8,128)(2,1)S(1)} %get-tuple-element.32), channel_id=1, source_target_pairs={{96,0},{33,1},{98,2},{35,3},{100,4},{37,5},{102,6},{39,7},{104,8},... | collective-permute-start | bytes 3145736 | tf_op jit(solution)/shard_map/ppermute | solution.py:58
  50.8 2.0 %shard_map.84.refs_0_ = f32[4,256,256]{2,1,0:T(8,128)S(1)} custom-call(s32[41,128]{1,0:T(8,128)S(1)} %get-tuple-element.25.lists, s32[40]{0:T(128)S(1)} %get-tuple-element.26.counts, bf16[352,128,128]{2,1,0:T(8,128)(2,1)S(1)} %get-tuple-element.27.tiles, bf16[21,128,256]{2,1,0:T(8,128)(2,1)S(1)} %bitcast.66, f32[4,256,256]{2,1,0:T(8,128)S(1)} %shard_map.83.refs_0_), custom_call_target="tpu_custom_call" | custom-call | flops 126000000 | bytes 2250000 | tf_op jit(solution)/shard_map/pallas_call | solution.py:194
  52.9 11.6 %collective-permute-done.9 = bf16[2048,256]{1,0:T(8,128)(2,1)S(1)} collective-permute-done((bf16[2048,256]{1,0:T(8,128)(2,1)S(1)}, bf16[2048,256]{1,0:T(8,128)(2,1)S(1)}, u32[]{:S(2)}, u32[]{:S(2)}) %collective-permute-start.9) | collective-permute-done | bytes 1048608 | tf_op jit(solution)/shard_map/ppermute | solution.py:58
  64.5 1.5 %collective-permute-done.8 = bf16[2560,256]{1,0:T(8,128)(2,1)S(1)} collective-permute-done((bf16[2560,256]{1,0:T(8,128)(2,1)S(1)}, bf16[2560,256]{1,0:T(8,128)(2,1)S(1)}, u32[]{:S(2)}, u32[]{:S(2)}) %collective-permute-start.8) | collective-permute-done | bytes 1310752 | tf_op jit(solution)/shard_map/ppermute | solution.py:58
  66.9 2.7 %collective-permute-start.10 = (bf16[1536,256]{1,0:T(8,128)(2,1)S(1)}, bf16[1536,256]{1,0:T(8,128)(2,1)S(1)}, u32[]{:S(2)}, u32[]{:S(2)}) collective-permute-start(bf16[1536,256]{1,0:T(8,128)(2,1)S(1)} %slice.118), channel_id=1, source_target_pairs={{5,0},{28,1},{7,2},{30,3},{9,4},{0,5},{11,6},{2,7},{13,8},{4,9},{1... | collective-permute-start | bytes 2359304 | tf_op jit(solution)/shard_map/ppermute | solution.py:58
  69.7 2.3 %shard_map.85.refs_0_ = f32[4,256,256]{2,1,0:T(8,128)S(1)} custom-call(s32[41,128]{1,0:T(8,128)S(1)} %get-tuple-element.25.lists, s32[40]{0:T(128)S(1)} %get-tuple-element.26.counts, bf16[352,128,128]{2,1,0:T(8,128)(2,1)S(1)} %get-tuple-element.27.tiles, bf16[21,128,256]{2,1,0:T(8,128)(2,1)S(1)} %bitcast.67, f32[4,256,256]{2,1,0:T(8,128)S(1)} %shard_map.84.refs_0_), custom_call_target="tpu_custom_call" | custom-call | flops 126000000 | bytes 2250000 | tf_op jit(solution)/shard_map/pallas_call | solution.py:194
  72.0 6.2 %collective-permute-done.11 = bf16[1536,256]{1,0:T(8,128)(2,1)S(1)} collective-permute-done((bf16[1536,256]{1,0:T(8,128)(2,1)S(1)}, bf16[1536,256]{1,0:T(8,128)(2,1)S(1)}, u32[]{:S(2)}, u32[]{:S(2)}) %collective-permute-start.11) | collective-permute-done | bytes 786464 | tf_op jit(solution)/shard_map/ppermute | solution.py:58
  79.3 2.2 %collective-permute-start.12 = (bf16[1536,256]{1,0:T(8,128)(2,1)S(1)}, bf16[1536,256]{1,0:T(8,128)(2,1)S(1)}, u32[]{:S(2)}, u32[]{:S(2)}) collective-permute-start(bf16[1536,256]{1,0:T(8,128)(2,1)S(1)} %collective-permute-done.10), channel_id=1, source_target_pairs={{159,0},{6,1},{29,2},{132,3},{131,4},{10,5},{1,6},{136,7},{135,8},... | collective-permute-start | bytes 2359304 | tf_op jit(solution)/shard_map/ppermute | solution.py:58
  83.1 2.3 %shard_map.86 = f32[4,256,256]{2,1,0:T(8,128)S(1)} custom-call(s32[41,128]{1,0:T(8,128)S(1)} %get-tuple-element.25.lists, s32[40]{0:T(128)S(1)} %get-tuple-element.26.counts, bf16[352,128,128]{2,1,0:T(8,128)(2,1)S(1)} %get-tuple-element.27.tiles, bf16[41,128,256]{2,1,0:T(8,128)(2,1)S(1)} %bitcast.65, f32[4,256,256]{2,1,0:T(8,128)S(1)} %shard_map.85.refs_0_), custom_call_target="tpu_custom_call" | custom-call | flops 252000000 | bytes 4500000 | tf_op jit(solution)/shard_map/pallas_call | solution.py:194
  85.4 6.4 %collective-permute-done.13 = bf16[1024,256]{1,0:T(8,128)(2,1)S(1)} collective-permute-done((bf16[1024,256]{1,0:T(8,128)(2,1)S(1)}, bf16[1024,256]{1,0:T(8,128)(2,1)S(1)}, u32[]{:S(2)}, u32[]{:S(2)}) %collective-permute-start.13) | collective-permute-done | bytes 524320 | tf_op jit(solution)/shard_map/ppermute | solution.py:58
  92.9 1.6 %shard_map.87 = f32[2,256,256]{2,1,0:T(8,128)S(1)} custom-call(s32[41,128]{1,0:T(8,128)S(1)} %get-tuple-element.25.lists, s32[40]{0:T(128)S(1)} %get-tuple-element.26.counts, bf16[352,128,128]{2,1,0:T(8,128)(2,1)S(1)} %get-tuple-element.27.tiles, bf16[21,128,256]{2,1,0:T(8,128)(2,1)S(1)} %bitcast.63, f32[2,256,256]{2,1,0:T(8,128)S(1)} %slice.123.refs_0_), custom_call_target="tpu_custom_call" | custom-call | flops 260400000 | bytes 4650000 | tf_op jit(solution)/shard_map/pallas_call | solution.py:194
  94.5 4.8 %collective-permute-start.14 = (f32[256,256]{1,0:T(8,128)S(1)}, f32[256,256]{1,0:T(8,128)S(1)}, u32[]{:S(2)}, u32[]{:S(2)}) collective-permute-start(f32[256,256]{1,0:T(8,128)S(1)} %slice_bitcast_fusion.1), channel_id=1, source_target_pairs={{0,1},{1,0},{2,3},{3,2},{4,5},{5,4},{6,7},{7,6},{8,9},{9,8},{10,11... | collective-permute-start | bytes 786440 | tf_op jit(solution)/shard_map/ppermute | solution.py:256
  99.4 1.2 %collective-permute-done.14 = f32[256,256]{1,0:T(8,128)S(1)} collective-permute-done((f32[256,256]{1,0:T(8,128)S(1)}, f32[256,256]{1,0:T(8,128)S(1)}, u32[]{:S(2)}, u32[]{:S(2)}) %collective-permute-start.14) | collective-permute-done | bytes 262176 | tf_op jit(solution)/shard_map/ppermute | solution.py:256
  100.8 1.6 %shard_map.88 = f32[2,256,256]{2,1,0:T(8,128)S(1)} custom-call(s32[41,128]{1,0:T(8,128)S(1)} %get-tuple-element.25.lists, s32[40]{0:T(128)S(1)} %get-tuple-element.26.counts, bf16[352,128,128]{2,1,0:T(8,128)(2,1)S(1)} %get-tuple-element.27.tiles, bf16[21,128,256]{2,1,0:T(8,128)(2,1)S(1)} %bitcast.64, f32[2,256,256]{2,1,0:T(8,128)S(1)} %slice.106.refs_0_), custom_call_target="tpu_custom_call" | custom-call | flops 260400000 | bytes 4650000 | tf_op jit(solution)/shard_map/pallas_call | solution.py:194
  103.0 6.3 %collective-permute-done.17 = f32[256,256]{1,0:T(8,128)S(1)} collective-permute-done((f32[256,256]{1,0:T(8,128)S(1)}, f32[256,256]{1,0:T(8,128)S(1)}, u32[]{:S(2)}, u32[]{:S(2)}) %collective-permute-start.17) | collective-permute-done | bytes 262176 | tf_op jit(solution)/shard_map/ppermute | solution.py:250
  (72 shorter events, 12.8 us)
Async XLA Ops:
  0.0 109.3 %copy-start = (bf16[256,256]{1,0:T(8,128)(2,1)S(1)}, bf16[256,256]{1,0:T(8,128)(2,1)}, u32[]{:S(2)}) copy-start(bf16[256,256]{1,0:T(8,128)(2,1)} %param.14) | copy-start | bytes 393220
  1.7 10.1 %collective-permute-start.1 = (bf16[256,256]{1,0:T(8,128)(2,1)S(1)}, bf16[256,256]{1,0:T(8,128)(2,1)S(1)}, u32[]{:S(2)}, u32[]{:S(2)}) collective-permute-start(bf16[256,256]{1,0:T(8,128)(2,1)S(1)} %multiply_convert_fusion), channel_id=1, source_target_pairs={{128,0},{158,1},{153,2},{135,3},{132,4},{130,5},{157,6},{139,7},{1... | collective-permute-start | bytes 393224 | tf_op jit(solution)/shard_map/ppermute | solution.py:58
  3.1 9.9 %collective-permute-start = (bf16[256,256]{1,0:T(8,128)(2,1)S(1)}, bf16[256,256]{1,0:T(8,128)(2,1)S(1)}, u32[]{:S(2)}, u32[]{:S(2)}) collective-permute-start(bf16[256,256]{1,0:T(8,128)(2,1)S(1)} %multiply_convert_fusion), channel_id=1, source_target_pairs={{0,0},{30,1},{25,2},{7,3},{4,4},{2,5},{29,6},{11,7},{8,8},{6,9},{1... | collective-permute-start | bytes 393224 | tf_op jit(solution)/shard_map/ppermute | solution.py:58
  11.0 13.2 %copy-start.1 = (s32[1,1,16]{2,1,0:T(1,128)S(1)}, s32[1,1,16]{2,1,0:T(1,128)}, u32[]{:S(2)}) copy-start(s32[1,1,16]{2,1,0:T(1,128)} %param.13) | copy-start | bytes 196
  13.1 6.5 %collective-permute-start.3 = (bf16[512,256]{1,0:T(8,128)(2,1)S(1)}, bf16[512,256]{1,0:T(8,128)(2,1)S(1)}, u32[]{:S(2)}, u32[]{:S(2)}) collective-permute-start(bf16[512,256]{1,0:T(8,128)(2,1)S(1)} %pad_maximum_fusion.8), channel_id=1, source_target_pairs={{32,0},{97,1},{34,2},{99,3},{36,4},{101,5},{38,6},{103,7},{40,8},{... | collective-permute-start | bytes 786440 | tf_op jit(solution)/shard_map/ppermute | solution.py:58
  14.7 6.6 %collective-permute-start.2 = (bf16[512,256]{1,0:T(8,128)(2,1)S(1)}, bf16[512,256]{1,0:T(8,128)(2,1)S(1)}, u32[]{:S(2)}, u32[]{:S(2)}) collective-permute-start(bf16[512,256]{1,0:T(8,128)(2,1)S(1)} %pad_maximum_fusion.8), channel_id=1, source_target_pairs={{5,0},{28,1},{7,2},{30,3},{9,4},{0,5},{11,6},{2,7},{13,8},{4,9},{1... | collective-permute-start | bytes 786440 | tf_op jit(solution)/shard_map/ppermute | solution.py:58
  21.3 10.5 %collective-permute-start.5 = (bf16[1024,256]{1,0:T(8,128)(2,1)S(1)}, bf16[1024,256]{1,0:T(8,128)(2,1)S(1)}, u32[]{:S(2)}, u32[]{:S(2)}) collective-permute-start(bf16[1024,256]{1,0:T(8,128)(2,1)S(1)} %get-tuple-element.55), channel_id=1, source_target_pairs={{96,0},{33,1},{98,2},{35,3},{100,4},{37,5},{102,6},{39,7},{104,8},... | collective-permute-start | bytes 1572872 | tf_op jit(solution)/shard_map/ppermute | solution.py:58
  22.9 10.7 %collective-permute-start.4 = (bf16[1024,256]{1,0:T(8,128)(2,1)S(1)}, bf16[1024,256]{1,0:T(8,128)(2,1)S(1)}, u32[]{:S(2)}, u32[]{:S(2)}) collective-permute-start(bf16[1024,256]{1,0:T(8,128)(2,1)S(1)} %get-tuple-element.56), channel_id=1, source_target_pairs={{159,0},{6,1},{29,2},{132,3},{131,4},{10,5},{1,6},{136,7},{135,8},... | collective-permute-start | bytes 1572872 | tf_op jit(solution)/shard_map/ppermute | solution.py:58
  33.7 12.9 %collective-permute-start.6 = (bf16[1792,256]{1,0:T(8,128)(2,1)S(1)}, bf16[1792,256]{1,0:T(8,128)(2,1)S(1)}, u32[]{:S(2)}, u32[]{:S(2)}) collective-permute-start(bf16[1792,256]{1,0:T(8,128)(2,1)S(1)} %pad_maximum_fusion.3), channel_id=1, source_target_pairs={{5,0},{28,1},{7,2},{30,3},{9,4},{0,5},{11,6},{2,7},{13,8},{4,9},{1... | collective-permute-start | bytes 2752520 | tf_op jit(solution)/shard_map/ppermute | solution.py:58
  34.4 7.9 %collective-permute-start.7 = (bf16[768,256]{1,0:T(8,128)(2,1)S(1)}, bf16[768,256]{1,0:T(8,128)(2,1)S(1)}, u32[]{:S(2)}, u32[]{:S(2)}) collective-permute-start(bf16[768,256]{1,0:T(8,128)(2,1)S(1)} %pad_maximum_fusion.7), channel_id=1, source_target_pairs={{32,0},{97,1},{34,2},{99,3},{36,4},{101,5},{38,6},{103,7},{40,8},{... | collective-permute-start | bytes 1179656 | tf_op jit(solution)/shard_map/ppermute | solution.py:58
  46.8 19.2 %collective-permute-start.8 = (bf16[2560,256]{1,0:T(8,128)(2,1)S(1)}, bf16[2560,256]{1,0:T(8,128)(2,1)S(1)}, u32[]{:S(2)}, u32[]{:S(2)}) collective-permute-start(bf16[2560,256]{1,0:T(8,128)(2,1)S(1)} %slice_dynamic-update-slice_fusion.1), channel_id=1, source_target_pairs={{159,0},{6,1},{29,2},{132,3},{131,4},{10,5},{1,6},{136,7},{135,8},... | collective-permute-start | bytes 3932168 | tf_op jit(solution)/shard_map/ppermute | solution.py:58
  48.5 16.0 %collective-permute-start.9 = (bf16[2048,256]{1,0:T(8,128)(2,1)S(1)}, bf16[2048,256]{1,0:T(8,128)(2,1)S(1)}, u32[]{:S(2)}, u32[]{:S(2)}) collective-permute-start(bf16[2048,256]{1,0:T(8,128)(2,1)S(1)} %get-tuple-element.32), channel_id=1, source_target_pairs={{96,0},{33,1},{98,2},{35,3},{100,4},{37,5},{102,6},{39,7},{104,8},... | collective-permute-start | bytes 3145736 | tf_op jit(solution)/shard_map/ppermute | solution.py:58
  66.1 12.1 %collective-permute-start.11 = (bf16[1536,256]{1,0:T(8,128)(2,1)S(1)}, bf16[1536,256]{1,0:T(8,128)(2,1)S(1)}, u32[]{:S(2)}, u32[]{:S(2)}) collective-permute-start(bf16[1536,256]{1,0:T(8,128)(2,1)S(1)} %constant_dynamic-update-slice_fusion.13), channel_id=1, source_target_pairs={{32,0},{97,1},{34,2},{99,3},{36,4},{101,5},{38,6},{103,7},{40,8},{... | collective-permute-start | bytes 2359304 | tf_op jit(solution)/shard_map/ppermute | solution.py:58
  66.9 12.4 %collective-permute-start.10 = (bf16[1536,256]{1,0:T(8,128)(2,1)S(1)}, bf16[1536,256]{1,0:T(8,128)(2,1)S(1)}, u32[]{:S(2)}, u32[]{:S(2)}) collective-permute-start(bf16[1536,256]{1,0:T(8,128)(2,1)S(1)} %slice.118), channel_id=1, source_target_pairs={{5,0},{28,1},{7,2},{30,3},{9,4},{0,5},{11,6},{2,7},{13,8},{4,9},{1... | collective-permute-start | bytes 2359304 | tf_op jit(solution)/shard_map/ppermute | solution.py:58
  79.3 13.5 %collective-permute-start.12 = (bf16[1536,256]{1,0:T(8,128)(2,1)S(1)}, bf16[1536,256]{1,0:T(8,128)(2,1)S(1)}, u32[]{:S(2)}, u32[]{:S(2)}) collective-permute-start(bf16[1536,256]{1,0:T(8,128)(2,1)S(1)} %collective-permute-done.10), channel_id=1, source_target_pairs={{159,0},{6,1},{29,2},{132,3},{131,4},{10,5},{1,6},{136,7},{135,8},... | collective-permute-start | bytes 2359304 | tf_op jit(solution)/shard_map/ppermute | solution.py:58
  81.5 10.4 %collective-permute-start.13 = (bf16[1024,256]{1,0:T(8,128)(2,1)S(1)}, bf16[1024,256]{1,0:T(8,128)(2,1)S(1)}, u32[]{:S(2)}, u32[]{:S(2)}) collective-permute-start(bf16[1024,256]{1,0:T(8,128)(2,1)S(1)} %pad_maximum_fusion.6), channel_id=1, source_target_pairs={{96,0},{33,1},{98,2},{35,3},{100,4},{37,5},{102,6},{39,7},{104,8},... | collective-permute-start | bytes 1572872 | tf_op jit(solution)/shard_map/ppermute | solution.py:58
  92.9 7.8 %copy-start.2 = (s32[256]{0:T(256)S(1)}, s32[256]{0:T(256)}, u32[]{:S(2)}) copy-start(s32[256]{0:T(256)} %param.9) | copy-start | bytes 3076
  94.5 6.0 %collective-permute-start.14 = (f32[256,256]{1,0:T(8,128)S(1)}, f32[256,256]{1,0:T(8,128)S(1)}, u32[]{:S(2)}, u32[]{:S(2)}) collective-permute-start(f32[256,256]{1,0:T(8,128)S(1)} %slice_bitcast_fusion.1), channel_id=1, source_target_pairs={{0,1},{1,0},{2,3},{3,2},{4,5},{5,4},{6,7},{7,6},{8,9},{9,8},{10,11... | collective-permute-start | bytes 786440 | tf_op jit(solution)/shard_map/ppermute | solution.py:256
  100.6 8.7 %collective-permute-start.17 = (f32[256,256]{1,0:T(8,128)S(1)}, f32[256,256]{1,0:T(8,128)S(1)}, u32[]{:S(2)}, u32[]{:S(2)}) collective-permute-start(f32[256,256]{1,0:T(8,128)S(1)} %fusion.7), channel_id=1, source_target_pairs={{0,2},{1,3},{2,0},{3,1},{4,6},{5,7},{6,4},{7,5},{8,10},{9,11},{10,... | collective-permute-start | bytes 786440 | tf_op jit(solution)/shard_map/ppermute | solution.py:250
  102.4 7.2 %collective-permute-start.15 = (f32[128,256]{1,0:T(8,128)S(1)}, f32[128,256]{1,0:T(8,128)S(1)}, u32[]{:S(2)}, u32[]{:S(2)}) collective-permute-start(f32[128,256]{1,0:T(8,128)S(1)} %get-tuple-element.46), channel_id=1, source_target_pairs={{0,1},{1,0},{2,3},{3,2},{4,5},{5,4},{6,7},{7,6},{8,9},{9,8},{10,11... | collective-permute-start | bytes 393224 | tf_op jit(solution)/shard_map/ppermute | solution.py:256
  102.9 6.7 %collective-permute-start.16 = (f32[128,256]{1,0:T(8,128)S(1)}, f32[128,256]{1,0:T(8,128)S(1)}, u32[]{:S(2)}, u32[]{:S(2)}) collective-permute-start(f32[128,256]{1,0:T(8,128)S(1)} %get-tuple-element.47), channel_id=1, source_target_pairs={{0,1},{1,0},{2,3},{3,2},{4,5},{5,4},{6,7},{7,6},{8,9},{9,8},{10,11... | collective-permute-start | bytes 393224 | tf_op jit(solution)/shard_map/ppermute | solution.py:256

commit v6 on v5

--- a/solution.py
+++ b/solution.py
@@ -15,7 +15,7 @@
 N_TILES = STEPS * SLOTS
 LIST = 128
 BATCH = 4
-AT_ONCE = 3
+AT_ONCE = 4
 PHASES = 5
 
 HOME = (0, 1, 2, -1)

time: 111 us -> 111 us (level)
  transfers between devices with their start and end apart: 18 -> 18, of which waited for: 15 -> 15; matrix products, arithmetic and copies ran while one was open for 4% -> 4% of each run, Pallas kernels for 15% -> 14%
where the time goes in v6:
time: 111 us; the launch traced here: 110 us
  waiting for transfers between devices  52.3 us (47%)
  starting transfers between devices  32.5 us (29%)
  Pallas kernels  17.4 us (16%)
  other arithmetic  5.43 us (5%)
  matrix products  1.3 us (1%)
    ppermute x14, waiting for transfers between devices, moved(): lax.ppermute(self.rows, AXES, [(sender(*d), member(*d)) for d in here])  45 us
    ppermute x14, starting transfers between devices, moved(): lax.ppermute(self.rows, AXES, [(sender(*d), member(*d)) for d in here])  27.1 us
    pallas_call x6, Pallas kernels, products(): pl.pallas_call(functools.partial(product_kernel, buckets, first_bucket, m...  11.5 us
    ppermute x1, waiting for transfers between devices, add(): theirs = lax.ppermute(theirs, AXES, [(i, i ^ 2) for i in devices])  6.17 us
    pallas_call x1, Pallas kernels, slot_lists(): pl.pallas_call(list_kernel, out_shape=(jax.ShapeDtypeStruct((8 * PHASES +...  5.95 us
    ppermute x3, starting transfers between devices, to_owner_core(): got = [lax.ppermute(x, AXES, [(i, i ^ 1) for i in devices]) for x in sent]  5.28 us
  transfers between devices with their start and end apart: 18, of which 15 were waited for; matrix products, arithmetic and copies ran while one was open for 4% of the time, Pallas kernels for 14%

profile of v6, /device:TPU:6, one launch (start us, length us, event | category | flops | bytes accessed | tf_op | source)
XLA Modules:
  0.0 110.4 jit_solution(4760524183042840752)
XLA Ops:
  1.7 1.3 %collective-permute-start.1 = (bf16[256,256]{1,0:T(8,128)(2,1)S(1)}, bf16[256,256]{1,0:T(8,128)(2,1)S(1)}, u32[]{:S(2)}, u32[]{:S(2)}) collective-permute-start(bf16[256,256]{1,0:T(8,128)(2,1)S(1)} %multiply_convert_fusion), channel_id=1, source_target_pairs={{128,0},{158,1},{153,2},{135,3},{132,4},{130,5},{157,6},{139,7},{1... | collective-permute-start | bytes 393224 | tf_op jit(solution)/shard_map/ppermute | solution.py:58
  3.1 5.8 %collective-permute-start = (bf16[256,256]{1,0:T(8,128)(2,1)S(1)}, bf16[256,256]{1,0:T(8,128)(2,1)S(1)}, u32[]{:S(2)}, u32[]{:S(2)}) collective-permute-start(bf16[256,256]{1,0:T(8,128)(2,1)S(1)} %multiply_convert_fusion), channel_id=1, source_target_pairs={{0,0},{30,1},{25,2},{7,3},{4,4},{2,5},{29,6},{11,7},{8,8},{6,9},{1... | collective-permute-start | bytes 393224 | tf_op jit(solution)/shard_map/ppermute | solution.py:58
  9.8 1.2 %select_reduce_fusion = s32[16,22]{0,1:T(8,128)S(1)} fusion(s32[128]{0:T(128)} %constant.11.clone, s32[16,22]{0,1:T(8,128)S(1)} %copy.9), kind=kLoop, calls=%fused_computation.29 | loop fusion | flops 134816 | bytes 3328 | tf_op jit(solution)/shard_map/reduce_sum | solution.py:229
  13.1 1.7 %collective-permute-start.3 = (bf16[512,256]{1,0:T(8,128)(2,1)S(1)}, bf16[512,256]{1,0:T(8,128)(2,1)S(1)}, u32[]{:S(2)}, u32[]{:S(2)}) collective-permute-start(bf16[512,256]{1,0:T(8,128)(2,1)S(1)} %pad_maximum_fusion.8), channel_id=1, source_target_pairs={{32,0},{97,1},{34,2},{99,3},{36,4},{101,5},{38,6},{103,7},{40,8},{... | collective-permute-start | bytes 786440 | tf_op jit(solution)/shard_map/ppermute | solution.py:58
  14.7 2.5 %collective-permute-start.2 = (bf16[512,256]{1,0:T(8,128)(2,1)S(1)}, bf16[512,256]{1,0:T(8,128)(2,1)S(1)}, u32[]{:S(2)}, u32[]{:S(2)}) collective-permute-start(bf16[512,256]{1,0:T(8,128)(2,1)S(1)} %pad_maximum_fusion.8), channel_id=1, source_target_pairs={{5,0},{28,1},{7,2},{30,3},{9,4},{0,5},{11,6},{2,7},{13,8},{4,9},{1... | collective-permute-start | bytes 786440 | tf_op jit(solution)/shard_map/ppermute | solution.py:58
  17.2 2.3 %collective-permute-done.3 = bf16[512,256]{1,0:T(8,128)(2,1)S(1)} collective-permute-done((bf16[512,256]{1,0:T(8,128)(2,1)S(1)}, bf16[512,256]{1,0:T(8,128)(2,1)S(1)}, u32[]{:S(2)}, u32[]{:S(2)}) %collective-permute-start.3) | collective-permute-done | bytes 262176 | tf_op jit(solution)/shard_map/ppermute | solution.py:58
  19.5 1.8 %collective-permute-done.2 = bf16[512,256]{1,0:T(8,128)(2,1)S(1)} collective-permute-done((bf16[512,256]{1,0:T(8,128)(2,1)S(1)}, bf16[512,256]{1,0:T(8,128)(2,1)S(1)}, u32[]{:S(2)}, u32[]{:S(2)}) %collective-permute-start.2) | collective-permute-done | bytes 262176 | tf_op jit(solution)/shard_map/ppermute | solution.py:58
  21.3 1.5 %collective-permute-start.5 = (bf16[1024,256]{1,0:T(8,128)(2,1)S(1)}, bf16[1024,256]{1,0:T(8,128)(2,1)S(1)}, u32[]{:S(2)}, u32[]{:S(2)}) collective-permute-start(bf16[1024,256]{1,0:T(8,128)(2,1)S(1)} %get-tuple-element.55), channel_id=1, source_target_pairs={{96,0},{33,1},{98,2},{35,3},{100,4},{37,5},{102,6},{39,7},{104,8},... | collective-permute-start | bytes 1572872 | tf_op jit(solution)/shard_map/ppermute | solution.py:58
  22.9 1.3 %collective-permute-start.4 = (bf16[1024,256]{1,0:T(8,128)(2,1)S(1)}, bf16[1024,256]{1,0:T(8,128)(2,1)S(1)}, u32[]{:S(2)}, u32[]{:S(2)}) collective-permute-start(bf16[1024,256]{1,0:T(8,128)(2,1)S(1)} %get-tuple-element.56), channel_id=1, source_target_pairs={{159,0},{6,1},{29,2},{132,3},{131,4},{10,5},{1,6},{136,7},{135,8},... | collective-permute-start | bytes 1572872 | tf_op jit(solution)/shard_map/ppermute | solution.py:58
  24.2 6.0 %shard_map.82 = (s32[41,128]{1,0:T(8,128)S(1)}, s32[40]{0:T(128)S(1)}, bf16[352,128,128]{2,1,0:T(8,128)(2,1)S(1)}) custom-call(s32[16]{0:T(128)S(1)} %bitcast.69, s32[16,22]{1,0:T(8,128)S(1)} %fusion.19.coded, bf16[352,128,128]{2,1,0:T(8,128)(2,1)} %bitcast.70), custom_call_target="tpu_custom_call" | custom-call | bytes 23000000 | tf_op jit(solution)/shard_map/pallas_call | solution.py:146
  30.3 1.5 %collective-permute-done.5 = bf16[1024,256]{1,0:T(8,128)(2,1)S(1)} collective-permute-done((bf16[1024,256]{1,0:T(8,128)(2,1)S(1)}, bf16[1024,256]{1,0:T(8,128)(2,1)S(1)}, u32[]{:S(2)}, u32[]{:S(2)}) %collective-permute-start.5) | collective-permute-done | bytes 524320 | tf_op jit(solution)/shard_map/ppermute | solution.py:58
  31.8 1.7 %collective-permute-done.4 = bf16[1024,256]{1,0:T(8,128)(2,1)S(1)} collective-permute-done((bf16[1024,256]{1,0:T(8,128)(2,1)S(1)}, bf16[1024,256]{1,0:T(8,128)(2,1)S(1)}, u32[]{:S(2)}, u32[]{:S(2)}) %collective-permute-start.4) | collective-permute-done | bytes 524320 | tf_op jit(solution)/shard_map/ppermute | solution.py:58
  34.4 1.5 %collective-permute-start.7 = (bf16[768,256]{1,0:T(8,128)(2,1)S(1)}, bf16[768,256]{1,0:T(8,128)(2,1)S(1)}, u32[]{:S(2)}, u32[]{:S(2)}) collective-permute-start(bf16[768,256]{1,0:T(8,128)(2,1)S(1)} %pad_maximum_fusion.7), channel_id=1, source_target_pairs={{32,0},{97,1},{34,2},{99,3},{36,4},{101,5},{38,6},{103,7},{40,8},{... | collective-permute-start | bytes 1179656 | tf_op jit(solution)/shard_map/ppermute | solution.py:58
  36.1 1.8 %shard_map.83.refs_0_ = f32[4,256,256]{2,1,0:T(8,128)S(1)} custom-call(s32[41,128]{1,0:T(8,128)S(1)} %get-tuple-element.25.lists, s32[40]{0:T(128)S(1)} %get-tuple-element.26.counts, bf16[352,128,128]{2,1,0:T(8,128)(2,1)S(1)} %get-tuple-element.27.tiles, bf16[29,128,256]{2,1,0:T(8,128)(2,1)S(1)} %bitcast.68), custom_call_target="tpu_custom_call" | custom-call | flops 176400000 | bytes 3150000 | tf_op jit(solution)/shard_map/pallas_call | solution.py:194
  37.9 4.4 %collective-permute-done.7 = bf16[768,256]{1,0:T(8,128)(2,1)S(1)} collective-permute-done((bf16[768,256]{1,0:T(8,128)(2,1)S(1)}, bf16[768,256]{1,0:T(8,128)(2,1)S(1)}, u32[]{:S(2)}, u32[]{:S(2)}) %collective-permute-start.7) | collective-permute-done | bytes 393248 | tf_op jit(solution)/shard_map/ppermute | solution.py:58
  42.3 4.2 %collective-permute-done.6 = bf16[1792,256]{1,0:T(8,128)(2,1)S(1)} collective-permute-done((bf16[1792,256]{1,0:T(8,128)(2,1)S(1)}, bf16[1792,256]{1,0:T(8,128)(2,1)S(1)}, u32[]{:S(2)}, u32[]{:S(2)}) %collective-permute-start.6) | collective-permute-done | bytes 917536 | tf_op jit(solution)/shard_map/ppermute | solution.py:58
  46.8 1.7 %collective-permute-start.8 = (bf16[2560,256]{1,0:T(8,128)(2,1)S(1)}, bf16[2560,256]{1,0:T(8,128)(2,1)S(1)}, u32[]{:S(2)}, u32[]{:S(2)}) collective-permute-start(bf16[2560,256]{1,0:T(8,128)(2,1)S(1)} %slice_dynamic-update-slice_fusion.1), channel_id=1, source_target_pairs={{159,0},{6,1},{29,2},{132,3},{131,4},{10,5},{1,6},{136,7},{135,8},... | collective-permute-start | bytes 3932168 | tf_op jit(solution)/shard_map/ppermute | solution.py:58
  48.5 2.2 %collective-permute-start.9 = (bf16[2048,256]{1,0:T(8,128)(2,1)S(1)}, bf16[2048,256]{1,0:T(8,128)(2,1)S(1)}, u32[]{:S(2)}, u32[]{:S(2)}) collective-permute-start(bf16[2048,256]{1,0:T(8,128)(2,1)S(1)} %get-tuple-element.32), channel_id=1, source_target_pairs={{96,0},{33,1},{98,2},{35,3},{100,4},{37,5},{102,6},{39,7},{104,8},... | collective-permute-start | bytes 3145736 | tf_op jit(solution)/shard_map/ppermute | solution.py:58
  50.8 1.8 %shard_map.84.refs_0_ = f32[4,256,256]{2,1,0:T(8,128)S(1)} custom-call(s32[41,128]{1,0:T(8,128)S(1)} %get-tuple-element.25.lists, s32[40]{0:T(128)S(1)} %get-tuple-element.26.counts, bf16[352,128,128]{2,1,0:T(8,128)(2,1)S(1)} %get-tuple-element.27.tiles, bf16[21,128,256]{2,1,0:T(8,128)(2,1)S(1)} %bitcast.66, f32[4,256,256]{2,1,0:T(8,128)S(1)} %shard_map.83.refs_0_), custom_call_target="tpu_custom_call" | custom-call | flops 126000000 | bytes 2250000 | tf_op jit(solution)/shard_map/pallas_call | solution.py:194
  52.6 11.9 %collective-permute-done.9 = bf16[2048,256]{1,0:T(8,128)(2,1)S(1)} collective-permute-done((bf16[2048,256]{1,0:T(8,128)(2,1)S(1)}, bf16[2048,256]{1,0:T(8,128)(2,1)S(1)}, u32[]{:S(2)}, u32[]{:S(2)}) %collective-permute-start.9) | collective-permute-done | bytes 1048608 | tf_op jit(solution)/shard_map/ppermute | solution.py:58
  64.5 1.5 %collective-permute-done.8 = bf16[2560,256]{1,0:T(8,128)(2,1)S(1)} collective-permute-done((bf16[2560,256]{1,0:T(8,128)(2,1)S(1)}, bf16[2560,256]{1,0:T(8,128)(2,1)S(1)}, u32[]{:S(2)}, u32[]{:S(2)}) %collective-permute-start.8) | collective-permute-done | bytes 1310752 | tf_op jit(solution)/shard_map/ppermute | solution.py:58
  66.9 2.7 %collective-permute-start.10 = (bf16[1536,256]{1,0:T(8,128)(2,1)S(1)}, bf16[1536,256]{1,0:T(8,128)(2,1)S(1)}, u32[]{:S(2)}, u32[]{:S(2)}) collective-permute-start(bf16[1536,256]{1,0:T(8,128)(2,1)S(1)} %slice.118), channel_id=1, source_target_pairs={{5,0},{28,1},{7,2},{30,3},{9,4},{0,5},{11,6},{2,7},{13,8},{4,9},{1... | collective-permute-start | bytes 2359304 | tf_op jit(solution)/shard_map/ppermute | solution.py:58
  69.7 1.8 %shard_map.85.refs_0_ = f32[4,256,256]{2,1,0:T(8,128)S(1)} custom-call(s32[41,128]{1,0:T(8,128)S(1)} %get-tuple-element.25.lists, s32[40]{0:T(128)S(1)} %get-tuple-element.26.counts, bf16[352,128,128]{2,1,0:T(8,128)(2,1)S(1)} %get-tuple-element.27.tiles, bf16[21,128,256]{2,1,0:T(8,128)(2,1)S(1)} %bitcast.67, f32[4,256,256]{2,1,0:T(8,128)S(1)} %shard_map.84.refs_0_), custom_call_target="tpu_custom_call" | custom-call | flops 126000000 | bytes 2250000 | tf_op jit(solution)/shard_map/pallas_call | solution.py:194
  71.5 6.7 %collective-permute-done.11 = bf16[1536,256]{1,0:T(8,128)(2,1)S(1)} collective-permute-done((bf16[1536,256]{1,0:T(8,128)(2,1)S(1)}, bf16[1536,256]{1,0:T(8,128)(2,1)S(1)}, u32[]{:S(2)}, u32[]{:S(2)}) %collective-permute-start.11) | collective-permute-done | bytes 786464 | tf_op jit(solution)/shard_map/ppermute | solution.py:58
  79.3 2.2 %collective-permute-start.12 = (bf16[1536,256]{1,0:T(8,128)(2,1)S(1)}, bf16[1536,256]{1,0:T(8,128)(2,1)S(1)}, u32[]{:S(2)}, u32[]{:S(2)}) collective-permute-start(bf16[1536,256]{1,0:T(8,128)(2,1)S(1)} %collective-permute-done.10), channel_id=1, source_target_pairs={{159,0},{6,1},{29,2},{132,3},{131,4},{10,5},{1,6},{136,7},{135,8},... | collective-permute-start | bytes 2359304 | tf_op jit(solution)/shard_map/ppermute | solution.py:58
  83.1 2.8 %shard_map.86 = f32[4,256,256]{2,1,0:T(8,128)S(1)} custom-call(s32[41,128]{1,0:T(8,128)S(1)} %get-tuple-element.25.lists, s32[40]{0:T(128)S(1)} %get-tuple-element.26.counts, bf16[352,128,128]{2,1,0:T(8,128)(2,1)S(1)} %get-tuple-element.27.tiles, bf16[41,128,256]{2,1,0:T(8,128)(2,1)S(1)} %bitcast.65, f32[4,256,256]{2,1,0:T(8,128)S(1)} %shard_map.85.refs_0_), custom_call_target="tpu_custom_call" | custom-call | flops 252000000 | bytes 4500000 | tf_op jit(solution)/shard_map/pallas_call | solution.py:194
  86.0 5.9 %collective-permute-done.13 = bf16[1024,256]{1,0:T(8,128)(2,1)S(1)} collective-permute-done((bf16[1024,256]{1,0:T(8,128)(2,1)S(1)}, bf16[1024,256]{1,0:T(8,128)(2,1)S(1)}, u32[]{:S(2)}, u32[]{:S(2)}) %collective-permute-start.13) | collective-permute-done | bytes 524320 | tf_op jit(solution)/shard_map/ppermute | solution.py:58
  92.9 1.5 %shard_map.87 = f32[2,256,256]{2,1,0:T(8,128)S(1)} custom-call(s32[41,128]{1,0:T(8,128)S(1)} %get-tuple-element.25.lists, s32[40]{0:T(128)S(1)} %get-tuple-element.26.counts, bf16[352,128,128]{2,1,0:T(8,128)(2,1)S(1)} %get-tuple-element.27.tiles, bf16[21,128,256]{2,1,0:T(8,128)(2,1)S(1)} %bitcast.63, f32[2,256,256]{2,1,0:T(8,128)S(1)} %slice.123.refs_0_), custom_call_target="tpu_custom_call" | custom-call | flops 260400000 | bytes 4650000 | tf_op jit(solution)/shard_map/pallas_call | solution.py:194
  94.5 4.7 %collective-permute-start.14 = (f32[256,256]{1,0:T(8,128)S(1)}, f32[256,256]{1,0:T(8,128)S(1)}, u32[]{:S(2)}, u32[]{:S(2)}) collective-permute-start(f32[256,256]{1,0:T(8,128)S(1)} %slice_bitcast_fusion.1), channel_id=1, source_target_pairs={{0,1},{1,0},{2,3},{3,2},{4,5},{5,4},{6,7},{7,6},{8,9},{9,8},{10,11... | collective-permute-start | bytes 786440 | tf_op jit(solution)/shard_map/ppermute | solution.py:256
  99.2 1.2 %collective-permute-done.14 = f32[256,256]{1,0:T(8,128)S(1)} collective-permute-done((f32[256,256]{1,0:T(8,128)S(1)}, f32[256,256]{1,0:T(8,128)S(1)}, u32[]{:S(2)}, u32[]{:S(2)}) %collective-permute-start.14) | collective-permute-done | bytes 262176 | tf_op jit(solution)/shard_map/ppermute | solution.py:256
  100.5 1.7 %shard_map.88 = f32[2,256,256]{2,1,0:T(8,128)S(1)} custom-call(s32[41,128]{1,0:T(8,128)S(1)} %get-tuple-element.25.lists, s32[40]{0:T(128)S(1)} %get-tuple-element.26.counts, bf16[352,128,128]{2,1,0:T(8,128)(2,1)S(1)} %get-tuple-element.27.tiles, bf16[21,128,256]{2,1,0:T(8,128)(2,1)S(1)} %bitcast.64, f32[2,256,256]{2,1,0:T(8,128)S(1)} %slice.106.refs_0_), custom_call_target="tpu_custom_call" | custom-call | flops 260400000 | bytes 4650000 | tf_op jit(solution)/shard_map/pallas_call | solution.py:194
  102.9 6.2 %collective-permute-done.17 = f32[256,256]{1,0:T(8,128)S(1)} collective-permute-done((f32[256,256]{1,0:T(8,128)S(1)}, f32[256,256]{1,0:T(8,128)S(1)}, u32[]{:S(2)}, u32[]{:S(2)}) %collective-permute-start.17) | collective-permute-done | bytes 262176 | tf_op jit(solution)/shard_map/ppermute | solution.py:250
  (72 shorter events, 12.8 us)
Async XLA Ops:
  0.0 109.0 %copy-start = (bf16[256,256]{1,0:T(8,128)(2,1)S(1)}, bf16[256,256]{1,0:T(8,128)(2,1)}, u32[]{:S(2)}) copy-start(bf16[256,256]{1,0:T(8,128)(2,1)} %param.14) | copy-start | bytes 393220
  1.7 10.1 %collective-permute-start.1 = (bf16[256,256]{1,0:T(8,128)(2,1)S(1)}, bf16[256,256]{1,0:T(8,128)(2,1)S(1)}, u32[]{:S(2)}, u32[]{:S(2)}) collective-permute-start(bf16[256,256]{1,0:T(8,128)(2,1)S(1)} %multiply_convert_fusion), channel_id=1, source_target_pairs={{128,0},{158,1},{153,2},{135,3},{132,4},{130,5},{157,6},{139,7},{1... | collective-permute-start | bytes 393224 | tf_op jit(solution)/shard_map/ppermute | solution.py:58
  3.1 9.9 %collective-permute-start = (bf16[256,256]{1,0:T(8,128)(2,1)S(1)}, bf16[256,256]{1,0:T(8,128)(2,1)S(1)}, u32[]{:S(2)}, u32[]{:S(2)}) collective-permute-start(bf16[256,256]{1,0:T(8,128)(2,1)S(1)} %multiply_convert_fusion), channel_id=1, source_target_pairs={{0,0},{30,1},{25,2},{7,3},{4,4},{2,5},{29,6},{11,7},{8,8},{6,9},{1... | collective-permute-start | bytes 393224 | tf_op jit(solution)/shard_map/ppermute | solution.py:58
  11.0 13.2 %copy-start.1 = (s32[1,1,16]{2,1,0:T(1,128)S(1)}, s32[1,1,16]{2,1,0:T(1,128)}, u32[]{:S(2)}) copy-start(s32[1,1,16]{2,1,0:T(1,128)} %param.13) | copy-start | bytes 196
  13.1 6.5 %collective-permute-start.3 = (bf16[512,256]{1,0:T(8,128)(2,1)S(1)}, bf16[512,256]{1,0:T(8,128)(2,1)S(1)}, u32[]{:S(2)}, u32[]{:S(2)}) collective-permute-start(bf16[512,256]{1,0:T(8,128)(2,1)S(1)} %pad_maximum_fusion.8), channel_id=1, source_target_pairs={{32,0},{97,1},{34,2},{99,3},{36,4},{101,5},{38,6},{103,7},{40,8},{... | collective-permute-start | bytes 786440 | tf_op jit(solution)/shard_map/ppermute | solution.py:58
  14.7 6.6 %collective-permute-start.2 = (bf16[512,256]{1,0:T(8,128)(2,1)S(1)}, bf16[512,256]{1,0:T(8,128)(2,1)S(1)}, u32[]{:S(2)}, u32[]{:S(2)}) collective-permute-start(bf16[512,256]{1,0:T(8,128)(2,1)S(1)} %pad_maximum_fusion.8), channel_id=1, source_target_pairs={{5,0},{28,1},{7,2},{30,3},{9,4},{0,5},{11,6},{2,7},{13,8},{4,9},{1... | collective-permute-start | bytes 786440 | tf_op jit(solution)/shard_map/ppermute | solution.py:58
  21.3 10.5 %collective-permute-start.5 = (bf16[1024,256]{1,0:T(8,128)(2,1)S(1)}, bf16[1024,256]{1,0:T(8,128)(2,1)S(1)}, u32[]{:S(2)}, u32[]{:S(2)}) collective-permute-start(bf16[1024,256]{1,0:T(8,128)(2,1)S(1)} %get-tuple-element.55), channel_id=1, source_target_pairs={{96,0},{33,1},{98,2},{35,3},{100,4},{37,5},{102,6},{39,7},{104,8},... | collective-permute-start | bytes 1572872 | tf_op jit(solution)/shard_map/ppermute | solution.py:58
  22.9 10.7 %collective-permute-start.4 = (bf16[1024,256]{1,0:T(8,128)(2,1)S(1)}, bf16[1024,256]{1,0:T(8,128)(2,1)S(1)}, u32[]{:S(2)}, u32[]{:S(2)}) collective-permute-start(bf16[1024,256]{1,0:T(8,128)(2,1)S(1)} %get-tuple-element.56), channel_id=1, source_target_pairs={{159,0},{6,1},{29,2},{132,3},{131,4},{10,5},{1,6},{136,7},{135,8},... | collective-permute-start | bytes 1572872 | tf_op jit(solution)/shard_map/ppermute | solution.py:58
  33.7 12.9 %collective-permute-start.6 = (bf16[1792,256]{1,0:T(8,128)(2,1)S(1)}, bf16[1792,256]{1,0:T(8,128)(2,1)S(1)}, u32[]{:S(2)}, u32[]{:S(2)}) collective-permute-start(bf16[1792,256]{1,0:T(8,128)(2,1)S(1)} %pad_maximum_fusion.3), channel_id=1, source_target_pairs={{5,0},{28,1},{7,2},{30,3},{9,4},{0,5},{11,6},{2,7},{13,8},{4,9},{1... | collective-permute-start | bytes 2752520 | tf_op jit(solution)/shard_map/ppermute | solution.py:58
  34.4 7.9 %collective-permute-start.7 = (bf16[768,256]{1,0:T(8,128)(2,1)S(1)}, bf16[768,256]{1,0:T(8,128)(2,1)S(1)}, u32[]{:S(2)}, u32[]{:S(2)}) collective-permute-start(bf16[768,256]{1,0:T(8,128)(2,1)S(1)} %pad_maximum_fusion.7), channel_id=1, source_target_pairs={{32,0},{97,1},{34,2},{99,3},{36,4},{101,5},{38,6},{103,7},{40,8},{... | collective-permute-start | bytes 1179656 | tf_op jit(solution)/shard_map/ppermute | solution.py:58
  46.8 19.2 %collective-permute-start.8 = (bf16[2560,256]{1,0:T(8,128)(2,1)S(1)}, bf16[2560,256]{1,0:T(8,128)(2,1)S(1)}, u32[]{:S(2)}, u32[]{:S(2)}) collective-permute-start(bf16[2560,256]{1,0:T(8,128)(2,1)S(1)} %slice_dynamic-update-slice_fusion.1), channel_id=1, source_target_pairs={{159,0},{6,1},{29,2},{132,3},{131,4},{10,5},{1,6},{136,7},{135,8},... | collective-permute-start | bytes 3932168 | tf_op jit(solution)/shard_map/ppermute | solution.py:58
  48.5 16.0 %collective-permute-start.9 = (bf16[2048,256]{1,0:T(8,128)(2,1)S(1)}, bf16[2048,256]{1,0:T(8,128)(2,1)S(1)}, u32[]{:S(2)}, u32[]{:S(2)}) collective-permute-start(bf16[2048,256]{1,0:T(8,128)(2,1)S(1)} %get-tuple-element.32), channel_id=1, source_target_pairs={{96,0},{33,1},{98,2},{35,3},{100,4},{37,5},{102,6},{39,7},{104,8},... | collective-permute-start | bytes 3145736 | tf_op jit(solution)/shard_map/ppermute | solution.py:58
  66.1 12.1 %collective-permute-start.11 = (bf16[1536,256]{1,0:T(8,128)(2,1)S(1)}, bf16[1536,256]{1,0:T(8,128)(2,1)S(1)}, u32[]{:S(2)}, u32[]{:S(2)}) collective-permute-start(bf16[1536,256]{1,0:T(8,128)(2,1)S(1)} %constant_dynamic-update-slice_fusion.13), channel_id=1, source_target_pairs={{32,0},{97,1},{34,2},{99,3},{36,4},{101,5},{38,6},{103,7},{40,8},{... | collective-permute-start | bytes 2359304 | tf_op jit(solution)/shard_map/ppermute | solution.py:58
  66.9 12.4 %collective-permute-start.10 = (bf16[1536,256]{1,0:T(8,128)(2,1)S(1)}, bf16[1536,256]{1,0:T(8,128)(2,1)S(1)}, u32[]{:S(2)}, u32[]{:S(2)}) collective-permute-start(bf16[1536,256]{1,0:T(8,128)(2,1)S(1)} %slice.118), channel_id=1, source_target_pairs={{5,0},{28,1},{7,2},{30,3},{9,4},{0,5},{11,6},{2,7},{13,8},{4,9},{1... | collective-permute-start | bytes 2359304 | tf_op jit(solution)/shard_map/ppermute | solution.py:58
  79.3 13.5 %collective-permute-start.12 = (bf16[1536,256]{1,0:T(8,128)(2,1)S(1)}, bf16[1536,256]{1,0:T(8,128)(2,1)S(1)}, u32[]{:S(2)}, u32[]{:S(2)}) collective-permute-start(bf16[1536,256]{1,0:T(8,128)(2,1)S(1)} %collective-permute-done.10), channel_id=1, source_target_pairs={{159,0},{6,1},{29,2},{132,3},{131,4},{10,5},{1,6},{136,7},{135,8},... | collective-permute-start | bytes 2359304 | tf_op jit(solution)/shard_map/ppermute | solution.py:58
  81.5 10.4 %collective-permute-start.13 = (bf16[1024,256]{1,0:T(8,128)(2,1)S(1)}, bf16[1024,256]{1,0:T(8,128)(2,1)S(1)}, u32[]{:S(2)}, u32[]{:S(2)}) collective-permute-start(bf16[1024,256]{1,0:T(8,128)(2,1)S(1)} %pad_maximum_fusion.6), channel_id=1, source_target_pairs={{96,0},{33,1},{98,2},{35,3},{100,4},{37,5},{102,6},{39,7},{104,8},... | collective-permute-start | bytes 1572872 | tf_op jit(solution)/shard_map/ppermute | solution.py:58
  92.9 7.6 %copy-start.2 = (s32[256]{0:T(256)S(1)}, s32[256]{0:T(256)}, u32[]{:S(2)}) copy-start(s32[256]{0:T(256)} %param.9) | copy-start | bytes 3076
  94.5 5.8 %collective-permute-start.14 = (f32[256,256]{1,0:T(8,128)S(1)}, f32[256,256]{1,0:T(8,128)S(1)}, u32[]{:S(2)}, u32[]{:S(2)}) collective-permute-start(f32[256,256]{1,0:T(8,128)S(1)} %slice_bitcast_fusion.1), channel_id=1, source_target_pairs={{0,1},{1,0},{2,3},{3,2},{4,5},{5,4},{6,7},{7,6},{8,9},{9,8},{10,11... | collective-permute-start | bytes 786440 | tf_op jit(solution)/shard_map/ppermute | solution.py:256
  100.4 8.7 %collective-permute-start.17 = (f32[256,256]{1,0:T(8,128)S(1)}, f32[256,256]{1,0:T(8,128)S(1)}, u32[]{:S(2)}, u32[]{:S(2)}) collective-permute-start(f32[256,256]{1,0:T(8,128)S(1)} %fusion.7), channel_id=1, source_target_pairs={{0,2},{1,3},{2,0},{3,1},{4,6},{5,7},{6,4},{7,5},{8,10},{9,11},{10,... | collective-permute-start | bytes 786440 | tf_op jit(solution)/shard_map/ppermute | solution.py:250
  102.3 7.1 %collective-permute-start.15 = (f32[128,256]{1,0:T(8,128)S(1)}, f32[128,256]{1,0:T(8,128)S(1)}, u32[]{:S(2)}, u32[]{:S(2)}) collective-permute-start(f32[128,256]{1,0:T(8,128)S(1)} %get-tuple-element.46), channel_id=1, source_target_pairs={{0,1},{1,0},{2,3},{3,2},{4,5},{5,4},{6,7},{7,6},{8,9},{9,8},{10,11... | collective-permute-start | bytes 393224 | tf_op jit(solution)/shard_map/ppermute | solution.py:256
  102.7 6.6 %collective-permute-start.16 = (f32[128,256]{1,0:T(8,128)S(1)}, f32[128,256]{1,0:T(8,128)S(1)}, u32[]{:S(2)}, u32[]{:S(2)}) collective-permute-start(f32[128,256]{1,0:T(8,128)S(1)} %get-tuple-element.47), channel_id=1, source_target_pairs={{0,1},{1,0},{2,3},{3,2},{4,5},{5,4},{6,7},{7,6},{8,9},{9,8},{10,11... | collective-permute-start | bytes 393224 | tf_op jit(solution)/shard_map/ppermute | solution.py:256
